TPU v7x, 256 devices: a whole 4x4x8 slice. The times are simulated.
256 devices in a mesh: row: 8 (over z_hi, core), col: 32 (over z_lo, x, y).
Axes of the slice: x: 4, y: 4, z: 8 (z_hi: 4, z_lo: 2; z = z_hi * 2 + z_lo), core: 2. Of those that a mesh axis runs over, the one named last changes fastest.
Arguments:
- band_emb: bfloat16 [128, 256], P('row', 'col'), may hold values from -6 to 6
- col_emb: bfloat16 [16384, 256], P('col', 'row'), may hold values from -6 to 6
- w_row: bfloat16 [256, 32], replicated, may hold values from -0.375 to 0.375
- w_col: bfloat16 [256, 32], replicated, may hold values from -0.375 to 0.375
- first_kernel_weight: bfloat16 [32, 32, 3, 3], replicated, may hold values from -0.375 to 0.375
- second_kernel_weight: bfloat16 [32, 32, 3, 3], replicated, may hold values from -0.375 to 0.375
- cotangent: bfloat16 [32, 128, 16384], P(None, 'row', 'col'), may hold values from -6 to 6
- drop_seeds: int32 [8, 32], P('row', 'col'), may hold values from 0 to 16777215
- tile_mask: int32 [8, 32], P('row', 'col'), may hold values from 0 to 1, as said below
- dilations: int32 [2], replicated, may hold values from 1 to 4, as said below
Outputs:
- out_map: bfloat16 [32, 128, 16384], P(None, 'row', 'col')
- grad_band: bfloat16 [128, 256], P('row', 'col')
- grad_cols: bfloat16 [16384, 256], P('col', 'row')
- grad_w_row: float32 [256, 32], replicated
- grad_w_col: float32 [256, 32], replicated
- grad_conv_one: float32 [32, 32, 3, 3], replicated
- grad_conv_two: float32 [32, 32, 3, 3], replicated
Inputs may be any that keep to these rules, and one draw needn't show every extreme that they name: `dilations`: one of the two equals 4. For some first bin b0 of the band with b0 >= 512, tile_mask[r, c] is 1 exactly when (c + 1) * 512 > b0 + r * 16.
All inputs are finite; a program needn't handle non-finite values.
Results may differ from a plain program's by a relative error of at most 0.023.
Values may be sent and summed in bfloat16 or wider, within the bound.
No kernel may reach another device: no remote copies, remote signals or barrier semaphores. Data moves between devices by JAX's collectives and lax.ppermute only.
A program may use at most 64 MiB of HBM per device.

v0:
```python
import jax
import jax.numpy as jnp
from jax import lax
from jax.sharding import PartitionSpec as P

LARGEST_SPREAD = 4


tanh_scale = 0.7978845608028654
cubic_term = 0.044715
keep_boost = 4.0 / 3.0


def extended(array, sides, width):
    for axis, dim in sides:
        count, length = (lax.axis_size(axis), array.shape[dim])
        up = [(i, (i + 1) % count) for i in range(count - 1)]
        down = [(j, i) for i, j in up]
        last = lax.slice_in_dim(array, length - width, length, axis=dim)
        first = lax.slice_in_dim(array, 0, width, axis=dim)
        before = lax.ppermute(last, axis, up)
        after = lax.ppermute(first, axis, down)
        array = jnp.concatenate([before, array, after], axis=dim)
    return array


def gelu_value(values):
    inner = tanh_scale * (values + cubic_term * values * values * values)
    return 0.5 * values * (1.0 + jnp.tanh(inner))


def gelu_slope(values):
    tangent = jnp.tanh(tanh_scale * (values + cubic_term * values * values * values))
    return 0.5 * (1.0 + tangent) + 0.5 * values * (1.0 - tangent * tangent) * tanh_scale * (
        1.0 + 3.0 * cubic_term * values * values
    )


def keep_factor(tile_seed, layer_id, channel, row_ids, col_ids):
    hashed = tile_seed * 1000003 + layer_id * 7919
    hashed = hashed ^ channel * 73856093
    hashed = hashed ^ row_ids * 19349663
    hashed = hashed ^ col_ids * 83492791
    hashed = hashed * 668265261
    hashed = hashed ^ hashed >> 15 & 131071
    hashed = hashed * 374761393
    hashed = hashed ^ hashed >> 13 & 524287
    kept = hashed & 3 != 0
    return kept.astype(jnp.float32) * keep_boost


def spread_convolution(padded, kernel, spacing, border_rows, out_rows, out_cols):

    def build_branch(spread):

        def convolve(values):
            offset = border_rows - spread
            window = lax.slice(
                values,
                (0, offset, offset),
                (values.shape[0], offset + out_rows + 2 * spread, offset + out_cols + 2 * spread),
            )
            return lax.conv_general_dilated(
                window[None],
                kernel,
                (1, 1),
                "VALID",
                rhs_dilation=(spread, spread),
                dimension_numbers=("NCHW", "OIHW", "NCHW"),
                preferred_element_type=jnp.float32,
            )[0]

        return convolve

    return lax.switch(
        spacing - 1, [build_branch(spread) for spread in range(1, border_rows + 1)], padded
    )


def mirror_kernel(kernel):
    return jnp.transpose(kernel[:, :, ::-1, ::-1], (1, 0, 2, 3))


def kernel_gradient(padded, grads, spacing, border_rows):
    out_rows = grads.shape[1]
    out_cols = grads.shape[2]
    tap_terms = []
    for tap_row in range(3):
        for tap_col in range(3):
            starts = (
                jnp.zeros((), jnp.int32),
                border_rows + (tap_row - 1) * spacing,
                border_rows + (tap_col - 1) * spacing,
            )
            window = lax.dynamic_slice(padded, starts, (padded.shape[0], out_rows, out_cols))
            tap_terms.append(
                jnp.einsum("oij,cij->oc", grads, window, preferred_element_type=jnp.float32)
            )
    return jnp.stack(tap_terms, axis=2).reshape(grads.shape[0], padded.shape[0], 3, 3)


def margins(values):
    return extended(values, (("row", 1), ("col", 2)), LARGEST_SPREAD)


def per_device(
    band_emb,
    col_emb,
    w_row,
    w_col,
    first_kernel_weight,
    second_kernel_weight,
    cotangent,
    drop_seeds,
    tile_mask,
    dilations,
):
    channels = cotangent.shape[0]
    local_tile_rows = cotangent.shape[1]
    local_tile_columns = cotangent.shape[2]
    highest = lax.Precision.HIGHEST
    row_index = lax.axis_index("row")
    col_index = lax.axis_index("col")
    band_full = lax.all_gather(band_emb, "col", axis=1, tiled=True)
    col_full = lax.all_gather(col_emb, "row", axis=1, tiled=True)
    row_proj = jnp.dot(band_full, w_row, preferred_element_type=jnp.float32)
    col_proj = jnp.dot(col_full, w_col, preferred_element_type=jnp.float32)
    keep_tile = tile_mask[0, 0].astype(jnp.float32)
    tile_seed = drop_seeds[0, 0]
    first_spread = dilations[0]
    second_spread = dilations[1]
    channel = jnp.arange(channels, dtype=jnp.int32)[:, None, None]
    row_ids = (row_index * local_tile_rows + jnp.arange(local_tile_rows, dtype=jnp.int32))[
        None, :, None
    ]
    col_ids = (col_index * local_tile_columns + jnp.arange(local_tile_columns, dtype=jnp.int32))[
        None, None, :
    ]
    factor_one = keep_tile * keep_factor(tile_seed, 1, channel, row_ids, col_ids)
    factor_two = keep_tile * keep_factor(tile_seed, 2, channel, row_ids, col_ids)
    pair_map = (keep_tile * (row_proj.T[:, :, None] + col_proj.T[:, None, :])).astype(jnp.bfloat16)
    pair_padded = margins(pair_map)
    first_preactivation = spread_convolution(
        pair_padded,
        first_kernel_weight,
        first_spread,
        LARGEST_SPREAD,
        local_tile_rows,
        local_tile_columns,
    )
    hidden = (factor_one * gelu_value(first_preactivation)).astype(jnp.bfloat16)
    hidden_padded = margins(hidden)
    second_preactivation = spread_convolution(
        hidden_padded,
        second_kernel_weight,
        second_spread,
        LARGEST_SPREAD,
        local_tile_rows,
        local_tile_columns,
    )
    out_map = (factor_two * gelu_value(second_preactivation)).astype(jnp.bfloat16)
    second_gradient = (
        cotangent.astype(jnp.float32) * factor_two * gelu_slope(second_preactivation)
    ).astype(jnp.bfloat16)
    second_gradient_padded = margins(second_gradient)
    hidden_gradient = spread_convolution(
        second_gradient_padded,
        mirror_kernel(second_kernel_weight),
        second_spread,
        LARGEST_SPREAD,
        local_tile_rows,
        local_tile_columns,
    )
    first_gradient = (hidden_gradient * factor_one * gelu_slope(first_preactivation)).astype(
        jnp.bfloat16
    )
    second_kernel_share = kernel_gradient(
        hidden_padded, second_gradient, second_spread, LARGEST_SPREAD
    )
    first_gradient_padded = margins(first_gradient)
    pair_gradient = keep_tile * spread_convolution(
        first_gradient_padded,
        mirror_kernel(first_kernel_weight),
        first_spread,
        LARGEST_SPREAD,
        local_tile_rows,
        local_tile_columns,
    )
    first_kernel_share = kernel_gradient(pair_padded, first_gradient, first_spread, LARGEST_SPREAD)
    row_part = jnp.sum(pair_gradient, axis=2).T
    col_part = jnp.sum(pair_gradient, axis=1).T
    w_row_part = jnp.dot(band_full.astype(jnp.float32).T, row_part, precision=highest)
    w_col_part = jnp.dot(col_full.astype(jnp.float32).T, col_part, precision=highest)
    kernel_count = first_kernel_share.size
    weight_count = w_row_part.size
    flat_terms = jnp.concatenate(
        [
            first_kernel_share.reshape(-1),
            second_kernel_share.reshape(-1),
            w_row_part.reshape(-1),
            w_col_part.reshape(-1),
        ]
    )
    summed_slice = lax.psum_scatter(flat_terms, ("row", "col"), scatter_dimension=0, tiled=True)
    flat_totals = lax.all_gather(summed_slice, ("row", "col"), axis=0, tiled=True)
    grad_conv_one = flat_totals[:kernel_count].reshape(first_kernel_share.shape)
    grad_conv_two = flat_totals[kernel_count : 2 * kernel_count].reshape(second_kernel_share.shape)
    grad_w_row = flat_totals[2 * kernel_count : 2 * kernel_count + weight_count].reshape(
        w_row_part.shape
    )
    grad_w_col = flat_totals[2 * kernel_count + weight_count :].reshape(w_col_part.shape)
    w_row_wide = w_row.astype(jnp.float32)
    w_col_wide = w_col.astype(jnp.float32)
    band_term = jnp.dot(row_part, w_row_wide.T, precision=highest)
    grad_band = lax.psum_scatter(band_term, "col", scatter_dimension=1, tiled=True).astype(
        jnp.bfloat16
    )
    col_term = jnp.dot(col_part, w_col_wide.T, precision=highest)
    grad_cols = lax.psum_scatter(
        col_term.astype(jnp.bfloat16), "row", scatter_dimension=1, tiled=True
    )
    return (out_map, grad_band, grad_cols, grad_w_row, grad_w_col, grad_conv_one, grad_conv_two)


def solution(mesh):
    placed = (
        P("row", "col"),
        P("col", "row"),
        P(),
        P(),
        P(),
        P(),
        P(None, "row", "col"),
        P("row", "col"),
        P("row", "col"),
        P(),
    )
    return jax.shard_map(
        per_device,
        mesh=mesh,
        in_specs=placed,
        out_specs=(P(None, "row", "col"), P("row", "col"), P("col", "row"), P(), P(), P(), P()),
        check_vma=False,
    )
```

profile of v0, /device:TPU:6, one launch (start us, length us, event | category | flops | bytes accessed | tf_op | source)
XLA Modules:
  0.0 848.4 jit_solution(83508804691928326)
XLA Ops:
  8.7 71.9 %all_gather.9 = bf16[16,256]{0,1:T(8,128)(2,1)S(1)} all-gather(bf16[16,8]{0,1:T(8,128)(2,1)} %param.26), channel_id=1, replica_groups=mesh['row'=8,'col'=32] {'col'}, dimensions={1}, use_global_device_ids=true | all-gather | bytes 8448 | tf_op jit(solution)/shard_map/all_gather | solution.py:124
  80.6 18.5 %all_gather.10 = bf16[512,256]{0,1:T(8,128)(2,1)S(1)} all-gather(bf16[512,32]{0,1:T(8,128)(2,1)} %param.27), channel_id=1, replica_groups=mesh['row'=8,'col'=32] {'row'}, dimensions={1}, use_global_device_ids=true | all-gather | bytes 294912 | tf_op jit(solution)/shard_map/all_gather | solution.py:125
  107.1 3.8 collective-permute-start.2
  110.9 4.2 collective-permute-start.3
  119.4 27.4 %conditional.4 = (f32[32,16,512]{2,0,1:T(8,128)S(1)}) conditional(s32[]{:T(128)} %bitcast.64, (bf16[32,24,520]{2,0,1:T(8,128)(2,1)S(1)}, bf16[32,32,3,3]{1,0,3,2:T(8,128)(2,1)S(1)}) %tuple.130, (bf16[32,24,520]{2,0,1:T(8,128)(2,1)S(1)}, bf16[32,32,3,3]{1,0,3,2:T(8,128)(2,1)S(1)}) %tuple.131, ...), branch_computations={%region_0.0_spmd, %region_1.0_spmd, %region_2.0_spmd, %region_3.0_... | conditional | flops 156311552 | bytes 14201422 | solution.py:75
  124.8 6.0 broadcast_select_fusion
  130.8 3.9 copy.199
  147.6 6.6 collective-permute-start.4
  154.2 7.8 collective-permute-start.5
  163.7 5.9 collective-permute-start.6
  182.2 26.8 %conditional.5 = (f32[32,16,512]{2,0,1:T(8,128)S(1)}) conditional(s32[]{:T(128)} %bitcast.62, (bf16[32,24,520]{2,0,1:T(8,128)(2,1)S(1)}, bf16[32,32,3,3]{1,0,3,2:T(8,128)(2,1)}) %tuple.57, (bf16[32,24,520]{2,0,1:T(8,128)(2,1)S(1)}, bf16[32,32,3,3]{1,0,3,2:T(8,128)(2,1)}) %tuple.57, ...), branch_computations={%region_4.0_spmd, %region_5.0_spmd, %region_6.0_spmd, %region_7.0_... | conditional | flops 156311552 | bytes 14275178 | solution.py:75
  184.7 5.3 copy.219
  191.2 8.6 %broadcast_select_fusion.7 = f32[16,8,65,32]{3,1,2,0:T(8,128)} fusion(pred[8,65]{0,1:T(8,128)(4,1)S(1)} %copy-done.46, bf16[32,32,3,3]{1,0,3,2:T(8,128)(2,1)S(1)} %copy-done.22, bf16[32,24,1,7,8]{0,3,4,1,2:T(8,128)(2,1)S(1)} %slice.186, bf16[32,24,1,8,65]{0,3,4,1,2:T(8,128)(2,1)} %copy.219), kind=kOutput, calls=%fused_computation.112 | convolution fusion | flops 156311552 | bytes 1968648 | tf_op jit(solution)/shard_map/cond/branch_3_fun/conv_general_dilated | solution.py:63
  199.8 4.9 copy.220
  214.8 4.2 collective-permute-start.8
  221.0 2.9 collective-permute-done.9
  224.8 8.1 collective-permute-start.10
  239.1 3.8 collective-permute-done.11
  244.6 34.0 %conditional.6 = (f32[32,16,512]{2,0,1:T(8,128)}) conditional(s32[]{:T(128)} %bitcast.62, (bf16[32,24,520]{2,0,1:T(8,128)(2,1)S(1)}, bf16[32,32,3,3]{1,0,3,2:T(8,128)(2,1)}) %tuple.58, (bf16[32,24,520]{2,0,1:T(8,128)(2,1)S(1)}, bf16[32,32,3,3]{1,0,3,2:T(8,128)(2,1)}) %tuple.58, (bf16[32,24,520]{2,0,1:T(8,128)(2,1)S(1)}, ...), branch_computations={%region_8.0_spmd, %region_9.0_spmd, %region_10.0_spmd, %region_11.... | conditional | flops 156311552 | bytes 14201422 | solution.py:75
  255.5 5.3 copy.231
  261.9 8.6 %broadcast_select_fusion.11 = f32[16,8,65,32]{3,1,2,0:T(8,128)} fusion(pred[8,65]{0,1:T(8,128)(4,1)S(1)} %copy-done.47, bf16[32,32,3,3]{1,0,3,2:T(8,128)(2,1)S(1)} %copy-done.26, bf16[32,24,1,7,8]{0,3,4,1,2:T(8,128)(2,1)S(1)} %slice.194, bf16[32,24,1,8,65]{0,3,4,1,2:T(8,128)(2,1)} %copy.231), kind=kOutput, calls=%fused_computation.171 | convolution fusion | flops 156311552 | bytes 1968648 | tf_op jit(solution)/shard_map/cond/branch_3_fun/conv_general_dilated | solution.py:63
  270.5 4.9 copy.232
  283.3 5.7 collective-permute-start.12
  293.3 4.5 collective-permute-start.14
  297.8 3.5 collective-permute-start.15
  303.0 4.1 collective-permute-done.15
  307.7 18.6 %conditional.7 = (f32[32,16,512]{2,0,1:T(8,128)S(1)}) conditional(s32[]{:T(128)} %bitcast.64, (bf16[32,24,520]{2,0,1:T(8,128)(2,1)S(1)}, bf16[32,32,3,3]{1,0,3,2:T(8,128)(2,1)S(1)}) %tuple.134, (bf16[32,24,520]{2,0,1:T(8,128)(2,1)S(1)}, bf16[32,32,3,3]{1,0,3,2:T(8,128)(2,1)S(1)}) %tuple.135, ...), branch_computations={%region_12.0_spmd, %region_13.0_spmd, %region_14.0_spmd, %region_1... | conditional | flops 156311552 | bytes 14201422 | solution.py:75
  313.1 6.0 broadcast_select_fusion.12
  319.1 3.9 copy.235
  329.7 156.8 %all-reduce.1 = bf16[16,256]{0,1:T(8,128)(2,1)S(1)} all-reduce(f32[16,256]{0,1:T(8,128)S(1)} %fusion.289), channel_id=2, replica_groups=mesh['row'=8,'col'=32] {'col'}, use_global_device_ids=true, to_apply=%region_17.0.clone | all-reduce | flops 4096 | bytes 24576
  486.4 99.0 %all-reduce.8.cloned.1.call-done = f32[34816]{0:T(1024)} async-done(((f32[34816]{0:T(1024)}), f32[34816]{0:T(1024)}) %all-reduce.8.cloned.1.call-update) | async-done | bytes 139280
  587.7 244.5 %all-reduce.6.cloned.1.call-done = f32[34816]{0:T(1024)} async-done(((f32[34816]{0:T(1024)}), f32[34816]{0:T(1024)}) %all-reduce.6.cloned.1.call-update) | async-done | bytes 139280
  (186 shorter events, 92.3 us)
Async XLA Ops:
  8.0 92.0 %copy-start = (bf16[256,32]{0,1:T(8,128)(2,1)S(1)}, bf16[256,32]{0,1:T(8,128)(2,1)}, u32[]{:S(2)}) copy-start(bf16[256,32]{0,1:T(8,128)(2,1)} %param.29) | copy-start | bytes 49156
  8.0 111.3 %copy-start.17 = (bf16[32,32,3,3]{1,0,3,2:T(8,128)(2,1)S(1)}, bf16[32,32,3,3]{1,0,3,2:T(8,128)(2,1)}, u32[]{:S(2)}) copy-start(bf16[32,32,3,3]{1,0,3,2:T(8,128)(2,1)} %param.30) | copy-start | bytes 55300
  8.0 577.4 %all-reduce.8.cloned.1.call-start = ((), (), s32[]{:S(2)}) async-start(), calls=%async_computation.3 | async-start | bytes 278528
  80.6 36.2 %copy-start.6 = (bf16[16,256]{0,1:T(8,128)(2,1)}, bf16[16,256]{0,1:T(8,128)(2,1)S(1)}, u32[]{:S(2)}) copy-start(bf16[16,256]{0,1:T(8,128)(2,1)S(1)} %all_gather.9) | copy-start | bytes 24580
  100.8 6.2 collective-permute-start
  103.0 4.0 collective-permute-start.1
  105.7 41.1 %copy-start.15 = (s32[32,16]{0,1:T(8,128)}, s32[32,16]{0,1:T(8,128)S(1)}, u32[]{:S(2)}) copy-start(s32[32,16]{0,1:T(8,128)S(1)} %get-tuple-element.232) | copy-start | bytes 6148
  107.1 9.7 %collective-permute-start.2 = (bf16[32,24,4]{2,0,1:T(8,128)(2,1)S(1)}, bf16[32,24,4]{2,0,1:T(8,128)(2,1)S(1)}, u32[]{:S(2)}, u32[]{:S(2)}) collective-permute-start(bf16[32,24,4]{2,0,1:T(8,128)(2,1)S(1)} %get-tuple-element.217), channel_id=1, source_target_pairs={{0,1},{1,2},{2,3},{3,4},{4,5},{5,6},{6,7},{7,8},{8,9},{9,10},{10,1... | collective-permute-start | bytes 18440 | tf_op jit(solution)/shard_map/ppermute | solution.py:21
  110.9 7.8 collective-permute-start.3
  115.1 31.7 %copy-start.28 = (s32[512]{0:T(512)}, s32[512]{0:T(512)S(1)}, u32[]{:S(2)}) copy-start(s32[512]{0:T(512)S(1)} %add_multiply_fusion) | copy-start | bytes 6148
  119.4 42.7 %copy-start.18 = (bf16[32,32,3,3]{1,0,3,2:T(8,128)(2,1)S(1)}, bf16[32,32,3,3]{1,0,3,2:T(8,128)(2,1)}, u32[]{:S(2)}) copy-start(bf16[32,32,3,3]{1,0,3,2:T(8,128)(2,1)} %param.31) | copy-start | bytes 55300
  146.8 32.6 %copy-start.1 = (f32[32,16,512]{2,0,1:T(8,128)}, f32[32,16,512]{2,0,1:T(8,128)S(1)}, u32[]{:S(2)}) copy-start(f32[32,16,512]{2,0,1:T(8,128)S(1)} %get-tuple-element.237) | copy-start | bytes 3145732
  146.8 31.3 %copy-start.32 = (u32[256]{0:T(256)S(1)}, u32[256]{0:T(256)}, u32[]{:S(2)}) copy-start(u32[256]{0:T(256)} %constant.189) | copy-start | bytes 3076
  147.6 15.3 %collective-permute-start.4 = (bf16[32,4,512]{2,0,1:T(8,128)(2,1)S(1)}, bf16[32,4,512]{2,0,1:T(8,128)(2,1)S(1)}, u32[]{:S(2)}, u32[]{:S(2)}) collective-permute-start(bf16[32,4,512]{2,0,1:T(8,128)(2,1)S(1)} %get-tuple-element.223), channel_id=1, source_target_pairs={{0,32},{32,64},{64,96},{96,128},{128,160},{160,192},{192,224},{1,3... | collective-permute-start | bytes 393224 | tf_op jit(solution)/shard_map/ppermute | solution.py:21
  154.2 8.7 %collective-permute-start.5 = (bf16[32,4,512]{2,0,1:T(8,128)(2,1)S(1)}, bf16[32,4,512]{2,0,1:T(8,128)(2,1)S(1)}, u32[]{:S(2)}, u32[]{:S(2)}) collective-permute-start(bf16[32,4,512]{2,0,1:T(8,128)(2,1)S(1)} %get-tuple-element.224), channel_id=1, source_target_pairs={{32,0},{64,32},{96,64},{128,96},{160,128},{192,160},{224,192},{33,... | collective-permute-start | bytes 393224 | tf_op jit(solution)/shard_map/ppermute | solution.py:22
  163.7 15.7 %collective-permute-start.6 = (bf16[32,24,4]{2,0,1:T(8,128)(2,1)}, bf16[32,24,4]{2,0,1:T(8,128)(2,1)S(1)}, u32[]{:S(2)}, u32[]{:S(2)}) collective-permute-start(bf16[32,24,4]{2,0,1:T(8,128)(2,1)} %get-tuple-element.215), channel_id=1, source_target_pairs={{0,1},{1,2},{2,3},{3,4},{4,5},{5,6},{6,7},{7,8},{8,9},{9,10},{10,1... | collective-permute-start | bytes 18440 | tf_op jit(solution)/shard_map/ppermute | solution.py:21
  169.5 12.0 %collective-permute-start.7 = (bf16[32,24,4]{2,0,1:T(8,128)(2,1)S(1)}, bf16[32,24,4]{2,0,1:T(8,128)(2,1)S(1)}, u32[]{:S(2)}, u32[]{:S(2)}) collective-permute-start(bf16[32,24,4]{2,0,1:T(8,128)(2,1)S(1)} %get-tuple-element.216), channel_id=1, source_target_pairs={{1,0},{2,1},{3,2},{4,3},{5,4},{6,5},{7,6},{8,7},{9,8},{10,9},{11,1... | collective-permute-start | bytes 18440 | tf_op jit(solution)/shard_map/ppermute | solution.py:22
  214.8 6.2 collective-permute-start.8
  219.0 5.0 collective-permute-start.9
  224.8 14.3 %collective-permute-start.10 = (bf16[32,24,4]{2,0,1:T(8,128)(2,1)}, bf16[32,24,4]{2,0,1:T(8,128)(2,1)}, u32[]{:S(2)}, u32[]{:S(2)}) collective-permute-start(bf16[32,24,4]{2,0,1:T(8,128)(2,1)} %get-tuple-element.213), channel_id=1, source_target_pairs={{0,1},{1,2},{2,3},{3,4},{4,5},{5,6},{6,7},{7,8},{8,9},{9,10},{10,1... | collective-permute-start | bytes 18440 | tf_op jit(solution)/shard_map/ppermute | solution.py:21
  232.9 10.0 %collective-permute-start.11 = (bf16[32,24,4]{2,0,1:T(8,128)(2,1)}, bf16[32,24,4]{2,0,1:T(8,128)(2,1)}, u32[]{:S(2)}, u32[]{:S(2)}) collective-permute-start(bf16[32,24,4]{2,0,1:T(8,128)(2,1)} %get-tuple-element.214), channel_id=1, source_target_pairs={{1,0},{2,1},{3,2},{4,3},{5,4},{6,5},{7,6},{8,7},{9,8},{10,9},{11,1... | collective-permute-start | bytes 18440 | tf_op jit(solution)/shard_map/ppermute | solution.py:22
  244.6 34.1 %copy-start.2 = (f32[32,16,512]{2,0,1:T(8,128)S(1)}, f32[32,16,512]{2,0,1:T(8,128)}, u32[]{:S(2)}) copy-start(f32[32,16,512]{2,0,1:T(8,128)} %copy-done.1) | copy-start | bytes 3145732
  244.6 34.1 %copy-start.16 = (s32[32,16]{0,1:T(8,128)S(1)}, s32[32,16]{0,1:T(8,128)}, u32[]{:S(2)}) copy-start(s32[32,16]{0,1:T(8,128)} %copy-done.15) | copy-start | bytes 6148
  244.6 34.1 %copy-start.29 = (s32[512]{0:T(512)S(1)}, s32[512]{0:T(512)}, u32[]{:S(2)}) copy-start(s32[512]{0:T(512)} %copy-done.28) | copy-start | bytes 6148
  283.3 7.8 collective-permute-start.12
  289.0 4.2 collective-permute-start.13
  293.3 9.7 %collective-permute-start.14 = (bf16[32,24,4]{2,0,1:T(8,128)(2,1)S(1)}, bf16[32,24,4]{2,0,1:T(8,128)(2,1)S(1)}, u32[]{:S(2)}, u32[]{:S(2)}) collective-permute-start(bf16[32,24,4]{2,0,1:T(8,128)(2,1)S(1)} %get-tuple-element.211), channel_id=1, source_target_pairs={{0,1},{1,2},{2,3},{3,4},{4,5},{5,6},{6,7},{7,8},{8,9},{9,10},{10,1... | collective-permute-start | bytes 18440 | tf_op jit(solution)/shard_map/ppermute | solution.py:21
  297.8 9.2 %collective-permute-start.15 = (bf16[32,24,4]{2,0,1:T(8,128)(2,1)S(1)}, bf16[32,24,4]{2,0,1:T(8,128)(2,1)S(1)}, u32[]{:S(2)}, u32[]{:S(2)}) collective-permute-start(bf16[32,24,4]{2,0,1:T(8,128)(2,1)S(1)} %get-tuple-element.212), channel_id=1, source_target_pairs={{1,0},{2,1},{3,2},{4,3},{5,4},{6,5},{7,6},{8,7},{9,8},{10,9},{11,1... | collective-permute-start | bytes 18440 | tf_op jit(solution)/shard_map/ppermute | solution.py:22
  307.7 20.3 %copy-start.7 = (bf16[16,256]{0,1:T(8,128)(2,1)S(1)}, bf16[16,256]{0,1:T(8,128)(2,1)}, u32[]{:S(2)}) copy-start(bf16[16,256]{0,1:T(8,128)(2,1)} %copy-done.6) | copy-start | bytes 24580
  307.7 21.0 %copy-start.14 = (f32[9216]{0:T(1024)S(1)}, f32[9216]{0:T(1024)}, u32[]{:S(2)}) copy-start(f32[9216]{0:T(1024)} %reshape_reshape.7) | copy-start | bytes 110596
  329.3 502.9 %all-reduce.6.cloned.1.call-start = ((), (), s32[]{:S(2)}) async-start(), calls=%async_computation.2 | async-start | bytes 278528
  587.0 253.5 %reduce-scatter.2.cloned.1.call-start = ((), (), s32[]{:S(2)}) async-start(), calls=%async_computation.1 | async-start | bytes 294912 | tf_op jit(solution)/shard_map/reduce_scatter | solution.py:219
  (19 other events, 140.0 us)
Sparse Core Ops, SparseCore 0:
  329.5 255.9 all-reduce.7
  592.4 239.7 all-reduce.5
Sparse Core Ops, SparseCore 1:
  590.5 34.8 reduce-scatter.1
where the time goes:
time: 857 us; the launch traced here: 848 us
  waiting for transfers between devices  362 us (42%)
  blocking collectives  247 us (29%)
  local copies, waits for them, and re-layouts  79.8 us (9%)
  starting transfers between devices  64.4 us (8%)
  matrix products  38.6 us (5%)
  between operations  25 us (3%)
  loops' own time  18.1 us (2%)
  other arithmetic  12.9 us (2%)
    unnamed x5, waiting for transfers between devices  344 us
    unnamed x1, blocking collectives  157 us
    all_gather x1, blocking collectives, per_device(): band_full = lax.all_gather(band_emb, 'col', axis=1, tiled=True)  71.9 us
    conv_general_dilated x20, local copies, waits for them, and re-layouts, convolve(): lax.conv_general_dilated(window[None], kernel, (1, 1), 'VALID', rhs_dilat...  53.5 us
    ppermute x8, starting transfers between devices, extended(): before = lax.ppermute(last, axis, up)  41 us
    conv_general_dilated x4, matrix products, convolve(): lax.conv_general_dilated(window[None], kernel, (1, 1), 'VALID', rhs_dilat...  29.3 us
    ppermute x8, starting transfers between devices, extended(): after = lax.ppermute(first, axis, down)  23.3 us
    all_gather x1, blocking collectives, per_device(): col_full = lax.all_gather(col_emb, 'row', axis=1, tiled=True)  18.5 us
  transfers between devices with their start and end apart: 19, of which 10 were waited for; matrix products, arithmetic and copies ran while one was open for 2% of the time, Pallas kernels for 0%

commit v1 on v0

v1 whole, which is shorter than its diff:
```python
import functools

import jax
import jax.numpy as jnp
from jax import lax
from jax.experimental import pallas as pl
from jax.experimental.pallas import tpu as pltpu
from jax.sharding import PartitionSpec as P

tanh_scale = 0.7978845608028654
cubic_term = 0.044715
keep_boost = 4.0 / 3.0
slope_cubic = 3.0 * tanh_scale * cubic_term

K = 32
ROWS = 16
COLS = 512
WIDE = 640
TAPS = 9
BLK = 8 * K
HIGH = lax.Precision.HIGHEST
f32 = jnp.float32
bf16 = jnp.bfloat16
VMEM_LIMIT = 56 * 1024 * 1024


def dot(a, b, precision=None):
    return lax.dot_general(
        a, b, (((1,), (0,)), ((), ())), precision=precision, preferred_element_type=f32
    )


def dot_nt(a, b, precision=None):
    return lax.dot_general(
        a, b, (((1,), (1,)), ((), ())), precision=precision, preferred_element_type=f32
    )


def dot_tn(a, b, precision=None):
    return lax.dot_general(
        a, b, (((0,), (0,)), ((), ())), precision=precision, preferred_element_type=f32
    )


def iota(shape, dim):
    return lax.broadcasted_iota(jnp.int32, shape, dim)


def ahead(x, s):
    lane = iota((x.shape[0], 128), 1)
    turned = [pltpu.roll(x[:, i : i + 128], 128 - s, 1) for i in range(0, x.shape[1], 128)]
    nxt = turned[1:] + turned[:1]
    return jnp.concatenate(
        [jnp.where(lane >= 128 - s, n, t) for t, n in zip(turned, nxt)], axis=1
    )


def behind(x, s):
    lane = iota((x.shape[0], 128), 1)
    turned = [pltpu.roll(x[:, i : i + 128], s, 1) for i in range(0, x.shape[1], 128)]
    prv = turned[-1:] + turned[:-1]
    return jnp.concatenate([jnp.where(lane < s, p, t) for t, p in zip(turned, prv)], axis=1)


def mixed(base, factor):
    h = base * 668265261
    h = h ^ lax.shift_right_logical(h, 15)
    h = h * 374761393
    h = h ^ lax.shift_right_logical(h, 13)
    return jnp.where((h & 3) != 0, factor, 0.0)


def gelu_parts(v):
    v2 = v * v
    t = jnp.tanh(v * (tanh_scale + (tanh_scale * cubic_term) * v2))
    p = 0.5 + 0.5 * t
    value = v * p
    slope = p + value * (1.0 - t) * (tanh_scale + slope_cubic * v2)
    return value, slope


def pack_kernel(place, got_ref, cols_ref, out_ref):
    c = place[3]
    left = got_ref[lax.rem(c + 31, 32)].astype(f32)
    right = got_ref[lax.rem(c + 1, 32)].astype(f32)
    own = got_ref[c].astype(f32)
    lane = iota((16, 128), 1)
    low = jnp.where(lane < 64, right, left)
    high = jnp.where(
        lane < 16,
        pltpu.roll(right, 128 - 16, 1),
        jnp.where(lane < 112, own, pltpu.roll(left, 16, 1)),
    )
    out_ref[:, :COLS] = cols_ref[...]
    out_ref[:, COLS:WIDE] = jnp.concatenate([low, high], axis=0).astype(bf16)
    features = got_ref[...].astype(f32)[:, 0:8, :].reshape(256, 128).astype(bf16)
    pick = (iota((16, 128), 1) == iota((16, 128), 0) + 64).astype(f32).astype(bf16)
    band = dot_nt(pick, features)
    out_ref[:, WIDE:] = jnp.concatenate([band[:, :128], band[:, 128:]], axis=0).astype(bf16)


def main_kernel(
    place,
    got_ref,
    wr_ref,
    wc_ref,
    w1_ref,
    w2_ref,
    cot_ref,
    cot_up_ref,
    cot_down_ref,
    out_ref,
    send_ref,
    rowsum_ref,
    t1,
    t2,
    t2m,
    pv,
    hv,
    gv,
    g1,
    d1,
    acc,
    first_out,
    row3,
    qv,
    keep_rows,
    seed_rows,
    base_ref,
    keep_ref,
):
    s1 = place[0]
    s2 = place[1]
    r = place[2]
    c = place[3]

    spread = (iota((K, BLK), 1) // 8 == iota((K, BLK), 0)).astype(f32).astype(bf16)
    sub = iota((8, BLK), 0)
    far = iota((8, BLK), 1) % 8 - sub

    def hits(s, half):
        return [far + 8 * half == 4 + (a - 1) * s for a in range(3)]

    def build(target, weight, s, mirrored):
        masks = [hits(s, half) for half in range(2)]
        for b in range(3):
            grown = []
            for a in range(3):
                if mirrored:
                    grown.append(dot_tn(weight[(2 - a) * 3 + (2 - b)], spread))
                else:
                    grown.append(dot(weight[a * 3 + b], spread))
            for half in range(2):
                m = masks[half]
                whole = jnp.zeros((K, 8, BLK), f32)
                for a in range(3):
                    whole = jnp.where(
                        jnp.broadcast_to(m[a][None], (K, 8, BLK)),
                        jnp.broadcast_to(grown[a][:, None, :], (K, 8, BLK)),
                        whole,
                    )
                at = (half * 3 + b) * BLK
                target[:, at : at + BLK] = whole.reshape(BLK, BLK).astype(bf16)

    build(t1, w1_ref, s1, False)
    build(t2, w2_ref, s2, False)
    build(t2m, w2_ref, s2, True)

    q = jnp.zeros((K, WIDE), f32)
    for slot in range(8):
        at = place[4 + slot]
        weight = wc_ref[pl.ds(pl.multiple_of(at * K, K), K), :]
        q = q + dot_tn(weight, got_ref[slot, :, 0:WIDE])
    qv[0] = behind(q, s1)
    qv[1] = q
    qv[2] = ahead(q, s1)

    lane = iota((1, WIDE), 1)
    for step in range(3):
        slot = place[12 + step]
        low = wr_ref[0:128, :]
        high = wr_ref[128:256, :]
        row3[16 * step : 16 * step + 16, :] = dot(
            got_ref[slot, 0:16, WIDE:], low
        ) + dot(got_ref[slot, 16:32, WIDE:], high)
        seen = got_ref[slot, :, COLS:WIDE].astype(f32)
        sides = []
        for row, first in ((24, 32), (8, 32), (8, 64)):
            piece = seen[row : row + 1, first : first + 4]
            number = piece[:, 0:1] * 65536.0 + piece[:, 1:2] * 256.0 + piece[:, 2:3]
            sides.append((number, piece[:, 3:4]))
        row_ok = jnp.logical_and(r + step >= 1, r + step <= 8).astype(f32)
        right_ok = row_ok * (c < 31).astype(f32)
        left_ok = row_ok * (c > 0).astype(f32)
        keep = jnp.where(
            lane < COLS,
            sides[0][1] * row_ok,
            jnp.where(lane < 576, sides[1][1] * right_ok, sides[2][1] * left_ok),
        )
        seed = jnp.where(
            lane < COLS, sides[0][0], jnp.where(lane < 576, sides[1][0], sides[2][0])
        )
        seed_rows[step] = seed.astype(jnp.int32)
        keep_rows[step * 3 + 0] = behind(keep, s1)
        keep_rows[step * 3 + 1] = keep
        keep_rows[step * 3 + 2] = ahead(keep, s1)

    def pair_block(k, carry):
        rows = row3[pl.ds(pl.multiple_of(8 * k, 8), 8), :]
        step = k // 2
        for b in range(3):
            keep = keep_rows[step * 3 + b]
            for p in range(K // 2):
                parts = []
                for ch in (2 * p, 2 * p + 1):
                    parts.append(keep * (rows[:, ch : ch + 1] + qv[b, ch : ch + 1, :]))
                at = pl.multiple_of(k * 3 * BLK + b * BLK + 16 * p, 16)
                pv[pl.ds(at, 16), :] = jnp.concatenate(parts, axis=0).astype(bf16)
        return carry

    lax.fori_loop(0, 6, pair_block, 0)

    column = iota((8, WIDE), 1)
    column = c * COLS + jnp.where(column < 576, column, column - WIDE)

    def prepare(first_row, layer):
        local = first_row + iota((8, WIDE), 0)
        seed = jnp.where(
            local < 0, seed_rows[0], jnp.where(local < ROWS, seed_rows[1], seed_rows[2])
        )
        keep = jnp.where(
            local < 0, keep_rows[1], jnp.where(local < ROWS, keep_rows[4], keep_rows[7])
        )
        base = seed * 1000003 + layer * 7919
        base = base ^ ((r * ROWS + local) * 19349663)
        base_ref[...] = base ^ (column * 83492791)
        keep_ref[...] = keep * keep_boost

    def factor_of(p):
        keep = keep_ref[...]
        base = base_ref[...]
        parts = [mixed(base ^ (ch * 73856093), keep) for ch in (2 * p, 2 * p + 1)]
        return jnp.concatenate(parts, axis=0)

    def store_shifted(target, block, p, values, s):
        for b, moved in enumerate((behind(values, s), values, ahead(values, s))):
            at = pl.multiple_of(block * 3 * BLK + b * BLK + 16 * p, 16)
            target[pl.ds(at, 16), :] = moved.astype(bf16)

    for k in range(5):
        acc[...] = dot(t1[...], pv[k * 3 * BLK : (k + 2) * 3 * BLK, :])
        prepare(8 * k - 12, 1)

        def hidden_pair(p, carry, k=k):
            at = pl.multiple_of(16 * p, 16)
            value, slope = gelu_parts(acc[pl.ds(at, 16), :])
            factor = factor_of(p)
            store_shifted(hv, k, p, factor * value, s2)
            if 1 <= k <= 3:
                d1[pl.ds(pl.multiple_of((k - 1) * BLK + 16 * p, 16), 16), :] = factor * slope
            return carry

        lax.fori_loop(0, K // 2, hidden_pair, 0, unroll=4)

    for k in range(4):
        acc[...] = dot(t2[...], hv[k * 3 * BLK : (k + 2) * 3 * BLK, :])
        prepare(8 * k - 8, 2)

        def grad_pair_of(p, carry, k=k):
            at = pl.multiple_of(16 * p, 16)
            value, slope = gelu_parts(acc[pl.ds(at, 16), :])
            factor = factor_of(p)
            if k == 0:
                cot = cot_up_ref[pl.ds(at, 16), :].astype(f32)
            elif k == 3:
                cot = cot_down_ref[pl.ds(at, 16), :].astype(f32)
            else:
                parts = []
                for ch in (2 * p, 2 * p + 1):
                    parts.append(cot_ref[ch].astype(f32)[8 * (k - 1) : 8 * k])
                cot = jnp.concatenate(parts, axis=0)
            store_shifted(gv, k, p, cot * factor * slope, s2)
            if k == 1:
                first_out[pl.ds(at, 16), :] = (factor * value)[:, :COLS]
            if k == 2:
                upper = first_out[pl.ds(at, 16), :]
                lower = (factor * value)[:, :COLS]
                for i in range(2):
                    both = jnp.concatenate(
                        [upper[8 * i : 8 * i + 8], lower[8 * i : 8 * i + 8]], axis=0
                    )
                    out_ref[2 * p + i] = both.astype(bf16)
            return carry

        lax.fori_loop(0, K // 2, grad_pair_of, 0, unroll=4)

    for k in range(3):
        hidden_grad = dot(t2m[...], gv[k * 3 * BLK : (k + 2) * 3 * BLK, :])
        g1[k * BLK : (k + 1) * BLK, :] = (hidden_grad * d1[k * BLK : (k + 1) * BLK, :]).astype(
            bf16
        )

    crossed = []
    for half in range(2):
        total = jnp.zeros((BLK, 3 * BLK), f32)
        for k in (1, 2):
            start = k * 3 * BLK + BLK
            grads = gv[start : start + BLK, 0:COLS]
            start = (k + half) * 3 * BLK
            total = total + dot_nt(grads, hv[start : start + 3 * BLK, 0:COLS])
        crossed.append(total)
    gather8 = (iota((3 * BLK, 96), 0) // 8 == iota((3 * BLK, 96), 1)).astype(f32)
    masks = [hits(s2, half) for half in range(2)]
    second_rows = []
    for a in range(3):
        found = jnp.zeros((K, 8, 3 * BLK), f32)
        for half in range(2):
            m = jnp.concatenate([masks[half][a].astype(f32)] * 3, axis=1)
            found = found + crossed[half].reshape(K, 8, 3 * BLK) * m[None]
        second_rows.append(dot(jnp.sum(found, axis=1), gather8, HIGH))
    second_total = jnp.concatenate(second_rows, axis=0)

    place_j = iota((WIDE, 384), 0)
    place_j = jnp.where(place_j < 576, place_j, place_j - WIDE)
    moved_j = place_j + (iota((WIDE, 384), 1) // 128 - 1) * s1
    window = jnp.logical_and(moved_j >= 0, moved_j < COLS).astype(f32).astype(bf16)
    by_row = dot(g1[...], window)
    which = iota((3 * BLK, 384), 0)
    which = which // BLK * 8 + which % 8
    by_row = jnp.where(iota((3 * BLK, 384), 1) % 128 == which, by_row, 0.0)
    same = (iota((K, 3 * BLK), 1) % BLK // 8 == iota((K, 3 * BLK), 0)).astype(f32)
    by_row = dot(same, by_row, HIGH)
    across = iota((96, 3 * BLK), 1)
    down = iota((96, 3 * BLK), 0)
    moved_i = across // BLK * 8 + across % 8 - 4 + (down // K - 1) * s1
    inside = jnp.logical_and(moved_i >= 0, moved_i < ROWS)
    inside = jnp.logical_and(inside, across % BLK // 8 == down % K)
    by_col = dot(inside.astype(f32).astype(bf16), g1[...])
    by_col = [ahead(by_col, s1), by_col, behind(by_col, s1)]

    keep_own = keep_rows[4][:, 0:1]
    slot = place[13]
    band = jnp.concatenate([got_ref[slot, 0:16, WIDE:], got_ref[slot, 16:32, WIDE:]], axis=1)
    row_t = dot_tn(wr_ref[...], jnp.concatenate([band.T, jnp.zeros((256, 112), bf16)], axis=1))

    col_sum = jnp.zeros((K, WIDE), f32)
    row_sum = jnp.zeros((K, 128), f32)
    first_cols = []
    row_taps = []
    for a in range(3):
        seen = jnp.zeros((K, 128), f32)
        for b in range(3):
            seen = seen + dot_tn(
                w1_ref[a * 3 + b].astype(f32), by_row[:, 128 * b : 128 * b + 128], HIGH
            )
        row_sum = row_sum + pltpu.roll(seen, 128 - (4 - (a - 1) * s1), 1)
    for b in range(3):
        flat = jnp.concatenate([w1_ref[a * 3 + b] for a in range(3)], axis=0).astype(f32)
        col_sum = col_sum + dot_tn(flat, by_col[b], HIGH)
        from_cols = dot_nt(by_col[b][:, :COLS], q[:, :COLS], HIGH)
        from_rows = []
        for a in range(3):
            moved = pltpu.roll(by_row[:, 128 * b : 128 * b + 128], 128 - (4 - (a - 1) * s1), 1)
            from_rows.append(dot_nt(moved, row_t, HIGH))
        first_cols.append(from_cols + jnp.concatenate(from_rows, axis=0))
    first_total = jnp.concatenate(first_cols, axis=1) * keep_own
    rowsum_ref[...] = row_sum * keep_own

    col_sum = (col_sum * keep_own).astype(bf16)
    blank = jnp.zeros((96, 32), f32)
    both = jnp.concatenate(
        [
            jnp.concatenate([first_total, blank], axis=1),
            jnp.concatenate([second_total, blank], axis=1),
        ],
        axis=0,
    )
    for to in range(8):
        for g in range(4):
            send_ref[to, 32 * g : 32 * g + 32, :] = col_sum[:, 128 * g : 128 * g + 128]
        piece = jnp.concatenate([both[24 * to : 24 * to + 24], jnp.zeros((8, 128), f32)], axis=0)
        send_ref[to, 128:160, :] = piece.astype(bf16)


def middle_kernel(place, got_ref, cols_ref, wc_ref, rowsum_ref, gcols_ref, send_ref):
    r = place[2]
    total = got_ref[0].astype(f32)
    for i in range(1, 8):
        total = total + got_ref[i].astype(f32)
    weight = wc_ref[pl.ds(pl.multiple_of(r * K, K), K), :].astype(f32)
    grad_w = jnp.zeros((K, K), f32)
    for g in range(4):
        part = total[32 * g : 32 * g + 32, :]
        gcols_ref[:, 128 * g : 128 * g + 128] = dot(weight, part, HIGH).astype(bf16)
        grad_w = grad_w + dot_nt(cols_ref[:, 128 * g : 128 * g + 128].astype(f32), part, HIGH)
    packed = jnp.concatenate([grad_w[8 * g : 8 * g + 8] for g in range(4)], axis=1)
    send_ref[:, 0:128] = jnp.concatenate([total[128:152], packed], axis=0)
    send_ref[:, 128:256] = rowsum_ref[...]


def sum_kernel(got_ref, send_ref):
    line = jnp.sum(got_ref[...], axis=0, keepdims=True)
    send_ref[...] = jnp.broadcast_to(line[None], send_ref.shape)


def last_kernel(place, got_ref, all_ref, wr_ref, gband_ref, gwr_ref, gwc_ref, g1_ref, g2_ref):
    r = place[2]
    c = place[3]
    pieces = [got_ref[i] for i in range(8)]
    whole = jnp.concatenate([piece[0:24, 0:128] for piece in pieces], axis=0)
    for a in range(3):
        for b in range(3):
            g1_ref[a * 3 + b] = whole[32 * a : 32 * a + 32, 32 * b : 32 * b + 32]
            g2_ref[a * 3 + b] = whole[96 + 32 * a : 128 + 32 * a, 32 * b : 32 * b + 32]
    gwr = jnp.zeros((K, 256), f32)
    gwc = []
    for i in range(8):
        for g in range(4):
            gwc.append(pieces[i][24:32, 32 * g : 32 * g + 32])
    gwc_ref[...] = jnp.concatenate(gwc, axis=0)
    for slot in range(8):
        at = place[4 + slot]
        rows = got_ref[at, :, 128:144]
        low = dot(rows, all_ref[slot, 0:16, WIDE:].astype(f32), HIGH)
        high = dot(rows, all_ref[slot, 16:32, WIDE:].astype(f32), HIGH)
        gwr = gwr + jnp.concatenate([low, high], axis=1)
    gwr_ref[...] = gwr
    mine = wr_ref[pl.ds(pl.multiple_of(c * 8, 8), 8), :]
    gband_ref[...] = dot(mine, got_ref[r, :, 128:144], HIGH).astype(bf16)


def spaces(count, with_place=True):
    whole = [pl.BlockSpec(memory_space=pltpu.VMEM)] * count
    if with_place:
        return [pl.BlockSpec(memory_space=pltpu.SMEM)] + whole
    return whole


def call(kernel, shapes, args, scratch=(), with_place=True):
    return pl.pallas_call(
        kernel,
        out_shape=shapes,
        in_specs=spaces(len(args) - int(with_place), with_place),
        out_specs=jax.tree.map(lambda _: pl.BlockSpec(memory_space=pltpu.VMEM), shapes),
        scratch_shapes=list(scratch),
        compiler_params=pltpu.CompilerParams(vmem_limit_bytes=VMEM_LIMIT),
    )(*args)


def shape(dims, kind):
    return jax.ShapeDtypeStruct(dims, kind)


def per_device(
    band_emb,
    col_emb,
    w_row,
    w_col,
    first_kernel_weight,
    second_kernel_weight,
    cotangent,
    drop_seeds,
    tile_mask,
    dilations,
):
    r = lax.axis_index("row")
    c = lax.axis_index("col")
    rows = lax.axis_size("row")
    cols = lax.axis_size("col")
    order = jnp.arange(8, dtype=jnp.int32)
    around = jnp.stack([(r + 7) % 8, r, (r + 1) % 8]).astype(jnp.int32)
    place = jnp.concatenate(
        [dilations, jnp.stack([r, c]).astype(jnp.int32), order, around, jnp.zeros((1,), jnp.int32)]
    )

    east = [(i, (i + 1) % cols) for i in range(cols - 1)]
    west = [(j, i) for i, j in east]
    south = [(i, (i + 1) % rows) for i in range(rows - 1)]
    north = [(j, i) for i, j in south]
    right = lax.ppermute(cotangent[:, :, :8], "col", west)
    left = lax.ppermute(cotangent[:, :, COLS - 8 :], "col", east)

    cols_t = col_emb.T
    seed = drop_seeds.reshape(1, 1)
    numbers = jnp.concatenate(
        [seed >> 16 & 255, seed >> 8 & 255, seed & 255, tile_mask.reshape(1, 1)], axis=1
    ).astype(bf16)
    edge = jnp.zeros((16, 128), bf16)
    edge = edge.at[:, 0:16].set(cols_t[0:16, 0:16])
    edge = edge.at[:, 16:32].set(cols_t[16:32, 0:16])
    edge = edge.at[8:9, 32:36].set(numbers)
    edge = edge.at[8:9, 64:68].set(numbers)
    edge = edge.at[0:8, 64:80].set(band_emb.T)
    edge = edge.at[:, 96:112].set(cols_t[16:32, COLS - 16 :])
    edge = edge.at[:, 112:128].set(cols_t[0:16, COLS - 16 :])
    got = lax.all_to_all(jnp.broadcast_to(edge[None], (32, 16, 128)), "col", 0, 0)
    packed = call(pack_kernel, shape((32, 768), bf16), (place, got, cols_t))

    gap = jnp.zeros((K, ROWS, 112), bf16)
    cot_ext = jnp.concatenate([cotangent, right, gap, left], axis=2)
    cot_up = lax.ppermute(cot_ext[:, 8:, :].reshape(BLK, WIDE), "row", south)
    cot_down = lax.ppermute(cot_ext[:, :8, :].reshape(BLK, WIDE), "row", north)

    features = lax.all_to_all(jnp.broadcast_to(packed[None], (8, 32, 768)), "row", 0, 0)

    w1 = jnp.transpose(first_kernel_weight, (2, 3, 0, 1)).reshape(TAPS, K, K)
    w2 = jnp.transpose(second_kernel_weight, (2, 3, 0, 1)).reshape(TAPS, K, K)
    out_map, sums, row_sum = call(
        main_kernel,
        (
            shape((K, ROWS, COLS), bf16),
            shape((8, 160, 128), bf16),
            shape((K, 128), f32),
        ),
        (place, features, w_row, w_col, w1, w2, cot_ext, cot_up, cot_down),
        scratch=(
            pltpu.VMEM((BLK, 6 * BLK), bf16),
            pltpu.VMEM((BLK, 6 * BLK), bf16),
            pltpu.VMEM((BLK, 6 * BLK), bf16),
            pltpu.VMEM((18 * BLK, WIDE), bf16),
            pltpu.VMEM((15 * BLK, WIDE), bf16),
            pltpu.VMEM((12 * BLK, WIDE), bf16),
            pltpu.VMEM((3 * BLK, WIDE), bf16),
            pltpu.VMEM((3 * BLK, WIDE), f32),
            pltpu.VMEM((BLK, WIDE), f32),
            pltpu.VMEM((BLK, COLS), f32),
            pltpu.VMEM((48, K), f32),
            pltpu.VMEM((3, K, WIDE), f32),
            pltpu.VMEM((9, 1, WIDE), f32),
            pltpu.VMEM((3, 1, WIDE), jnp.int32),
            pltpu.VMEM((8, WIDE), jnp.int32),
            pltpu.VMEM((8, WIDE), f32),
        ),
    )

    got = lax.all_to_all(sums, "row", 0, 0)
    grad_cols, terms = call(
        middle_kernel,
        (shape((K, COLS), bf16), shape((32, 256), f32)),
        (place, got, cols_t, w_col, row_sum),
    )
    got = lax.all_to_all(terms, "col", 0, 0, tiled=True)
    line = call(sum_kernel, shape((256, 1, 256), f32), (got,), with_place=False)
    got = lax.all_to_all(line, ("row", "col"), 0, 0, tiled=True).reshape(8, 32, 256)
    grad_band, grad_w_row, grad_w_col, grad_one, grad_two = call(
        last_kernel,
        (
            shape((8, ROWS), bf16),
            shape((K, 256), f32),
            shape((256, K), f32),
            shape((TAPS, K, K), f32),
            shape((TAPS, K, K), f32),
        ),
        (place, got, features, w_row.astype(f32)),
    )
    unfold = lambda x: jnp.transpose(x.reshape(3, 3, K, K), (2, 3, 0, 1))
    return (
        out_map,
        grad_band.T,
        grad_cols.T,
        grad_w_row.T,
        grad_w_col,
        unfold(grad_one),
        unfold(grad_two),
    )


def solution(mesh):
    placed = (
        P("row", "col"),
        P("col", "row"),
        P(),
        P(),
        P(),
        P(),
        P(None, "row", "col"),
        P("row", "col"),
        P("row", "col"),
        P(),
    )
    return jax.shard_map(
        per_device,
        mesh=mesh,
        in_specs=placed,
        out_specs=(P(None, "row", "col"), P("row", "col"), P("col", "row"), P(), P(), P(), P()),
        check_vma=False,
    )
```

time: 857 us -> 160 us (0.19)
  waiting for transfers between devices: 362 us -> 21.4 us
  blocking collectives: 247 us -> 39.3 us
  local copies, waits for them, and re-layouts: 79.8 us -> 14.9 us
  matrix products: 38.6 us -> 0 us
  Pallas kernels: 0 us -> 35.2 us
  starting transfers between devices: 64.4 us -> 34.3 us
  between operations: 25 us -> 2.17 us
  loops' own time: 18.1 us -> 0 us
    unnamed x5 -> x0, waiting for transfers between devices: 344 us -> none
    unnamed x1 -> x0, blocking collectives: 157 us -> none
    all_gather x2 -> x0, blocking collectives: 90.3 us -> none  [the longest x1 71.9 us: per_device(): band_full = lax.all_gather(band_emb, 'col', axis=1, tiled=True)]
    ppermute x16 -> x4, starting transfers between devices: 64.3 us -> 10.7 us  [the longest x1 4.87 us: per_device(): right = lax.ppermute(cotangent[:, :, :8], 'col', west)]
    conv_general_dilated x20 -> x0, local copies, waits for them, and re-layouts: 53.5 us -> none  [convolve(): lax.conv_general_dilated(window[None], kernel, (1, 1), 'VALID', rhs_dilat...]
    all_to_all x0 -> x2, blocking collectives: none -> 39.3 us  [the longest x1 24.7 us: per_device(): got = lax.all_to_all(sums, 'row', 0, 0)]
    pallas_call x0 -> x5, Pallas kernels: none -> 35.2 us  [call(): pl.pallas_call(kernel, out_shape=shapes, in_specs=spaces(len(args) - int(...]
    conv_general_dilated x4 -> x0, matrix products: 29.3 us -> none  [convolve(): lax.conv_general_dilated(window[None], kernel, (1, 1), 'VALID', rhs_dilat...]
  transfers between devices with their start and end apart: 19 -> 7, of which waited for: 10 -> 3; matrix products, arithmetic and copies ran while one was open for 2% -> 3% of each run, Pallas kernels for 0% -> 1%
where the time goes in v1:
time: 160 us; the launch traced here: 157 us
  blocking collectives  39.3 us (25%)
  Pallas kernels  35.2 us (22%)
  starting transfers between devices  34.3 us (21%)
  waiting for transfers between devices  21.4 us (13%)
  local copies, waits for them, and re-layouts  14.9 us (9%)
  other arithmetic  9.6 us (6%)
  between operations  2.17 us (1%)
    pallas_call x5, Pallas kernels, call(): pl.pallas_call(kernel, out_shape=shapes, in_specs=spaces(len(args) - int(...  35.2 us
    all_to_all x1, blocking collectives, per_device(): got = lax.all_to_all(sums, 'row', 0, 0)  24.7 us
    all_to_all x1, blocking collectives, per_device(): got = lax.all_to_all(terms, 'col', 0, 0, tiled=True)  14.6 us
    all_to_all x1, waiting for transfers between devices, per_device(): lax.all_to_all(line, ('row', 'col'), 0, 0, tiled=True).reshape(8, 32, 256)  13.6 us
    all_to_all x1, starting transfers between devices, per_device(): lax.all_to_all(jnp.broadcast_to(edge[None], (32, 16, 128)), 'col', 0, 0)  8.92 us
    another operation x7, other arithmetic  7.92 us
    all_to_all x1, starting transfers between devices, per_device(): lax.all_to_all(jnp.broadcast_to(packed[None], (8, 32, 768)), 'row', 0, 0)  7.57 us
    all_to_all x1, starting transfers between devices, per_device(): lax.all_to_all(line, ('row', 'col'), 0, 0, tiled=True).reshape(8, 32, 256)  7.12 us
  transfers between devices with their start and end apart: 7, of which 3 were waited for; matrix products, arithmetic and copies ran while one was open for 3% of the time, Pallas kernels for 1%

profile of v1, /device:TPU:6, one launch (start us, length us, event | category | flops | bytes accessed | tf_op | source)
XLA Modules:
  0.0 156.9 jit_solution(7085990484351421117)
XLA Ops:
  4.5 1.3 and_reduce_fusion
  5.8 2.0 %slice_select_fusion.1 = (bf16[16,16]{1,0:T(8,128)(2,1)S(1)}, bf16[16,16]{1,0:T(8,128)(2,1)S(1)}) fusion(bf16[32,512]{1,0:T(8,128)(2,1)} %bitcast.34, pred[]{:T(512)} %compare_reduce_fusion.1, pred[]{:T(512)} %compare_reduce_fusion.2), kind=kLoop, calls=%fused_computation.5 | loop fusion | flops 512 | bytes 2050 | tf_op jit(solution)/shard_map/select.8
  8.6 2.7 %bitcast_select_fusion = bf16[8,16]{1,0:T(8,128)(2,1)S(1)} fusion(bf16[16,8]{0,1:T(8,128)(2,1)} %param.24, bf16[16,128]{1,0:T(8,128)(2,1)S(1)} %scatter.29, s32[]{:T(128)} %bitcast.6, s32[]{:T(128)} %bitcast.7, pred[]{:T(512)} %and_reduce_fusion), kind=kLoop, calls=%fused_computation.7 | loop fusion | flops 128 | bytes 777 | tf_op jit(solution)/shard_map/select.11
  11.3 1.8 %scatter.30 = bf16[16,128]{1,0:T(8,128)(2,1)S(1)} dynamic-update-slice(bf16[16,128]{1,0:T(8,128)(2,1)S(1)} %scatter.29, bf16[8,16]{1,0:T(8,128)(2,1)S(1)} %bitcast_select_fusion, s32[]{:T(128)} %bitcast.6, s32[]{:T(128)} %bitcast.7) | dynamic-update-slice | bytes 516 | tf_op jit(solution)/shard_map/scatter | solution.py:493
  13.1 1.4 fusion.1
  15.0 0.7 broadcast_in_dim.6
  15.7 8.9 %all-to-all-start = ((bf16[32,16,128]{2,1,0:T(8,128)(2,1)}), bf16[32,16,128]{2,1,0:T(8,128)(2,1)S(1)}, u32[]{:S(2)}, u32[]{:S(2)}) async-start(bf16[32,16,128]{2,1,0:T(8,128)(2,1)} %broadcast_in_dim.6), calls=%async_computation | async-start | bytes 262144 | tf_op jit(solution)/shard_map/all_to_all | solution.py:496
  24.7 4.9 %collective-permute-start = (bf16[32,16,8]{2,1,0:T(8,128)(2,1)S(1)}, bf16[32,16,8]{2,1,0:T(8,128)(2,1)S(1)}, u32[]{:S(2)}, u32[]{:S(2)}) collective-permute-start(bf16[32,16,8]{2,1,0:T(8,128)(2,1)S(1)} %get-tuple-element.134), channel_id=1, source_target_pairs={{1,0},{2,1},{3,2},{4,3},{5,4},{6,5},{7,6},{8,7},{9,8},{10,9},{11,1... | collective-permute-start | bytes 24584 | tf_op jit(solution)/shard_map/ppermute | solution.py:480
  29.6 1.9 %collective-permute-start.1 = (bf16[32,16,8]{2,1,0:T(8,128)(2,1)S(1)}, bf16[32,16,8]{2,1,0:T(8,128)(2,1)S(1)}, u32[]{:S(2)}, u32[]{:S(2)}) collective-permute-start(bf16[32,16,8]{2,1,0:T(8,128)(2,1)S(1)} %get-tuple-element.135), channel_id=1, source_target_pairs={{0,1},{1,2},{2,3},{3,4},{4,5},{5,6},{6,7},{7,8},{8,9},{9,10},{10,1... | collective-permute-start | bytes 24584 | tf_op jit(solution)/shard_map/ppermute | solution.py:481
  33.0 1.7 %shard_map.153 = bf16[32,768]{1,0:T(8,128)(2,1)} custom-call(s32[16]{0:T(128)} %concatenate.32.place, bf16[32,16,128]{2,1,0:T(8,128)(2,1)} %copy-done.3, bf16[32,512]{1,0:T(8,128)(2,1)} %bitcast.36), custom_call_target="tpu_custom_call" | custom-call | tf_op jit(solution)/shard_map/pallas_call | solution.py:440
  34.7 1.6 %broadcast_in_dim.7 = bf16[8,32,768]{2,1,0:T(8,128)(2,1)} broadcast(bf16[32,768]{1,0:T(8,128)(2,1)} %shard_map.153), dimensions={1,2} | broadcast | bytes 442368 | tf_op jit(solution)/shard_map/broadcast_in_dim | solution.py:504
  36.2 7.6 %all-to-all-start.1 = ((bf16[8,32,768]{2,1,0:T(8,128)(2,1)}), bf16[8,32,768]{2,1,0:T(8,128)(2,1)S(1)}, u32[]{:S(2)}, u32[]{:S(2)}) async-start(bf16[8,32,768]{2,1,0:T(8,128)(2,1)} %broadcast_in_dim.7), calls=%async_computation.1 | async-start | bytes 786432 | tf_op jit(solution)/shard_map/all_to_all | solution.py:504
  44.1 0.7 copy-done
  44.9 2.4 %collective-permute-start.2 = (bf16[256,640]{1,0:T(8,128)(2,1)S(1)}, bf16[256,640]{1,0:T(8,128)(2,1)S(1)}, u32[]{:S(2)}, u32[]{:S(2)}) collective-permute-start(bf16[256,640]{1,0:T(8,128)(2,1)S(1)} %get-tuple-element.133), channel_id=1, source_target_pairs={{0,32},{32,64},{64,96},{96,128},{128,160},{160,192},{192,224},{1,3... | collective-permute-start | bytes 983048 | tf_op jit(solution)/shard_map/ppermute | solution.py:501
  47.3 1.5 collective-permute-start.3
  48.8 0.7 copy.29.wc_ref
  49.5 0.7 copy.28.wr_ref
  50.2 2.6 %collective-permute-done.3.cot_down_ref = bf16[256,640]{1,0:T(8,128)(2,1)S(1)} collective-permute-done((bf16[256,640]{1,0:T(8,128)(2,1)S(1)}, bf16[256,640]{1,0:T(8,128)(2,1)S(1)}, u32[]{:S(2)}, u32[]{:S(2)}) %collective-permute-start.3) | collective-permute-done | bytes 327712 | tf_op jit(solution)/shard_map/ppermute | solution.py:502
  52.8 5.2 %all-to-all-done.1.got_ref.all_ref = bf16[8,32,768]{2,1,0:T(8,128)(2,1)S(1)} async-done(((bf16[8,32,768]{2,1,0:T(8,128)(2,1)}), bf16[8,32,768]{2,1,0:T(8,128)(2,1)S(1)}, u32[]{:S(2)}, u32[]{:S(2)}) %all-to-all-start.1) | async-done | bytes 393248 | tf_op jit(solution)/shard_map/all_to_all | solution.py:504
  58.0 0.8 copy-done.1
  58.8 27.7 %shard_map.154 = (bf16[32,16,512]{2,1,0:T(8,128)(2,1)}, bf16[8,160,128]{2,1,0:T(8,128)(2,1)}, f32[32,128]{1,0:T(8,128)}) custom-call(s32[16]{0:T(128)} %concatenate.32.place, bf16[8,32,768]{2,1,0:T(8,128)(2,1)} %copy-done.1, bf16[256,32]{1,0:T(8,128)(2,1)} %copy.28.wr_ref, bf16[256,32]{1,0:T(8,128)(2,1)} %copy.29.wc_ref, bf16[9,32,32]{2,1,0:T(8,128)(2,1)} %bitcast.39, ...), custom_call_target="tpu_custom_call" | custom-call | tf_op jit(solution)/shard_map/pallas_call | solution.py:440
  86.6 24.7 %all_to_all.31.got_ref = bf16[8,160,128]{2,1,0:T(8,128)(2,1)} all-to-all(bf16[8,160,128]{2,1,0:T(8,128)(2,1)} %get-tuple-element.102), channel_id=1, replica_groups=mesh['row'=8,'col'=32] {'row'}, dimensions={0} | all-to-all | bytes 655360 | tf_op jit(solution)/shard_map/all_to_all | solution.py:536
  111.2 2.0 %shard_map.155 = (bf16[32,512]{1,0:T(8,128)(2,1)}, f32[32,256]{1,0:T(8,128)}) custom-call(s32[16]{0:T(128)} %concatenate.32.place, bf16[8,160,128]{2,1,0:T(8,128)(2,1)} %all_to_all.31.got_ref, bf16[32,512]{1,0:T(8,128)(2,1)} %bitcast.37, bf16[256,32]{1,0:T(8,128)(2,1)} %copy.29.wc_ref, f32[32,128]{1,0:T(8,128)} %get-tuple-element.103.rowsum_ref), custom_call_target="tpu_custom_call" | custom-call | tf_op jit(solution)/shard_map/pallas_call | solution.py:440
  113.3 0.8 copy.31
  114.0 14.6 %all_to_all.32 = f32[32,1,256]{2,1,0:T(1,128)S(1)} all-to-all(f32[32,1,256]{2,1,0:T(1,128)S(1)} %copy.31), channel_id=1, replica_groups=mesh['row'=8,'col'=32] {'col'}, dimensions={0} | all-to-all | bytes 65536 | tf_op jit(solution)/shard_map/all_to_all | solution.py:542
  129.3 1.5 shard_map.156
  130.8 7.1 %all-to-all-start.4 = ((f32[256,1,256]{2,1,0:T(1,128)}), f32[256,1,256]{2,1,0:T(1,128)S(1)}, u32[]{:S(2)}, u32[]{:S(2)}) async-start(f32[256,1,256]{2,1,0:T(1,128)} %shard_map.156), calls=%async_computation.4 | async-start | bytes 524288 | tf_op jit(solution)/shard_map/all_to_all | solution.py:544
  137.9 0.8 copy.32.wr_ref
  138.7 13.6 %all-to-all-done.4 = f32[256,1,256]{2,1,0:T(1,128)S(1)} async-done(((f32[256,1,256]{2,1,0:T(1,128)}), f32[256,1,256]{2,1,0:T(1,128)S(1)}, u32[]{:S(2)}, u32[]{:S(2)}) %all-to-all-start.4) | async-done | bytes 262176 | tf_op jit(solution)/shard_map/all_to_all | solution.py:544
  152.3 0.7 copy.35
  153.0 2.2 %shard_map.157 = (bf16[8,16]{1,0:T(8,128)(2,1)}, f32[32,256]{1,0:T(8,128)}, f32[256,32]{1,0:T(8,128)}, f32[9,32,32]{2,1,0:T(8,128)}, f32[9,32,32]{2,1,0:T(8,128)}) custom-call(s32[16]{0:T(128)} %concatenate.32.place, f32[8,32,256]{2,1,0:T(8,128)} %bitcast.33, bf16[8,32,768]{2,1,0:T(8,128)(2,1)} %copy-done.1, f32[256,32]{1,0:T(8,128)} %copy.32.wr_ref), custom_call_target="tpu_custom_call" | custom-call | tf_op jit(solution)/shard_map/pallas_call | solution.py:440
  155.3 1.6 %copy.33 = f32[256,32]{0,1:T(8,128)} copy(f32[256,32]{1,0:T(8,128)} %get-tuple-element.129) | data formatting | bytes 65536
  (40 shorter events, 6.2 us)
Async XLA Ops:
  0.6 24.0 %copy-start.2 = (bf16[32,16,512]{2,1,0:T(8,128)(2,1)S(1)}, bf16[32,16,512]{2,1,0:T(8,128)(2,1)}, u32[]{:S(2)}) copy-start(bf16[32,16,512]{2,1,0:T(8,128)(2,1)} %param.30) | copy-start | bytes 1572868
  0.6 31.0 %copy-start.8 = (s32[2]{0:T(128)S(1)}, s32[2]{0:T(128)}, u32[]{:S(2)}) copy-start(s32[2]{0:T(128)} %param.33) | copy-start | bytes 28
  15.7 16.6 %all-to-all-start = ((bf16[32,16,128]{2,1,0:T(8,128)(2,1)}), bf16[32,16,128]{2,1,0:T(8,128)(2,1)S(1)}, u32[]{:S(2)}, u32[]{:S(2)}) async-start(bf16[32,16,128]{2,1,0:T(8,128)(2,1)} %broadcast_in_dim.6), calls=%async_computation | async-start | bytes 262144 | tf_op jit(solution)/shard_map/all_to_all | solution.py:496
  24.7 19.1 %collective-permute-start = (bf16[32,16,8]{2,1,0:T(8,128)(2,1)S(1)}, bf16[32,16,8]{2,1,0:T(8,128)(2,1)S(1)}, u32[]{:S(2)}, u32[]{:S(2)}) collective-permute-start(bf16[32,16,8]{2,1,0:T(8,128)(2,1)S(1)} %get-tuple-element.134), channel_id=1, source_target_pairs={{1,0},{2,1},{3,2},{4,3},{5,4},{6,5},{7,6},{8,7},{9,8},{10,9},{11,1... | collective-permute-start | bytes 24584 | tf_op jit(solution)/shard_map/ppermute | solution.py:480
  29.6 14.2 %collective-permute-start.1 = (bf16[32,16,8]{2,1,0:T(8,128)(2,1)S(1)}, bf16[32,16,8]{2,1,0:T(8,128)(2,1)S(1)}, u32[]{:S(2)}, u32[]{:S(2)}) collective-permute-start(bf16[32,16,8]{2,1,0:T(8,128)(2,1)S(1)} %get-tuple-element.135), channel_id=1, source_target_pairs={{0,1},{1,2},{2,3},{3,4},{4,5},{5,6},{6,7},{7,8},{8,9},{9,10},{10,1... | collective-permute-start | bytes 24584 | tf_op jit(solution)/shard_map/ppermute | solution.py:481
  32.3 0.7 copy-start.3
  36.2 21.8 %all-to-all-start.1 = ((bf16[8,32,768]{2,1,0:T(8,128)(2,1)}), bf16[8,32,768]{2,1,0:T(8,128)(2,1)S(1)}, u32[]{:S(2)}, u32[]{:S(2)}) async-start(bf16[8,32,768]{2,1,0:T(8,128)(2,1)} %broadcast_in_dim.7), calls=%async_computation.1 | async-start | bytes 786432 | tf_op jit(solution)/shard_map/all_to_all | solution.py:504
  44.0 0.8 copy-start
  44.0 4.7 %copy-start.7 = (bf16[256,32]{0,1:T(8,128)(2,1)S(1)}, bf16[256,32]{0,1:T(8,128)(2,1)}, u32[]{:S(2)}) copy-start(bf16[256,32]{0,1:T(8,128)(2,1)} %param.27) | copy-start | bytes 49156
  44.0 5.5 %copy-start.6 = (bf16[256,32]{0,1:T(8,128)(2,1)S(1)}, bf16[256,32]{0,1:T(8,128)(2,1)}, u32[]{:S(2)}) copy-start(bf16[256,32]{0,1:T(8,128)(2,1)} %param.26) | copy-start | bytes 49156
  44.9 5.4 %collective-permute-start.2 = (bf16[256,640]{1,0:T(8,128)(2,1)S(1)}, bf16[256,640]{1,0:T(8,128)(2,1)S(1)}, u32[]{:S(2)}, u32[]{:S(2)}) collective-permute-start(bf16[256,640]{1,0:T(8,128)(2,1)S(1)} %get-tuple-element.133), channel_id=1, source_target_pairs={{0,32},{32,64},{64,96},{96,128},{128,160},{160,192},{192,224},{1,3... | collective-permute-start | bytes 983048 | tf_op jit(solution)/shard_map/ppermute | solution.py:501
  47.3 5.5 %collective-permute-start.3 = (bf16[256,640]{1,0:T(8,128)(2,1)S(1)}, bf16[256,640]{1,0:T(8,128)(2,1)S(1)}, u32[]{:S(2)}, u32[]{:S(2)}) collective-permute-start(bf16[256,640]{1,0:T(8,128)(2,1)S(1)} %get-tuple-element.132), channel_id=1, source_target_pairs={{32,0},{64,32},{96,64},{128,96},{160,128},{192,160},{224,192},{33,... | collective-permute-start | bytes 983048 | tf_op jit(solution)/shard_map/ppermute | solution.py:502
  50.2 7.8 %copy-start.4 = (bf16[256,640]{1,0:T(8,128)(2,1)}, bf16[256,640]{1,0:T(8,128)(2,1)S(1)}, u32[]{:S(2)}) copy-start(bf16[256,640]{1,0:T(8,128)(2,1)S(1)} %collective-permute-done.2.cot_up_ref) | copy-start | bytes 983044
  52.8 5.2 %copy-start.5 = (bf16[256,640]{1,0:T(8,128)(2,1)}, bf16[256,640]{1,0:T(8,128)(2,1)S(1)}, u32[]{:S(2)}) copy-start(bf16[256,640]{1,0:T(8,128)(2,1)S(1)} %collective-permute-done.3.cot_down_ref) | copy-start | bytes 983044
  58.0 0.8 copy-start.1
  130.8 21.5 %all-to-all-start.4 = ((f32[256,1,256]{2,1,0:T(1,128)}), f32[256,1,256]{2,1,0:T(1,128)S(1)}, u32[]{:S(2)}, u32[]{:S(2)}) async-start(f32[256,1,256]{2,1,0:T(1,128)} %shard_map.156), calls=%async_computation.4 | async-start | bytes 524288 | tf_op jit(solution)/shard_map/all_to_all | solution.py:544

commit v2 on v1

v2 whole, which is shorter than its diff:
```python
import functools

import jax
import jax.numpy as jnp
from jax import lax
from jax.experimental import pallas as pl
from jax.experimental.pallas import tpu as pltpu
from jax.sharding import PartitionSpec as P

tanh_scale = 0.7978845608028654
cubic_term = 0.044715
keep_boost = 4.0 / 3.0
slope_cubic = 3.0 * tanh_scale * cubic_term

K = 32
ROWS = 16
COLS = 512
WIDE = 640
TAPS = 9
BLK = 8 * K
HIGH = lax.Precision.HIGHEST
f32 = jnp.float32
bf16 = jnp.bfloat16
VMEM_LIMIT = 56 * 1024 * 1024


def dot(a, b, precision=None):
    return lax.dot_general(
        a, b, (((1,), (0,)), ((), ())), precision=precision, preferred_element_type=f32
    )


def dot_nt(a, b, precision=None):
    return lax.dot_general(
        a, b, (((1,), (1,)), ((), ())), precision=precision, preferred_element_type=f32
    )


def dot_tn(a, b, precision=None):
    return lax.dot_general(
        a, b, (((0,), (0,)), ((), ())), precision=precision, preferred_element_type=f32
    )


def iota(shape, dim):
    return lax.broadcasted_iota(jnp.int32, shape, dim)


def ahead(x, s):
    lane = iota((x.shape[0], 128), 1)
    turned = [pltpu.roll(x[:, i : i + 128], 128 - s, 1) for i in range(0, x.shape[1], 128)]
    nxt = turned[1:] + turned[:1]
    return jnp.concatenate(
        [jnp.where(lane >= 128 - s, n, t) for t, n in zip(turned, nxt)], axis=1
    )


def behind(x, s):
    lane = iota((x.shape[0], 128), 1)
    turned = [pltpu.roll(x[:, i : i + 128], s, 1) for i in range(0, x.shape[1], 128)]
    prv = turned[-1:] + turned[:-1]
    return jnp.concatenate([jnp.where(lane < s, p, t) for t, p in zip(turned, prv)], axis=1)


def mixed(base, factor):
    h = base * 668265261
    h = h ^ lax.shift_right_logical(h, 15)
    h = h * 374761393
    h = h ^ lax.shift_right_logical(h, 13)
    return jnp.where((h & 3) != 0, factor, 0.0)


def wrapped(number):
    return (number + 2**31) % 2**32 - 2**31


def gelu_parts(v):
    v2 = v * v
    t = jnp.tanh(v * (tanh_scale + (tanh_scale * cubic_term) * v2))
    p = 0.5 + 0.5 * t
    value = v * p
    slope = p + value * (1.0 - t) * (tanh_scale + slope_cubic * v2)
    return value, slope


def first_kernel(seed_ref, mask_ref, cols_ref, band_ref, out_ref):
    out_ref[0:32, :] = cols_ref[...]
    lane = iota((8, 128), 1)
    seed = seed_ref[0, 0]
    bytes_of = [seed >> 16 & 255, seed >> 8 & 255, seed & 255, mask_ref[0, 0]]
    numbers = jnp.zeros((8, 128), jnp.int32)
    for i, value in enumerate(bytes_of):
        numbers = jnp.where(lane == i, value, numbers)
    band = jnp.concatenate([band_ref[...].astype(f32), jnp.zeros((8, 112), f32)], axis=1)
    out_ref[32:48, 0:128] = jnp.concatenate([band, numbers.astype(f32)], axis=0).astype(bf16)
    out_ref[32:48, 128:] = jnp.zeros((16, COLS - 128), bf16)


def pack_kernel(
    own_ref, one_ref, two_ref, three_ref, other_ref, cot_ref, up_ref, down_ref,
    feats_ref, west_ref, east_ref, bands_ref,
):
    even = lax.rem(lax.axis_index("row"), 2) == 0
    lane = iota((32, 128), 1)
    mine = [own_ref, one_ref, two_ref, three_ref]
    west = jnp.zeros((32, 128), f32)
    east = jnp.zeros((32, 128), f32)
    bands = jnp.zeros((8, 128), f32)
    seeds = jnp.zeros((8, 128), f32)
    for t in range(8):
        a = mine[t // 2]
        b = other_ref.at[t // 2]
        if t % 2 == 0:
            pick = lambda rows, cols: jnp.where(even, a[rows, cols], b[rows, cols])
        else:
            pick = lambda rows, cols: jnp.where(even, b[rows, cols], a[rows, cols])
        feats_ref[t] = pick(slice(0, 32), slice(0, COLS))
        here = jnp.logical_and(lane >= 16 * t, lane < 16 * t + 16)
        first = pick(slice(0, 32), slice(0, 128)).astype(f32)
        west = jnp.where(here, pltpu.roll(first, 16 * t, 1) if t else first, west)
        last = pick(slice(0, 32), slice(COLS - 128, COLS)).astype(f32)
        turn = (16 * t + 16) % 128
        east = jnp.where(here, pltpu.roll(last, turn, 1) if turn else last, east)
        extra = pick(slice(32, 48), slice(0, 128)).astype(f32)
        extra = pltpu.roll(extra, 16 * t, 1) if t else extra
        bands = jnp.where(here[:8], extra[0:8], bands)
        seeds = jnp.where(here[:8], extra[8:16], seeds)
    blank = jnp.zeros((8, 128), f32)
    tail = jnp.concatenate([seeds, blank], axis=0).astype(bf16)
    for ref, value in ((west_ref, west), (east_ref, east)):
        ref[0:32, :] = value.astype(bf16)
        ref[96:112, :] = tail
    lane = iota((64, 128), 1)
    for ref, cols, shift in ((west_ref, slice(0, 128), 0), (east_ref, slice(COLS - 128, COLS), 8)):
        total = jnp.zeros((64, 128), f32)
        for g in range(16):
            parts = []
            for ch in (2 * g, 2 * g + 1):
                parts.append(up_ref[ch, :, cols].astype(f32))
                parts.append(cot_ref[ch, :, cols].astype(f32))
                parts.append(down_ref[ch, :, cols].astype(f32))
            whole = jnp.concatenate(parts, axis=0)
            turn = (8 * g + shift) % 128
            whole = pltpu.roll(whole, turn, 1) if turn else whole
            total = jnp.where(jnp.logical_and(lane >= 8 * g, lane < 8 * g + 8), whole, total)
        ref[32:96, :] = total.astype(bf16)
    chunk = jnp.concatenate([bands, blank], axis=0).astype(bf16)
    bands_ref[...] = jnp.broadcast_to(chunk[None], (32, 16, 128))


def main_kernel(
    place,
    feats_ref,
    bands_ref,
    own_ref,
    right_ref,
    left_ref,
    wr_ref,
    wc_ref,
    w1_ref,
    w2_ref,
    cot_ref,
    cot_up_ref,
    cot_down_ref,
    out_ref,
    send_ref,
    t1,
    t2,
    t2m,
    pv,
    hv,
    gv,
    g1,
    d1,
    acc,
    first_out,
    row_all,
    row3,
    qv,
    keep_rows,
    seed_rows,
    base_ref,
    keep_ref,
    cot_halo,
    every,
):
    s1 = place[0]
    s2 = place[1]
    r = lax.axis_index("row")
    c = lax.axis_index("col")
    turn = r // 2

    spread = (iota((K, BLK), 1) // 8 == iota((K, BLK), 0)).astype(f32).astype(bf16)
    sub = iota((8, BLK), 0)
    far = iota((8, BLK), 1) % 8 - sub

    def hits(s, half):
        return [far + 8 * half == 4 + (a - 1) * s for a in range(3)]

    def build(target, weight, s, mirrored):
        masks = [hits(s, half) for half in range(2)]
        for b in range(3):
            grown = []
            for a in range(3):
                if mirrored:
                    grown.append(dot_tn(weight[(2 - a) * 3 + (2 - b)], spread))
                else:
                    grown.append(dot(weight[a * 3 + b], spread))
            for half in range(2):
                m = masks[half]
                whole = jnp.zeros((K, 8, BLK), f32)
                for a in range(3):
                    whole = jnp.where(
                        jnp.broadcast_to(m[a][None], (K, 8, BLK)),
                        jnp.broadcast_to(grown[a][:, None, :], (K, 8, BLK)),
                        whole,
                    )
                at = (half * 3 + b) * BLK
                target[:, at : at + BLK] = whole.reshape(BLK, BLK).astype(bf16)

    build(t1, w1_ref, s1, False)
    build(t2, w2_ref, s2, False)
    build(t2m, w2_ref, s2, True)

    lane = iota((K, 128), 1)
    right = right_ref[0:32, :].astype(f32)
    left = left_ref[0:32, :].astype(f32)
    for t in range(8):
        r_turn = (128 - 16 * t) % 128
        l_turn = (112 - 16 * t) % 128
        halo = jnp.where(
            lane < 64,
            pltpu.roll(right, r_turn, 1) if r_turn else right,
            pltpu.roll(left, l_turn, 1) if l_turn else left,
        ).astype(bf16)
        every[32 * t : 32 * t + 32, 0:COLS] = feats_ref[t]
        every[32 * t : 32 * t + 32, COLS:] = halo
    weight = pltpu.roll(wc_ref[...].astype(f32), lax.rem(256 - 64 * turn, 256), 1).astype(bf16)
    q = dot(weight, every[...])
    qv[...] = q

    bands = bands_ref[...].astype(f32)[:, 0:8, :].reshape(256, 128).astype(bf16)
    row_t = dot(wr_ref[...], bands)
    row_all[...] = row_t.T
    core = lax.rem(r, 2)
    lane128 = iota((1, 128), 1)
    row_t = pltpu.roll(row_t, lax.rem(128 - 16 * core, 128), 1)
    row_t = jnp.where(lane128 < 16, row_t, 0.0)

    lane = iota((1, WIDE), 1)
    for step in range(3):
        slot = lax.rem(core + step + 7, 8)
        row3[16 * step : 16 * step + 16, :] = row_all[
            pl.ds(pl.multiple_of(16 * slot, 16), 16), :
        ]
        sides = []
        for ref in (own_ref, right_ref, left_ref):
            piece = ref[96:112, :].astype(f32)[0:1]
            piece = pltpu.roll(piece, lax.rem(128 - 16 * slot, 128), 1)
            number = piece[:, 0:1] * 65536.0 + piece[:, 1:2] * 256.0 + piece[:, 2:3]
            sides.append((number, piece[:, 3:4]))
        row_ok = jnp.logical_and(r + step >= 1, r + step <= 8).astype(f32)
        right_ok = row_ok * (c < 31).astype(f32)
        left_ok = row_ok * (c > 0).astype(f32)
        keep = jnp.where(
            lane < COLS,
            sides[0][1] * row_ok,
            jnp.where(lane < 576, sides[1][1] * right_ok, sides[2][1] * left_ok),
        )
        seed = jnp.where(
            lane < COLS, sides[0][0], jnp.where(lane < 576, sides[1][0], sides[2][0])
        )
        seed_rows[step] = seed.astype(jnp.int32)
        keep_rows[step] = keep

    lane64 = iota((64, 128), 1)
    right = right_ref[32:96, :].astype(f32)
    left = left_ref[32:96, :].astype(f32)
    for g in range(16):
        r_turn = (128 - 8 * g) % 128
        l_turn = 120 - 8 * g
        cot_halo[64 * g : 64 * g + 64, :] = jnp.where(
            lane64 < 64,
            pltpu.roll(right, r_turn, 1) if r_turn else right,
            pltpu.roll(left, l_turn, 1) if l_turn else left,
        )

    column = iota((8, WIDE), 1)
    column = c * COLS + jnp.where(column < 576, column, column - WIDE)

    def prepare(first_row, layer):
        local = first_row + iota((8, WIDE), 0)
        seed = jnp.where(
            local < 0, seed_rows[0], jnp.where(local < ROWS, seed_rows[1], seed_rows[2])
        )
        keep = jnp.where(
            local < 0, keep_rows[0], jnp.where(local < ROWS, keep_rows[1], keep_rows[2])
        )
        base = seed * 1000003 + layer * 7919
        base = base ^ ((r * ROWS + local) * 19349663)
        base_ref[...] = base ^ (column * 83492791)
        keep_ref[...] = keep * keep_boost

    def factor_of(p):
        keep = keep_ref[...]
        base = base_ref[...]
        parts = [mixed(base ^ wrapped(ch * 73856093), keep) for ch in (2 * p, 2 * p + 1)]
        return jnp.concatenate(parts, axis=0)

    def store_shifted(target, block, p, values, s):
        values = values.astype(bf16)
        for b, moved in enumerate((behind(values, s), values, ahead(values, s))):
            at = pl.multiple_of(block * 3 * BLK + b * BLK + 16 * p, 16)
            target[pl.ds(at, 16), :] = moved

    def pair_block(k, carry):
        rows = row3[pl.ds(pl.multiple_of(8 * k, 8), 8), :]
        keep = keep_rows[k // 2]
        for p in range(K // 2):
            parts = []
            for ch in (2 * p, 2 * p + 1):
                parts.append(keep * (rows[:, ch : ch + 1] + qv[ch : ch + 1, :]))
            store_shifted(pv, k, p, jnp.concatenate(parts, axis=0), s1)
        return carry

    lax.fori_loop(0, 6, pair_block, 0)

    def convolve(k, weight, values, to):
        acc[to] = dot(weight[...], values[k * 3 * BLK : (k + 2) * 3 * BLK, :])

    def hidden_block(k, at_acc):
        prepare(8 * k - 12, 1)
        for p in range(K // 2):
            at = 16 * p
            value, slope = gelu_parts(acc[at_acc, at : at + 16, :])
            factor = factor_of(p)
            store_shifted(hv, k, p, factor * value, s2)
            if 1 <= k <= 3:
                d1[(k - 1) * BLK + at : (k - 1) * BLK + at + 16, :] = factor * slope

    def grad_block(k, at_acc):
        prepare(8 * k - 8, 2)
        for p in range(K // 2):
            at = 16 * p
            value, slope = gelu_parts(acc[at_acc, at : at + 16, :])
            factor = factor_of(p)
            if k == 0:
                cot = cot_up_ref[at : at + 16, :].astype(f32)
            elif k == 3:
                cot = cot_down_ref[at : at + 16, :].astype(f32)
            else:
                parts = []
                for ch in (2 * p, 2 * p + 1):
                    parts.append(cot_ref[ch].astype(f32)[8 * (k - 1) : 8 * k])
                cot = jnp.concatenate(parts, axis=0)
            halo = []
            for i in range(2):
                first = 64 * p + 32 * i + 8 * k
                halo.append(cot_halo[first : first + 8, :])
            cot = jnp.concatenate([cot, jnp.concatenate(halo, axis=0)], axis=1)
            store_shifted(gv, k, p, cot * factor * slope, s2)
            if k == 1:
                first_out[at : at + 16, :] = (factor * value)[:, :COLS]
            if k == 2:
                upper = first_out[at : at + 16, :]
                lower = (factor * value)[:, :COLS]
                for i in range(2):
                    both = jnp.concatenate(
                        [upper[8 * i : 8 * i + 8], lower[8 * i : 8 * i + 8]], axis=0
                    )
                    out_ref[2 * p + i] = both.astype(bf16)

    def back_block(k, at_acc):
        g1[k * BLK : (k + 1) * BLK, :] = (
            acc[at_acc] * d1[k * BLK : (k + 1) * BLK, :]
        ).astype(bf16)

    jobs = [(convolve, k, t1, pv, functools.partial(hidden_block, k)) for k in range(5)]
    jobs += [(convolve, k, t2, hv, functools.partial(grad_block, k)) for k in range(4)]
    jobs += [(convolve, k, t2m, gv, functools.partial(back_block, k)) for k in range(3)]
    for i, (start, k, weight, values, _) in enumerate(jobs):
        start(k, weight, values, i % 2)
        if i:
            jobs[i - 1][4]((i - 1) % 2)
    jobs[-1][4]((len(jobs) - 1) % 2)

    crossed = []
    for half in range(2):
        total = jnp.zeros((BLK, 3 * BLK), f32)
        for k in (1, 2):
            start = k * 3 * BLK + BLK
            grads = gv[start : start + BLK, 0:COLS]
            start = (k + half) * 3 * BLK
            total = total + dot_nt(grads, hv[start : start + 3 * BLK, 0:COLS])
        crossed.append(total)
    gather8 = (iota((3 * BLK, 96), 0) // 8 == iota((3 * BLK, 96), 1)).astype(f32)
    masks = [hits(s2, half) for half in range(2)]
    second_rows = []
    for a in range(3):
        found = jnp.zeros((K, 8, 3 * BLK), f32)
        for half in range(2):
            m = jnp.concatenate([masks[half][a].astype(f32)] * 3, axis=1)
            found = found + crossed[half].reshape(K, 8, 3 * BLK) * m[None]
        second_rows.append(dot(jnp.sum(found, axis=1), gather8, HIGH))
    second_total = jnp.concatenate(second_rows, axis=0)

    place_j = iota((WIDE, 384), 0)
    place_j = jnp.where(place_j < 576, place_j, place_j - WIDE)
    moved_j = place_j + (iota((WIDE, 384), 1) // 128 - 1) * s1
    window = jnp.logical_and(moved_j >= 0, moved_j < COLS).astype(f32).astype(bf16)
    by_row = dot(g1[...], window)
    which = iota((3 * BLK, 384), 0)
    which = which // BLK * 8 + which % 8
    by_row = jnp.where(iota((3 * BLK, 384), 1) % 128 == which, by_row, 0.0)
    same = (iota((K, 3 * BLK), 1) % BLK // 8 == iota((K, 3 * BLK), 0)).astype(f32)
    by_row = dot(same, by_row, HIGH)
    across = iota((96, 3 * BLK), 1)
    down = iota((96, 3 * BLK), 0)
    moved_i = across // BLK * 8 + across % 8 - 4 + (down // K - 1) * s1
    inside = jnp.logical_and(moved_i >= 0, moved_i < ROWS)
    inside = jnp.logical_and(inside, across % BLK // 8 == down % K)
    by_col = dot(inside.astype(f32).astype(bf16), g1[...])
    by_col = [ahead(by_col, s1), by_col, behind(by_col, s1)]

    keep_own = keep_rows[1][:, 0:1]

    col_sum = jnp.zeros((K, WIDE), f32)
    row_sum = jnp.zeros((K, 128), f32)
    first_cols = []
    row_taps = []
    for a in range(3):
        seen = jnp.zeros((K, 128), f32)
        for b in range(3):
            seen = seen + dot_tn(
                w1_ref[a * 3 + b].astype(f32), by_row[:, 128 * b : 128 * b + 128], HIGH
            )
        row_sum = row_sum + pltpu.roll(seen, 128 - (4 - (a - 1) * s1), 1)
    for b in range(3):
        flat = jnp.concatenate([w1_ref[a * 3 + b] for a in range(3)], axis=0).astype(f32)
        col_sum = col_sum + dot_tn(flat, by_col[b], HIGH)
        from_cols = dot_nt(by_col[b][:, :COLS], q[:, :COLS], HIGH)
        from_rows = []
        for a in range(3):
            moved = pltpu.roll(by_row[:, 128 * b : 128 * b + 128], 128 - (4 - (a - 1) * s1), 1)
            from_rows.append(dot_nt(moved, row_t, HIGH))
        first_cols.append(from_cols + jnp.concatenate(from_rows, axis=0))
    first_total = jnp.concatenate(first_cols, axis=1) * keep_own
    row_sum = jnp.where(lane128 < 16, row_sum * keep_own, 0.0)
    row_sum = pltpu.roll(row_sum, 16 * r, 1)

    col_sum = col_sum * keep_own
    for g in range(4):
        send_ref[32 * g : 32 * g + 32, :] = col_sum[:, 128 * g : 128 * g + 128].astype(bf16)
    send_ref[128:224, :] = jnp.concatenate([first_total, second_total[:, 0:32]], axis=1).astype(bf16)
    send_ref[224:272, :] = jnp.concatenate(
        [second_total[0:48, 32:96], second_total[48:96, 32:96]], axis=1
    ).astype(bf16)
    send_ref[272:304, :] = row_sum.astype(bf16)


def four(own_ref, a_ref, b_ref, c_ref):
    pair = own_ref[...].astype(f32) + b_ref[...].astype(f32)
    return pair + (a_ref[...].astype(f32) + c_ref[...].astype(f32))


def middle_kernel(
    own_ref, a_ref, b_ref, c_ref, feats_ref, wc_ref, gcols_ref, send_ref
):
    r = lax.axis_index("row")
    total = four(own_ref, a_ref, b_ref, c_ref)
    weight = pltpu.roll(wc_ref[...].astype(f32), lax.rem(256 - 32 * r, 256), 1)[:, 0:K]
    grad_w = jnp.zeros((K, 256), f32)
    for g in range(4):
        part = total[32 * g : 32 * g + 32, :]
        gcols_ref[:, 128 * g : 128 * g + 128] = dot_tn(weight, part, HIGH).astype(bf16)
        seen = feats_ref[:, :, 128 * g : 128 * g + 128].reshape(256, 128)
        grad_w = grad_w + dot_nt(part, seen.astype(f32), HIGH)
    grad_w = pltpu.roll(grad_w, 64 * (r // 2), 1)
    send_ref[0:176, :] = total[128:304].astype(bf16)
    send_ref[176:208, :] = grad_w[:, 0:128].astype(bf16)
    send_ref[208:240, :] = grad_w[:, 128:256].astype(bf16)


def last_kernel(
    own_ref, a_ref, bands_ref, wr_ref, gband_ref, gwr_ref, gwc_ref, g1_ref, g2_ref
):
    r = lax.axis_index("row")
    c = lax.axis_index("col")
    total = own_ref[...].astype(f32) + a_ref[...].astype(f32)
    rest = jnp.concatenate([total[96:144, 0:64], total[96:144, 64:128]], axis=0)
    for a in range(3):
        for b in range(3):
            g1_ref[a * 3 + b] = total[32 * a : 32 * a + 32, 32 * b : 32 * b + 32]
        g2_ref[a * 3] = total[32 * a : 32 * a + 32, 96:128]
        g2_ref[a * 3 + 1] = rest[32 * a : 32 * a + 32, 0:32]
        g2_ref[a * 3 + 2] = rest[32 * a : 32 * a + 32, 32:64]
    rows = total[144:176, :]
    gwc_ref[:, 0:128] = total[176:208]
    gwc_ref[:, 128:256] = total[208:240]
    bands = bands_ref[...].astype(f32)[:, 0:8, :].reshape(256, 128)
    turned = pltpu.roll(rows, lax.rem(128 - 32 * (r // 2), 128), 1)
    gwr_ref[...] = dot_nt(turned, bands, HIGH)
    mine = pltpu.roll(wr_ref[...].astype(f32), lax.rem(256 - 8 * c, 256), 1)[:, 0:128]
    mine = dot_tn(mine, pltpu.roll(rows, lax.rem(128 - 16 * r, 128), 1), HIGH)
    gband_ref[...] = mine[0:8, 0:16].astype(bf16)


def call(kernel, shapes, args, scratch=(), scalars=0):
    whole = pl.BlockSpec(memory_space=pltpu.VMEM)
    return pl.pallas_call(
        kernel,
        out_shape=shapes,
        in_specs=[pl.BlockSpec(memory_space=pltpu.SMEM)] * scalars
        + [whole] * (len(args) - scalars),
        out_specs=jax.tree.map(lambda _: whole, shapes),
        scratch_shapes=list(scratch),
        compiler_params=pltpu.CompilerParams(vmem_limit_bytes=VMEM_LIMIT),
    )(*args)


def shape(dims, kind):
    return jax.ShapeDtypeStruct(dims, kind)


def per_device(
    band_emb,
    col_emb,
    w_row,
    w_col,
    first_kernel_weight,
    second_kernel_weight,
    cotangent,
    drop_seeds,
    tile_mask,
    dilations,
):
    rows = lax.axis_size("row")
    cols = lax.axis_size("col")

    south = [(i, (i + 1) % rows) for i in range(rows)]
    north = [(j, i) for i, j in south]
    cot_up = lax.ppermute(cotangent[:, 8:, :], "row", south)
    cot_down = lax.ppermute(cotangent[:, :8, :], "row", north)

    cols_t = col_emb.T
    own = call(
        first_kernel,
        shape((48, COLS), bf16),
        (drop_seeds, tile_mask, cols_t, band_emb.T),
        scalars=2,
    )
    beyond = [
        lax.ppermute(own, "row", [((i + 2 * s) % rows, i) for i in range(rows)]) for s in (1, 2, 3)
    ]
    flip = [(i, i ^ 1) for i in range(rows)]
    other = lax.ppermute(jnp.stack([own] + beyond), "row", flip)

    feats, west_edge, east_edge, bands = call(
        pack_kernel,
        (
            shape((8, K, COLS), bf16),
            shape((112, 128), bf16),
            shape((112, 128), bf16),
            shape((32, 16, 128), bf16),
        ),
        (own, *beyond, other, cotangent, cot_up, cot_down),
    )
    east = [(i, (i + 1) % cols) for i in range(cols)]
    west = [(j, i) for i, j in east]
    right = lax.ppermute(west_edge, "col", west)
    left = lax.ppermute(east_edge, "col", east)
    bands = lax.all_to_all(bands, "col", 0, 0)

    w1 = jnp.transpose(first_kernel_weight, (2, 3, 0, 1)).reshape(TAPS, K, K)
    w2 = jnp.transpose(second_kernel_weight, (2, 3, 0, 1)).reshape(TAPS, K, K)
    out_map, sums = call(
        main_kernel,
        (shape((K, ROWS, COLS), bf16), shape((304, 128), bf16)),
        (
            dilations,
            feats,
            bands,
            west_edge,
            right,
            left,
            w_row.T,
            w_col.T,
            w1,
            w2,
            cotangent,
            cot_up.reshape(BLK, COLS),
            cot_down.reshape(BLK, COLS),
        ),
        scratch=(
            pltpu.VMEM((BLK, 6 * BLK), bf16),
            pltpu.VMEM((BLK, 6 * BLK), bf16),
            pltpu.VMEM((BLK, 6 * BLK), bf16),
            pltpu.VMEM((18 * BLK, WIDE), bf16),
            pltpu.VMEM((15 * BLK, WIDE), bf16),
            pltpu.VMEM((12 * BLK, WIDE), bf16),
            pltpu.VMEM((3 * BLK, WIDE), bf16),
            pltpu.VMEM((3 * BLK, WIDE), f32),
            pltpu.VMEM((2, BLK, WIDE), f32),
            pltpu.VMEM((BLK, COLS), f32),
            pltpu.VMEM((128, K), f32),
            pltpu.VMEM((48, K), f32),
            pltpu.VMEM((K, WIDE), f32),
            pltpu.VMEM((3, 1, WIDE), f32),
            pltpu.VMEM((3, 1, WIDE), jnp.int32),
            pltpu.VMEM((8, WIDE), jnp.int32),
            pltpu.VMEM((8, WIDE), f32),
            pltpu.VMEM((32 * K, 128), f32),
            pltpu.VMEM((8 * K, WIDE), bf16),
        ),
        scalars=1,
    )

    def added(x, y):
        return (x.astype(f32) + y.astype(f32)).astype(bf16)

    def quarters(x, axis, count, place):
        step, size = place
        turned = lambda i, s: i - i // step % size * step + (i // step + s) % size * step
        return [
            lax.ppermute(x, axis, [(i, turned(i, s)) for i in range(count)]) for s in (1, 2, 3)
        ]

    sums = added(sums, lax.ppermute(sums, "row", flip))
    grad_cols, terms = call(
        middle_kernel,
        (shape((K, COLS), bf16), shape((240, 128), bf16)),
        (sums, *quarters(sums, "row", rows, (2, 4)), feats, w_col.T),
    )
    for place in ((1, 4), (4, 4)):
        one, two, three = quarters(terms, "col", cols, place)
        pair = terms.astype(f32) + two.astype(f32)
        terms = (pair + (one.astype(f32) + three.astype(f32))).astype(bf16)
    grad_band, grad_w_row, grad_w_col, grad_one, grad_two = call(
        last_kernel,
        (
            shape((8, ROWS), bf16),
            shape((K, 256), f32),
            shape((K, 256), f32),
            shape((TAPS, K, K), f32),
            shape((TAPS, K, K), f32),
        ),
        (
            terms,
            lax.ppermute(terms, "col", [(i, (i + 16) % cols) for i in range(cols)]),
            bands,
            w_row.T,
        ),
    )
    unfold = lambda x: jnp.transpose(x.reshape(3, 3, K, K), (2, 3, 0, 1))
    return (
        out_map,
        grad_band.T,
        grad_cols.T,
        grad_w_row.T,
        grad_w_col.T,
        unfold(grad_one),
        unfold(grad_two),
    )


def solution(mesh):
    placed = (
        P("row", "col"),
        P("col", "row"),
        P(),
        P(),
        P(),
        P(),
        P(None, "row", "col"),
        P("row", "col"),
        P("row", "col"),
        P(),
    )
    return jax.shard_map(
        per_device,
        mesh=mesh,
        in_specs=placed,
        out_specs=(P(None, "row", "col"), P("row", "col"), P("col", "row"), P(), P(), P(), P()),
        check_vma=False,
    )
```

time: 160 us -> 117 us (0.73); the launches traced: 157 us -> 116 us
  blocking collectives: 39.3 us -> 0 us
  waiting for transfers between devices: 21.4 us -> 34.5 us
  local copies, waits for them, and re-layouts: 14.9 us -> 4.26 us
  other arithmetic: 9.6 us -> 1.84 us
  starting transfers between devices: 34.3 us -> 41.3 us
  Pallas kernels: 35.2 us -> 32.2 us
    all_to_all x2 -> x0, blocking collectives: 39.3 us -> none  [the longest x1 24.7 us: per_device(): got = lax.all_to_all(sums, 'row', 0, 0)]
    ppermute x4 -> x19, waiting for transfers between devices: 2.58 us -> 34.1 us  [the longest x9 18 us: quarters(): lax.ppermute(x, axis, [(i, turned(i, s)) for i in range(count)])]
    ppermute x4 -> x19, starting transfers between devices: 10.7 us -> 33.6 us  [the longest x9 16.5 us: quarters(): lax.ppermute(x, axis, [(i, turned(i, s)) for i in range(count)])]
    all_to_all x3 -> x1, waiting for transfers between devices: 18.9 us -> 0.46 us  [per_device(): bands = lax.all_to_all(bands, 'col', 0, 0)]
    all_to_all x3 -> x1, starting transfers between devices: 23.6 us -> 7.71 us  [per_device(): bands = lax.all_to_all(bands, 'col', 0, 0)]
    another operation x7 -> x1, other arithmetic: 7.92 us -> 0.03 us  [per_device(): other = lax.ppermute(jnp.stack([own] + beyond), 'row', flip)]
    unnamed x23 -> x36, local copies, waits for them, and re-layouts: 6.58 us -> 3.2 us
    pallas_call x5, Pallas kernels: 35.2 us -> 32.2 us  [call(): pl.pallas_call(kernel, out_shape=shapes, in_specs=[pl.BlockSpec(memory_sp...]
  transfers between devices with their start and end apart: 7 -> 20, of which waited for: 3 -> 16; matrix products, arithmetic and copies ran while one was open for 3% -> 1% of each run, Pallas kernels for 1% -> 0%
where the time goes in v2:
time: 117 us; the launch traced here: 116 us
  starting transfers between devices  41.3 us (35%)
  waiting for transfers between devices  34.5 us (29%)
  Pallas kernels  32.2 us (28%)
  local copies, waits for them, and re-layouts  4.26 us (4%)
  between operations  2.07 us (2%)
  other arithmetic  1.84 us (2%)
    pallas_call x5, Pallas kernels, call(): pl.pallas_call(kernel, out_shape=shapes, in_specs=[pl.BlockSpec(memory_sp...  32.2 us
    ppermute x9, waiting for transfers between devices, quarters(): lax.ppermute(x, axis, [(i, turned(i, s)) for i in range(count)])  18 us
    ppermute x9, starting transfers between devices, quarters(): lax.ppermute(x, axis, [(i, turned(i, s)) for i in range(count)])  16.5 us
    ppermute x3, starting transfers between devices, per_device(): lax.ppermute(own, 'row', [((i + 2 * s) % rows, i) for i in range(rows)])  11.3 us
    all_to_all x1, starting transfers between devices, per_device(): bands = lax.all_to_all(bands, 'col', 0, 0)  7.71 us
    ppermute x1, waiting for transfers between devices, per_device(): cot_up = lax.ppermute(cotangent[:, 8:, :], 'row', south)  3.51 us
    ppermute x1, waiting for transfers between devices, per_device(): lax.ppermute(terms, 'col', [(i, (i + 16) % cols) for i in range(cols)])  3.32 us
    unnamed x36, local copies, waits for them, and re-layouts  3.2 us
  transfers between devices with their start and end apart: 20, of which 16 were waited for; matrix products, arithmetic and copies ran while one was open for 1% of the time, Pallas kernels for 0%

profile of v2, /device:TPU:6, one launch (start us, length us, event | category | flops | bytes accessed | tf_op | source)
XLA Modules:
  0.0 116.2 jit_solution(9740263221119691265)
XLA Ops:
  1.9 1.4 %shard_map.153.own_ref = bf16[48,512]{1,0:T(8,128)(2,1)} custom-call(s32[1,1]{1,0:T(1,128)S(6)} %copy.17.seed_ref, s32[1,1]{1,0:T(1,128)S(6)} %copy.18.mask_ref, bf16[32,512]{1,0:T(8,128)(2,1)} %bitcast.38, bf16[8,16]{1,0:T(8,128)(2,1)} %bitcast.39), custom_call_target="tpu_custom_call" | custom-call | tf_op jit(solution)/shard_map/pallas_call | solution.py:510
  3.3 3.3 %collective-permute-start.2 = (bf16[48,512]{1,0:T(8,128)(2,1)}, bf16[48,512]{1,0:T(8,128)(2,1)S(1)}, u32[]{:S(2)}, u32[]{:S(2)}) collective-permute-start(bf16[48,512]{1,0:T(8,128)(2,1)} %shard_map.153.own_ref), channel_id=1, source_target_pairs={{192,0},{224,32},{0,64},{32,96},{64,128},{96,160},{128,192},{160,2... | collective-permute-start | bytes 147464 | tf_op jit(solution)/shard_map/ppermute | solution.py:553
  6.6 5.4 %collective-permute-start.1 = (bf16[48,512]{1,0:T(8,128)(2,1)}, bf16[48,512]{1,0:T(8,128)(2,1)S(1)}, u32[]{:S(2)}, u32[]{:S(2)}) collective-permute-start(bf16[48,512]{1,0:T(8,128)(2,1)} %shard_map.153.own_ref), channel_id=1, source_target_pairs={{128,0},{160,32},{192,64},{224,96},{0,128},{32,160},{64,192},{96,2... | collective-permute-start | bytes 147464 | tf_op jit(solution)/shard_map/ppermute | solution.py:553
  12.0 2.7 %collective-permute-start = (bf16[48,512]{1,0:T(8,128)(2,1)}, bf16[48,512]{1,0:T(8,128)(2,1)S(1)}, u32[]{:S(2)}, u32[]{:S(2)}) collective-permute-start(bf16[48,512]{1,0:T(8,128)(2,1)} %shard_map.153.own_ref), channel_id=1, source_target_pairs={{64,0},{96,32},{128,64},{160,96},{192,128},{224,160},{0,192},{32,2... | collective-permute-start | bytes 147464 | tf_op jit(solution)/shard_map/ppermute | solution.py:553
  14.6 1.1 fusion
  16.3 1.7 %collective-permute-done.one_ref = bf16[48,512]{1,0:T(8,128)(2,1)S(1)} collective-permute-done((bf16[48,512]{1,0:T(8,128)(2,1)}, bf16[48,512]{1,0:T(8,128)(2,1)S(1)}, u32[]{:S(2)}, u32[]{:S(2)}) %collective-permute-start) | collective-permute-done | bytes 49184 | tf_op jit(solution)/shard_map/ppermute | solution.py:553
  18.6 1.4 %collective-permute-done.3.other_ref = bf16[4,48,512]{2,1,0:T(8,128)(2,1)S(1)} collective-permute-done((bf16[4,48,512]{2,1,0:T(8,128)(2,1)S(1)}, bf16[4,48,512]{2,1,0:T(8,128)(2,1)S(1)}, u32[]{:S(2)}, u32[]{:S(2)}) %collective-permute-start.3) | collective-permute-done | bytes 196640 | tf_op jit(solution)/shard_map/ppermute | solution.py:556
  20.0 2.6 %collective-permute-done.5.down_ref = bf16[32,8,512]{2,1,0:T(8,128)(2,1)S(1)} collective-permute-done((bf16[32,8,512]{2,1,0:T(8,128)(2,1)S(1)}, bf16[32,8,512]{2,1,0:T(8,128)(2,1)S(1)}, u32[]{:S(2)}, u32[]{:S(2)}) %collective-permute-start.5) | collective-permute-done | bytes 262176 | tf_op jit(solution)/shard_map/ppermute | solution.py:543
  22.6 3.5 %collective-permute-done.4.up_ref = bf16[32,8,512]{2,1,0:T(8,128)(2,1)S(1)} collective-permute-done((bf16[32,8,512]{2,1,0:T(8,128)(2,1)S(1)}, bf16[32,8,512]{2,1,0:T(8,128)(2,1)S(1)}, u32[]{:S(2)}, u32[]{:S(2)}) %collective-permute-start.4) | collective-permute-done | bytes 262176 | tf_op jit(solution)/shard_map/ppermute | solution.py:542
  26.9 2.2 %shard_map.154 = (bf16[8,32,512]{2,1,0:T(8,128)(2,1)}, bf16[112,128]{1,0:T(8,128)(2,1)}, bf16[112,128]{1,0:T(8,128)(2,1)}, bf16[32,16,128]{2,1,0:T(8,128)(2,1)}) custom-call(bf16[48,512]{1,0:T(8,128)(2,1)} %shard_map.153.own_ref, bf16[48,512]{1,0:T(8,128)(2,1)} %copy-done.8, bf16[48,512]{1,0:T(8,128)(2,1)} %copy-done.7, bf16[48,512]{1,0:T(8,128)(2,1)} %copy-done.6, ...), custom_call_target="tpu_custom_call" | custom-call | tf_op jit(solution)/shard_map/pallas_call | solution.py:510
  29.1 7.7 %all-to-all-start = ((bf16[32,16,128]{2,1,0:T(8,128)(2,1)}), bf16[32,16,128]{2,1,0:T(8,128)(2,1)S(1)}, u32[]{:S(2)}, u32[]{:S(2)}) async-start(bf16[32,16,128]{2,1,0:T(8,128)(2,1)} %get-tuple-element.21), calls=%async_computation | async-start | bytes 262144 | tf_op jit(solution)/shard_map/all_to_all | solution.py:572
  36.8 1.5 %collective-permute-start.7 = (bf16[112,128]{1,0:T(8,128)(2,1)S(1)}, bf16[112,128]{1,0:T(8,128)(2,1)S(1)}, u32[]{:S(2)}, u32[]{:S(2)}) collective-permute-start(bf16[112,128]{1,0:T(8,128)(2,1)S(1)} %copy-done.17), channel_id=1, source_target_pairs={{0,1},{1,2},{2,3},{3,4},{4,5},{5,6},{6,7},{7,8},{8,9},{9,10},{10,1... | collective-permute-start | bytes 86024 | tf_op jit(solution)/shard_map/ppermute | solution.py:571
  38.4 2.7 %collective-permute-start.6 = (bf16[112,128]{1,0:T(8,128)(2,1)S(1)}, bf16[112,128]{1,0:T(8,128)(2,1)S(1)}, u32[]{:S(2)}, u32[]{:S(2)}) collective-permute-start(bf16[112,128]{1,0:T(8,128)(2,1)S(1)} %copy-done.14), channel_id=1, source_target_pairs={{1,0},{2,1},{3,2},{4,3},{5,4},{6,5},{7,6},{8,7},{9,8},{10,9},{11,1... | collective-permute-start | bytes 86024 | tf_op jit(solution)/shard_map/ppermute | solution.py:570
  41.0 2.1 %collective-permute-done.7.left_ref = bf16[112,128]{1,0:T(8,128)(2,1)S(1)} collective-permute-done((bf16[112,128]{1,0:T(8,128)(2,1)S(1)}, bf16[112,128]{1,0:T(8,128)(2,1)S(1)}, u32[]{:S(2)}, u32[]{:S(2)}) %collective-permute-start.7) | collective-permute-done | bytes 28704 | tf_op jit(solution)/shard_map/ppermute | solution.py:571
  44.3 24.0 %shard_map.155 = (bf16[32,16,512]{2,1,0:T(8,128)(2,1)}, bf16[304,128]{1,0:T(8,128)(2,1)}) custom-call(s32[2]{0:T(128)} %place.1, bf16[8,32,512]{2,1,0:T(8,128)(2,1)} %get-tuple-element.20.feats_ref, bf16[32,16,128]{2,1,0:T(8,128)(2,1)} %copy-done, bf16[112,128]{1,0:T(8,128)(2,1)} %get-tuple-element.22.own_ref, bf16[112,128]{1,0:T(8,128)(2,1)} %copy-done.16, ...), custom_call_target="tpu_custom_call" | custom-call | tf_op jit(solution)/shard_map/pallas_call | solution.py:510
  68.3 1.5 %collective-permute-done.8 = bf16[304,128]{1,0:T(8,128)(2,1)S(1)} collective-permute-done((bf16[304,128]{1,0:T(8,128)(2,1)}, bf16[304,128]{1,0:T(8,128)(2,1)S(1)}, u32[]{:S(2)}, u32[]{:S(2)}) %collective-permute-start.8) | collective-permute-done | bytes 77856 | tf_op jit(solution)/shard_map/ppermute | solution.py:628
  69.8 0.9 add_convert_fusion.own_ref
  71.2 4.2 %collective-permute-start.10 = (bf16[304,128]{1,0:T(8,128)(2,1)S(1)}, bf16[304,128]{1,0:T(8,128)(2,1)S(1)}, u32[]{:S(2)}, u32[]{:S(2)}) collective-permute-start(bf16[304,128]{1,0:T(8,128)(2,1)S(1)} %add_convert_fusion.own_ref), channel_id=1, source_target_pairs={{0,128},{32,160},{64,192},{96,224},{128,0},{160,32},{192,64},{224,... | collective-permute-start | bytes 233480 | tf_op jit(solution)/shard_map/ppermute | solution.py:625
  75.5 1.5 %collective-permute-start.9 = (bf16[304,128]{1,0:T(8,128)(2,1)S(1)}, bf16[304,128]{1,0:T(8,128)(2,1)S(1)}, u32[]{:S(2)}, u32[]{:S(2)}) collective-permute-start(bf16[304,128]{1,0:T(8,128)(2,1)S(1)} %add_convert_fusion.own_ref), channel_id=1, source_target_pairs={{0,64},{32,96},{64,128},{96,160},{128,192},{160,224},{192,0},{224,... | collective-permute-start | bytes 233480 | tf_op jit(solution)/shard_map/ppermute | solution.py:625
  76.9 0.9 collective-permute-done.11.c_ref
  77.9 1.7 %collective-permute-done.10.b_ref = bf16[304,128]{1,0:T(8,128)(2,1)S(1)} collective-permute-done((bf16[304,128]{1,0:T(8,128)(2,1)S(1)}, bf16[304,128]{1,0:T(8,128)(2,1)S(1)}, u32[]{:S(2)}, u32[]{:S(2)}) %collective-permute-start.10) | collective-permute-done | bytes 77856 | tf_op jit(solution)/shard_map/ppermute | solution.py:625
  79.6 4.7 %collective-permute-done.9.a_ref = bf16[304,128]{1,0:T(8,128)(2,1)S(1)} collective-permute-done((bf16[304,128]{1,0:T(8,128)(2,1)S(1)}, bf16[304,128]{1,0:T(8,128)(2,1)S(1)}, u32[]{:S(2)}, u32[]{:S(2)}) %collective-permute-start.9) | collective-permute-done | bytes 77856 | tf_op jit(solution)/shard_map/ppermute | solution.py:625
  84.9 2.6 %shard_map.156 = (bf16[32,512]{1,0:T(8,128)(2,1)}, bf16[240,128]{1,0:T(8,128)(2,1)}) custom-call(bf16[304,128]{1,0:T(8,128)(2,1)} %copy-done.4, bf16[304,128]{1,0:T(8,128)(2,1)} %copy-done.12, bf16[304,128]{1,0:T(8,128)(2,1)} %copy-done.11, bf16[304,128]{1,0:T(8,128)(2,1)} %copy-done.10, bf16[8,32,512]{2,1,0:T(8,128)(2,1)} %get-tuple-element.20.feats_ref, ...), custom_call_target="tpu_custom_call" | custom-call | tf_op jit(solution)/shard_map/pallas_call | solution.py:510
  87.5 5.5 %collective-permute-start.14 = (bf16[240,128]{1,0:T(8,128)(2,1)}, bf16[240,128]{1,0:T(8,128)(2,1)S(1)}, u32[]{:S(2)}, u32[]{:S(2)}) collective-permute-start(bf16[240,128]{1,0:T(8,128)(2,1)} %get-tuple-element.26), channel_id=1, source_target_pairs={{0,3},{1,0},{2,1},{3,2},{4,7},{5,4},{6,5},{7,6},{8,11},{9,8},{10,9... | collective-permute-start | bytes 184328 | tf_op jit(solution)/shard_map/ppermute | solution.py:625
  93.0 1.5 %collective-permute-start.12 = (bf16[240,128]{1,0:T(8,128)(2,1)}, bf16[240,128]{1,0:T(8,128)(2,1)S(1)}, u32[]{:S(2)}, u32[]{:S(2)}) collective-permute-start(bf16[240,128]{1,0:T(8,128)(2,1)} %get-tuple-element.26), channel_id=1, source_target_pairs={{0,2},{1,3},{2,0},{3,1},{4,6},{5,7},{6,4},{7,5},{8,10},{9,11},{10,... | collective-permute-start | bytes 184328 | tf_op jit(solution)/shard_map/ppermute | solution.py:625
  95.1 4.2 %collective-permute-done.13 = bf16[240,128]{1,0:T(8,128)(2,1)S(1)} collective-permute-done((bf16[240,128]{1,0:T(8,128)(2,1)}, bf16[240,128]{1,0:T(8,128)(2,1)S(1)}, u32[]{:S(2)}, u32[]{:S(2)}) %collective-permute-start.13) | collective-permute-done | bytes 61472 | tf_op jit(solution)/shard_map/ppermute | solution.py:625
  100.3 3.2 %collective-permute-start.16 = (bf16[240,128]{1,0:T(8,128)(2,1)S(1)}, bf16[240,128]{1,0:T(8,128)(2,1)S(1)}, u32[]{:S(2)}, u32[]{:S(2)}) collective-permute-start(bf16[240,128]{1,0:T(8,128)(2,1)S(1)} %add_convert_fusion.2), channel_id=1, source_target_pairs={{0,4},{1,5},{2,6},{3,7},{4,8},{5,9},{6,10},{7,11},{8,12},{9,13},{1... | collective-permute-start | bytes 184328 | tf_op jit(solution)/shard_map/ppermute | solution.py:625
  103.5 2.2 %collective-permute-done.17 = bf16[240,128]{1,0:T(8,128)(2,1)S(1)} collective-permute-done((bf16[240,128]{1,0:T(8,128)(2,1)S(1)}, bf16[240,128]{1,0:T(8,128)(2,1)S(1)}, u32[]{:S(2)}, u32[]{:S(2)}) %collective-permute-start.17) | collective-permute-done | bytes 61472 | tf_op jit(solution)/shard_map/ppermute | solution.py:625
  106.0 3.3 %collective-permute-done.15 = bf16[240,128]{1,0:T(8,128)(2,1)S(1)} collective-permute-done((bf16[240,128]{1,0:T(8,128)(2,1)S(1)}, bf16[240,128]{1,0:T(8,128)(2,1)S(1)}, u32[]{:S(2)}, u32[]{:S(2)}) %collective-permute-start.15) | collective-permute-done | bytes 61472 | tf_op jit(solution)/shard_map/ppermute | solution.py:625
  109.3 1.0 collective-permute-start.18
  110.3 3.3 %collective-permute-done.18.a_ref = bf16[240,128]{1,0:T(8,128)(2,1)S(1)} collective-permute-done((bf16[240,128]{1,0:T(8,128)(2,1)S(1)}, bf16[240,128]{1,0:T(8,128)(2,1)S(1)}, u32[]{:S(2)}, u32[]{:S(2)}) %collective-permute-start.18) | collective-permute-done | bytes 61472 | tf_op jit(solution)/shard_map/ppermute | solution.py:649
  114.2 2.0 %shard_map.157 = (bf16[8,16]{1,0:T(8,128)(2,1)}, f32[32,256]{1,0:T(8,128)}, f32[32,256]{1,0:T(8,128)}, f32[9,32,32]{2,1,0:T(8,128)}, f32[9,32,32]{2,1,0:T(8,128)}) custom-call(bf16[240,128]{1,0:T(8,128)(2,1)} %copy-done.5, bf16[240,128]{1,0:T(8,128)(2,1)} %copy-done.13, bf16[32,16,128]{2,1,0:T(8,128)(2,1)} %copy-done, bf16[32,256]{1,0:T(8,128)(2,1)} %bitcast.37), custom_call_target="tpu_custom_call" | custom-call | tf_op jit(solution)/shard_map/pallas_call | solution.py:510
  (54 shorter events, 6.8 us)
Async XLA Ops:
  3.3 14.7 %copy-start.3 = (bf16[48,512]{1,0:T(8,128)(2,1)S(1)}, bf16[48,512]{1,0:T(8,128)(2,1)}, u32[]{:S(2)}) copy-start(bf16[48,512]{1,0:T(8,128)(2,1)} %shard_map.153.own_ref) | copy-start | bytes 147460
  3.3 13.0 %collective-permute-start.2 = (bf16[48,512]{1,0:T(8,128)(2,1)}, bf16[48,512]{1,0:T(8,128)(2,1)S(1)}, u32[]{:S(2)}, u32[]{:S(2)}) collective-permute-start(bf16[48,512]{1,0:T(8,128)(2,1)} %shard_map.153.own_ref), channel_id=1, source_target_pairs={{192,0},{224,32},{0,64},{32,96},{64,128},{96,160},{128,192},{160,2... | collective-permute-start | bytes 147464 | tf_op jit(solution)/shard_map/ppermute | solution.py:553
  6.6 9.7 %collective-permute-start.1 = (bf16[48,512]{1,0:T(8,128)(2,1)}, bf16[48,512]{1,0:T(8,128)(2,1)S(1)}, u32[]{:S(2)}, u32[]{:S(2)}) collective-permute-start(bf16[48,512]{1,0:T(8,128)(2,1)} %shard_map.153.own_ref), channel_id=1, source_target_pairs={{128,0},{160,32},{192,64},{224,96},{0,128},{32,160},{64,192},{96,2... | collective-permute-start | bytes 147464 | tf_op jit(solution)/shard_map/ppermute | solution.py:553
  12.0 6.0 %collective-permute-start = (bf16[48,512]{1,0:T(8,128)(2,1)}, bf16[48,512]{1,0:T(8,128)(2,1)S(1)}, u32[]{:S(2)}, u32[]{:S(2)}) collective-permute-start(bf16[48,512]{1,0:T(8,128)(2,1)} %shard_map.153.own_ref), channel_id=1, source_target_pairs={{64,0},{96,32},{128,64},{160,96},{192,128},{224,160},{0,192},{32,2... | collective-permute-start | bytes 147464 | tf_op jit(solution)/shard_map/ppermute | solution.py:553
  15.7 6.9 %collective-permute-start.5 = (bf16[32,8,512]{2,1,0:T(8,128)(2,1)S(1)}, bf16[32,8,512]{2,1,0:T(8,128)(2,1)S(1)}, u32[]{:S(2)}, u32[]{:S(2)}) collective-permute-start(bf16[32,8,512]{2,1,0:T(8,128)(2,1)S(1)} %get-tuple-element.33), channel_id=1, source_target_pairs={{32,0},{64,32},{96,64},{128,96},{160,128},{192,160},{224,192},{0,2... | collective-permute-start | bytes 786440 | tf_op jit(solution)/shard_map/ppermute | solution.py:543
  15.8 10.3 %collective-permute-start.4 = (bf16[32,8,512]{2,1,0:T(8,128)(2,1)S(1)}, bf16[32,8,512]{2,1,0:T(8,128)(2,1)S(1)}, u32[]{:S(2)}, u32[]{:S(2)}) collective-permute-start(bf16[32,8,512]{2,1,0:T(8,128)(2,1)S(1)} %get-tuple-element.34), channel_id=1, source_target_pairs={{0,32},{32,64},{64,96},{96,128},{128,160},{160,192},{192,224},{224... | collective-permute-start | bytes 786440 | tf_op jit(solution)/shard_map/ppermute | solution.py:542
  16.3 1.7 %copy-start.6 = (bf16[48,512]{1,0:T(8,128)(2,1)}, bf16[48,512]{1,0:T(8,128)(2,1)S(1)}, u32[]{:S(2)}) copy-start(bf16[48,512]{1,0:T(8,128)(2,1)S(1)} %collective-permute-done.2.three_ref) | copy-start | bytes 147460
  16.3 1.7 %copy-start.7 = (bf16[48,512]{1,0:T(8,128)(2,1)}, bf16[48,512]{1,0:T(8,128)(2,1)S(1)}, u32[]{:S(2)}) copy-start(bf16[48,512]{1,0:T(8,128)(2,1)S(1)} %collective-permute-done.1.two_ref) | copy-start | bytes 147460
  18.6 1.4 %collective-permute-start.3 = (bf16[4,48,512]{2,1,0:T(8,128)(2,1)S(1)}, bf16[4,48,512]{2,1,0:T(8,128)(2,1)S(1)}, u32[]{:S(2)}, u32[]{:S(2)}) collective-permute-start(bf16[4,48,512]{2,1,0:T(8,128)(2,1)S(1)} %pad_maximum_fusion), channel_id=1, source_target_pairs={{0,32},{32,0},{64,96},{96,64},{128,160},{160,128},{192,224},{224,1... | collective-permute-start | bytes 589832 | tf_op jit(solution)/shard_map/ppermute | solution.py:556
  20.0 6.1 %copy-start.9 = (bf16[4,48,512]{2,1,0:T(8,128)(2,1)}, bf16[4,48,512]{2,1,0:T(8,128)(2,1)S(1)}, u32[]{:S(2)}) copy-start(bf16[4,48,512]{2,1,0:T(8,128)(2,1)S(1)} %collective-permute-done.3.other_ref) | copy-start | bytes 589828
  22.6 3.5 %copy-start.1 = (bf16[32,8,512]{2,1,0:T(8,128)(2,1)}, bf16[32,8,512]{2,1,0:T(8,128)(2,1)S(1)}, u32[]{:S(2)}) copy-start(bf16[32,8,512]{2,1,0:T(8,128)(2,1)S(1)} %collective-permute-done.5.down_ref) | copy-start | bytes 786436
  26.2 0.7 copy-start.2
  29.1 7.7 %copy-start.17 = (bf16[112,128]{1,0:T(8,128)(2,1)S(1)}, bf16[112,128]{1,0:T(8,128)(2,1)}, u32[]{:S(2)}) copy-start(bf16[112,128]{1,0:T(8,128)(2,1)} %get-tuple-element.23) | copy-start | bytes 86020
  29.1 9.3 %copy-start.14 = (bf16[112,128]{1,0:T(8,128)(2,1)S(1)}, bf16[112,128]{1,0:T(8,128)(2,1)}, u32[]{:S(2)}) copy-start(bf16[112,128]{1,0:T(8,128)(2,1)} %get-tuple-element.22.own_ref) | copy-start | bytes 86020
  29.1 14.5 %all-to-all-start = ((bf16[32,16,128]{2,1,0:T(8,128)(2,1)}), bf16[32,16,128]{2,1,0:T(8,128)(2,1)S(1)}, u32[]{:S(2)}, u32[]{:S(2)}) async-start(bf16[32,16,128]{2,1,0:T(8,128)(2,1)} %get-tuple-element.21), calls=%async_computation | async-start | bytes 262144 | tf_op jit(solution)/shard_map/all_to_all | solution.py:572
  36.8 6.3 %collective-permute-start.7 = (bf16[112,128]{1,0:T(8,128)(2,1)S(1)}, bf16[112,128]{1,0:T(8,128)(2,1)S(1)}, u32[]{:S(2)}, u32[]{:S(2)}) collective-permute-start(bf16[112,128]{1,0:T(8,128)(2,1)S(1)} %copy-done.17), channel_id=1, source_target_pairs={{0,1},{1,2},{2,3},{3,4},{4,5},{5,6},{6,7},{7,8},{8,9},{9,10},{10,1... | collective-permute-start | bytes 86024 | tf_op jit(solution)/shard_map/ppermute | solution.py:571
  38.4 4.8 %collective-permute-start.6 = (bf16[112,128]{1,0:T(8,128)(2,1)S(1)}, bf16[112,128]{1,0:T(8,128)(2,1)S(1)}, u32[]{:S(2)}, u32[]{:S(2)}) collective-permute-start(bf16[112,128]{1,0:T(8,128)(2,1)S(1)} %copy-done.14), channel_id=1, source_target_pairs={{1,0},{2,1},{3,2},{4,3},{5,4},{6,5},{7,6},{8,7},{9,8},{10,9},{11,1... | collective-permute-start | bytes 86024 | tf_op jit(solution)/shard_map/ppermute | solution.py:570
  68.3 1.5 %collective-permute-start.8 = (bf16[304,128]{1,0:T(8,128)(2,1)}, bf16[304,128]{1,0:T(8,128)(2,1)S(1)}, u32[]{:S(2)}, u32[]{:S(2)}) collective-permute-start(bf16[304,128]{1,0:T(8,128)(2,1)} %get-tuple-element.25), channel_id=1, source_target_pairs={{0,32},{32,0},{64,96},{96,64},{128,160},{160,128},{192,224},{224,1... | collective-permute-start | bytes 233480 | tf_op jit(solution)/shard_map/ppermute | solution.py:628
  70.7 13.6 %copy-start.4 = (bf16[304,128]{1,0:T(8,128)(2,1)}, bf16[304,128]{1,0:T(8,128)(2,1)S(1)}, u32[]{:S(2)}) copy-start(bf16[304,128]{1,0:T(8,128)(2,1)S(1)} %add_convert_fusion.own_ref) | copy-start | bytes 233476
  70.7 7.2 %collective-permute-start.11 = (bf16[304,128]{1,0:T(8,128)(2,1)S(1)}, bf16[304,128]{1,0:T(8,128)(2,1)S(1)}, u32[]{:S(2)}, u32[]{:S(2)}) collective-permute-start(bf16[304,128]{1,0:T(8,128)(2,1)S(1)} %add_convert_fusion.own_ref), channel_id=1, source_target_pairs={{0,192},{32,224},{64,0},{96,32},{128,64},{160,96},{192,128},{224,1... | collective-permute-start | bytes 233480 | tf_op jit(solution)/shard_map/ppermute | solution.py:625
  71.2 8.3 %collective-permute-start.10 = (bf16[304,128]{1,0:T(8,128)(2,1)S(1)}, bf16[304,128]{1,0:T(8,128)(2,1)S(1)}, u32[]{:S(2)}, u32[]{:S(2)}) collective-permute-start(bf16[304,128]{1,0:T(8,128)(2,1)S(1)} %add_convert_fusion.own_ref), channel_id=1, source_target_pairs={{0,128},{32,160},{64,192},{96,224},{128,0},{160,32},{192,64},{224,... | collective-permute-start | bytes 233480 | tf_op jit(solution)/shard_map/ppermute | solution.py:625
  75.5 8.8 %collective-permute-start.9 = (bf16[304,128]{1,0:T(8,128)(2,1)S(1)}, bf16[304,128]{1,0:T(8,128)(2,1)S(1)}, u32[]{:S(2)}, u32[]{:S(2)}) collective-permute-start(bf16[304,128]{1,0:T(8,128)(2,1)S(1)} %add_convert_fusion.own_ref), channel_id=1, source_target_pairs={{0,64},{32,96},{64,128},{96,160},{128,192},{160,224},{192,0},{224,... | collective-permute-start | bytes 233480 | tf_op jit(solution)/shard_map/ppermute | solution.py:625
  77.9 6.4 %copy-start.10 = (bf16[304,128]{1,0:T(8,128)(2,1)}, bf16[304,128]{1,0:T(8,128)(2,1)S(1)}, u32[]{:S(2)}) copy-start(bf16[304,128]{1,0:T(8,128)(2,1)S(1)} %collective-permute-done.11.c_ref) | copy-start | bytes 233476
  79.6 4.7 %copy-start.11 = (bf16[304,128]{1,0:T(8,128)(2,1)}, bf16[304,128]{1,0:T(8,128)(2,1)S(1)}, u32[]{:S(2)}) copy-start(bf16[304,128]{1,0:T(8,128)(2,1)S(1)} %collective-permute-done.10.b_ref) | copy-start | bytes 233476
  87.5 7.6 %collective-permute-start.14 = (bf16[240,128]{1,0:T(8,128)(2,1)}, bf16[240,128]{1,0:T(8,128)(2,1)S(1)}, u32[]{:S(2)}, u32[]{:S(2)}) collective-permute-start(bf16[240,128]{1,0:T(8,128)(2,1)} %get-tuple-element.26), channel_id=1, source_target_pairs={{0,3},{1,0},{2,1},{3,2},{4,7},{5,4},{6,5},{7,6},{8,11},{9,8},{10,9... | collective-permute-start | bytes 184328 | tf_op jit(solution)/shard_map/ppermute | solution.py:625
  93.0 6.4 %collective-permute-start.13 = (bf16[240,128]{1,0:T(8,128)(2,1)}, bf16[240,128]{1,0:T(8,128)(2,1)S(1)}, u32[]{:S(2)}, u32[]{:S(2)}) collective-permute-start(bf16[240,128]{1,0:T(8,128)(2,1)} %get-tuple-element.26), channel_id=1, source_target_pairs={{0,1},{1,2},{2,3},{3,0},{4,5},{5,6},{6,7},{7,4},{8,9},{9,10},{10,1... | collective-permute-start | bytes 184328 | tf_op jit(solution)/shard_map/ppermute | solution.py:625
  93.0 6.4 %collective-permute-start.12 = (bf16[240,128]{1,0:T(8,128)(2,1)}, bf16[240,128]{1,0:T(8,128)(2,1)S(1)}, u32[]{:S(2)}, u32[]{:S(2)}) collective-permute-start(bf16[240,128]{1,0:T(8,128)(2,1)} %get-tuple-element.26), channel_id=1, source_target_pairs={{0,2},{1,3},{2,0},{3,1},{4,6},{5,7},{6,4},{7,5},{8,10},{9,11},{10,... | collective-permute-start | bytes 184328 | tf_op jit(solution)/shard_map/ppermute | solution.py:625
  100.2 5.5 %collective-permute-start.17 = (bf16[240,128]{1,0:T(8,128)(2,1)S(1)}, bf16[240,128]{1,0:T(8,128)(2,1)S(1)}, u32[]{:S(2)}, u32[]{:S(2)}) collective-permute-start(bf16[240,128]{1,0:T(8,128)(2,1)S(1)} %add_convert_fusion.2), channel_id=1, source_target_pairs={{0,12},{1,13},{2,14},{3,15},{4,0},{5,1},{6,2},{7,3},{8,4},{9,5},{1... | collective-permute-start | bytes 184328 | tf_op jit(solution)/shard_map/ppermute | solution.py:625
  100.3 5.7 %collective-permute-start.16 = (bf16[240,128]{1,0:T(8,128)(2,1)S(1)}, bf16[240,128]{1,0:T(8,128)(2,1)S(1)}, u32[]{:S(2)}, u32[]{:S(2)}) collective-permute-start(bf16[240,128]{1,0:T(8,128)(2,1)S(1)} %add_convert_fusion.2), channel_id=1, source_target_pairs={{0,4},{1,5},{2,6},{3,7},{4,8},{5,9},{6,10},{7,11},{8,12},{9,13},{1... | collective-permute-start | bytes 184328 | tf_op jit(solution)/shard_map/ppermute | solution.py:625
  103.5 5.7 %collective-permute-start.15 = (bf16[240,128]{1,0:T(8,128)(2,1)S(1)}, bf16[240,128]{1,0:T(8,128)(2,1)S(1)}, u32[]{:S(2)}, u32[]{:S(2)}) collective-permute-start(bf16[240,128]{1,0:T(8,128)(2,1)S(1)} %add_convert_fusion.2), channel_id=1, source_target_pairs={{0,8},{1,9},{2,10},{3,11},{4,12},{5,13},{6,14},{7,15},{8,0},{9,1},... | collective-permute-start | bytes 184328 | tf_op jit(solution)/shard_map/ppermute | solution.py:625
  109.3 4.3 %copy-start.5 = (bf16[240,128]{1,0:T(8,128)(2,1)}, bf16[240,128]{1,0:T(8,128)(2,1)S(1)}, u32[]{:S(2)}) copy-start(bf16[240,128]{1,0:T(8,128)(2,1)S(1)} %add_convert_fusion.1.own_ref) | copy-start | bytes 184324
  109.3 4.3 %collective-permute-start.18 = (bf16[240,128]{1,0:T(8,128)(2,1)S(1)}, bf16[240,128]{1,0:T(8,128)(2,1)S(1)}, u32[]{:S(2)}, u32[]{:S(2)}) collective-permute-start(bf16[240,128]{1,0:T(8,128)(2,1)S(1)} %add_convert_fusion.1.own_ref), channel_id=1, source_target_pairs={{0,16},{1,17},{2,18},{3,19},{4,20},{5,21},{6,22},{7,23},{8,24},{9,... | collective-permute-start | bytes 184328 | tf_op jit(solution)/shard_map/ppermute | solution.py:649
  (6 other events, 3.7 us)

commit v3 on v2

--- a/solution.py
+++ b/solution.py
@@ -21,7 +21,6 @@
 HIGH = lax.Precision.HIGHEST
 f32 = jnp.float32
 bf16 = jnp.bfloat16
-VMEM_LIMIT = 56 * 1024 * 1024
 
 
 def dot(a, b, precision=None):
@@ -83,7 +82,7 @@
     return value, slope
 
 
-def first_kernel(seed_ref, mask_ref, cols_ref, band_ref, out_ref):
+def first_kernel(seed_ref, mask_ref, cols_ref, band_ref, cot_ref, out_ref):
     out_ref[0:32, :] = cols_ref[...]
     lane = iota((8, 128), 1)
     seed = seed_ref[0, 0]
@@ -94,10 +93,22 @@
     band = jnp.concatenate([band_ref[...].astype(f32), jnp.zeros((8, 112), f32)], axis=1)
     out_ref[32:48, 0:128] = jnp.concatenate([band, numbers.astype(f32)], axis=0).astype(bf16)
     out_ref[32:48, 128:] = jnp.zeros((16, COLS - 128), bf16)
+    lane = iota((16, 128), 1)
+    for side, cols, shift in ((0, slice(0, 128), 0), (1, slice(COLS - 128, COLS), 8)):
+        for half in range(2):
+            total = jnp.zeros((16, 128), f32)
+            for i in range(16):
+                piece = cot_ref[16 * half + i, :, cols].astype(f32)
+                turn = (8 * i + shift) % 128
+                piece = pltpu.roll(piece, turn, 1) if turn else piece
+                here = jnp.logical_and(lane >= 8 * i, lane < 8 * i + 8)
+                total = jnp.where(here, piece, total)
+            at = 256 * side + 128 * half
+            out_ref[48:64, at : at + 128] = total.astype(bf16)
 
 
 def pack_kernel(
-    own_ref, one_ref, two_ref, three_ref, other_ref, cot_ref, up_ref, down_ref,
+    own_ref, one_ref, two_ref, three_ref, other_ref,
     feats_ref, west_ref, east_ref, bands_ref,
 ):
     even = lax.rem(lax.axis_index("row"), 2) == 0
@@ -107,6 +118,7 @@
     east = jnp.zeros((32, 128), f32)
     bands = jnp.zeros((8, 128), f32)
     seeds = jnp.zeros((8, 128), f32)
+    edges = []
     for t in range(8):
         a = mine[t // 2]
         b = other_ref.at[t // 2]
@@ -121,6 +133,7 @@
         last = pick(slice(0, 32), slice(COLS - 128, COLS)).astype(f32)
         turn = (16 * t + 16) % 128
         east = jnp.where(here, pltpu.roll(last, turn, 1) if turn else last, east)
+        edges.append(pick(slice(48, 64), slice(0, COLS)).astype(f32) if t in (0, 1, 2, 7) else None)
         extra = pick(slice(32, 48), slice(0, 128)).astype(f32)
         extra = pltpu.roll(extra, 16 * t, 1) if t else extra
         bands = jnp.where(here[:8], extra[0:8], bands)
@@ -130,20 +143,12 @@
     for ref, value in ((west_ref, west), (east_ref, east)):
         ref[0:32, :] = value.astype(bf16)
         ref[96:112, :] = tail
-    lane = iota((64, 128), 1)
-    for ref, cols, shift in ((west_ref, slice(0, 128), 0), (east_ref, slice(COLS - 128, COLS), 8)):
-        total = jnp.zeros((64, 128), f32)
-        for g in range(16):
-            parts = []
-            for ch in (2 * g, 2 * g + 1):
-                parts.append(up_ref[ch, :, cols].astype(f32))
-                parts.append(cot_ref[ch, :, cols].astype(f32))
-                parts.append(down_ref[ch, :, cols].astype(f32))
-            whole = jnp.concatenate(parts, axis=0)
-            turn = (8 * g + shift) % 128
-            whole = pltpu.roll(whole, turn, 1) if turn else whole
-            total = jnp.where(jnp.logical_and(lane >= 8 * g, lane < 8 * g + 8), whole, total)
-        ref[32:96, :] = total.astype(bf16)
+    around = [edges[7], edges[0], edges[1]], [edges[0], edges[1], edges[2]]
+    three = [jnp.where(even, x, y) for x, y in zip(*around)]
+    rows = jnp.concatenate([three[0][8:16], three[1], three[2][0:8]], axis=0).astype(bf16)
+    for ref, at in ((west_ref, 0), (east_ref, 256)):
+        ref[32:64, :] = rows[:, at : at + 128]
+        ref[64:96, :] = rows[:, at + 128 : at + 256]
     chunk = jnp.concatenate([bands, blank], axis=0).astype(bf16)
     bands_ref[...] = jnp.broadcast_to(chunk[None], (32, 16, 128))
 
@@ -160,8 +165,8 @@
     w1_ref,
     w2_ref,
     cot_ref,
-    cot_up_ref,
-    cot_down_ref,
+    inner_ref,
+    outer_ref,
     out_ref,
     send_ref,
     t1,
@@ -273,14 +278,15 @@
         seed_rows[step] = seed.astype(jnp.int32)
         keep_rows[step] = keep
 
-    lane64 = iota((64, 128), 1)
-    right = right_ref[32:96, :].astype(f32)
-    left = left_ref[32:96, :].astype(f32)
-    for g in range(16):
-        r_turn = (128 - 8 * g) % 128
-        l_turn = 120 - 8 * g
-        cot_halo[64 * g : 64 * g + 64, :] = jnp.where(
-            lane64 < 64,
+    lane32 = iota((32, 128), 1)
+    for ch in range(K):
+        first = 32 + ch // 16 * 32
+        right = right_ref[first : first + 32, :].astype(f32)
+        left = left_ref[first : first + 32, :].astype(f32)
+        r_turn = (128 - 8 * ch) % 128
+        l_turn = (120 - 8 * ch) % 128
+        cot_halo[32 * ch : 32 * ch + 32, :] = jnp.where(
+            lane32 < 64,
             pltpu.roll(right, r_turn, 1) if r_turn else right,
             pltpu.roll(left, l_turn, 1) if l_turn else left,
         )
@@ -345,9 +351,11 @@
             value, slope = gelu_parts(acc[at_acc, at : at + 16, :])
             factor = factor_of(p)
             if k == 0:
-                cot = cot_up_ref[at : at + 16, :].astype(f32)
+                cot = jnp.where(core == 0, outer_ref[at : at + 16, :], inner_ref[at : at + 16, :])
+                cot = cot.astype(f32)
             elif k == 3:
-                cot = cot_down_ref[at : at + 16, :].astype(f32)
+                cot = jnp.where(core == 0, inner_ref[at : at + 16, :], outer_ref[at : at + 16, :])
+                cot = cot.astype(f32)
             else:
                 parts = []
                 for ch in (2 * p, 2 * p + 1):
@@ -505,7 +513,7 @@
     gband_ref[...] = mine[0:8, 0:16].astype(bf16)
 
 
-def call(kernel, shapes, args, scratch=(), scalars=0):
+def call(kernel, shapes, args, scratch=(), scalars=0, limit=8):
     whole = pl.BlockSpec(memory_space=pltpu.VMEM)
     return pl.pallas_call(
         kernel,
@@ -514,7 +522,7 @@
         + [whole] * (len(args) - scalars),
         out_specs=jax.tree.map(lambda _: whole, shapes),
         scratch_shapes=list(scratch),
-        compiler_params=pltpu.CompilerParams(vmem_limit_bytes=VMEM_LIMIT),
+        compiler_params=pltpu.CompilerParams(vmem_limit_bytes=limit * 1024 * 1024),
     )(*args)
 
 
@@ -537,16 +545,11 @@
     rows = lax.axis_size("row")
     cols = lax.axis_size("col")
 
-    south = [(i, (i + 1) % rows) for i in range(rows)]
-    north = [(j, i) for i, j in south]
-    cot_up = lax.ppermute(cotangent[:, 8:, :], "row", south)
-    cot_down = lax.ppermute(cotangent[:, :8, :], "row", north)
-
     cols_t = col_emb.T
     own = call(
         first_kernel,
-        shape((48, COLS), bf16),
-        (drop_seeds, tile_mask, cols_t, band_emb.T),
+        shape((64, COLS), bf16),
+        (drop_seeds, tile_mask, cols_t, band_emb.T, cotangent),
         scalars=2,
     )
     beyond = [
@@ -563,13 +566,20 @@
             shape((112, 128), bf16),
             shape((32, 16, 128), bf16),
         ),
-        (own, *beyond, other, cotangent, cot_up, cot_down),
+        (own, *beyond, other),
     )
     east = [(i, (i + 1) % cols) for i in range(cols)]
     west = [(j, i) for i, j in east]
     right = lax.ppermute(west_edge, "col", west)
     left = lax.ppermute(east_edge, "col", east)
     bands = lax.all_to_all(bands, "col", 0, 0)
+
+    core = lax.rem(lax.axis_index("row"), 2)
+    inner = lax.dynamic_slice_in_dim(cotangent, 8 * (1 - core), 8, 1)
+    outer = lax.dynamic_slice_in_dim(cotangent, 8 * core, 8, 1)
+    pairs = [(i, (i + 1 if i % 2 else i - 1) % rows) for i in range(rows)]
+    inner = lax.ppermute(inner, "row", flip).reshape(BLK, COLS)
+    outer = lax.ppermute(outer, "row", pairs).reshape(BLK, COLS)
 
     w1 = jnp.transpose(first_kernel_weight, (2, 3, 0, 1)).reshape(TAPS, K, K)
     w2 = jnp.transpose(second_kernel_weight, (2, 3, 0, 1)).reshape(TAPS, K, K)
@@ -588,8 +598,8 @@
             w1,
             w2,
             cotangent,
-            cot_up.reshape(BLK, COLS),
-            cot_down.reshape(BLK, COLS),
+            inner,
+            outer,
         ),
         scratch=(
             pltpu.VMEM((BLK, 6 * BLK), bf16),
@@ -613,6 +623,7 @@
             pltpu.VMEM((8 * K, WIDE), bf16),
         ),
         scalars=1,
+        limit=44,
     )
 
     def added(x, y):

time: 117 us -> 105 us (0.90)
  waiting for transfers between devices: 34.5 us -> 27.8 us
  Pallas kernels: 32.2 us -> 25.8 us
  starting transfers between devices: 41.3 us -> 45.4 us
  other arithmetic: 1.84 us -> 0.13 us
    pallas_call x5, Pallas kernels: 32.2 us -> 25.8 us  [call(): pl.pallas_call(kernel, out_shape=shapes, in_specs=[pl.BlockSpec(memory_sp...]
    ppermute x2, waiting for transfers between devices: 6.11 us -> 0.01 us  [the longest x1 0.01 us: per_device(): outer = lax.ppermute(outer, 'row', pairs).reshape(BLK, COLS)]
    ppermute x2, starting transfers between devices: 0.58 us -> 3.55 us  [the longest x1 3.55 us: per_device(): outer = lax.ppermute(outer, 'row', pairs).reshape(BLK, COLS)]
    ppermute x3, waiting for transfers between devices: 1.66 us -> 4.27 us  [per_device(): lax.ppermute(own, 'row', [((i + 2 * s) % rows, i) for i in range(rows)])]
    ppermute x1, waiting for transfers between devices: 1.44 us -> 0.01 us  [per_device(): other = lax.ppermute(jnp.stack([own] + beyond), 'row', flip)]
    unnamed x36 -> x18, local copies, waits for them, and re-layouts: 3.2 us -> 3.13 us
  transfers between devices with their start and end apart: 20 -> 20, of which waited for: 16 -> 13; matrix products, arithmetic and copies ran while one was open for 1% -> 0% of each run, Pallas kernels for 0% -> 1%
where the time goes in v3:
time: 105 us; the launch traced here: 104 us
  starting transfers between devices  45.4 us (43%)
  waiting for transfers between devices  27.8 us (26%)
  Pallas kernels  25.8 us (25%)
  local copies, waits for them, and re-layouts  3.17 us (3%)
  between operations  2.07 us (2%)
    pallas_call x5, Pallas kernels, call(): pl.pallas_call(kernel, out_shape=shapes, in_specs=[pl.BlockSpec(memory_sp...  25.8 us
    ppermute x9, waiting for transfers between devices, quarters(): lax.ppermute(x, axis, [(i, turned(i, s)) for i in range(count)])  17.5 us
    ppermute x9, starting transfers between devices, quarters(): lax.ppermute(x, axis, [(i, turned(i, s)) for i in range(count)])  16.2 us
    ppermute x3, starting transfers between devices, per_device(): lax.ppermute(own, 'row', [((i + 2 * s) % rows, i) for i in range(rows)])  11.4 us
    all_to_all x1, starting transfers between devices, per_device(): bands = lax.all_to_all(bands, 'col', 0, 0)  7.7 us
    ppermute x3, waiting for transfers between devices, per_device(): lax.ppermute(own, 'row', [((i + 2 * s) % rows, i) for i in range(rows)])  4.27 us
    ppermute x1, starting transfers between devices, per_device(): outer = lax.ppermute(outer, 'row', pairs).reshape(BLK, COLS)  3.55 us
    unnamed x18, local copies, waits for them, and re-layouts  3.13 us
  transfers between devices with their start and end apart: 20, of which 13 were waited for; matrix products, arithmetic and copies ran while one was open for 0% of the time, Pallas kernels for 1%

profile of v3, /device:TPU:6, one launch (start us, length us, event | category | flops | bytes accessed | tf_op | source)
XLA Modules:
  0.0 104.4 jit_solution(11022759398737546388)
XLA Ops:
  1.9 0.7 copy-done.7
  2.6 1.0 copy-done
  3.7 0.8 copy-done.6
  4.6 3.3 %collective-permute-start.2 = (bf16[64,512]{1,0:T(8,128)(2,1)S(1)}, bf16[64,512]{1,0:T(8,128)(2,1)S(1)}, u32[]{:S(2)}, u32[]{:S(2)}) collective-permute-start(bf16[64,512]{1,0:T(8,128)(2,1)S(1)} %shard_map.153.own_ref), channel_id=1, source_target_pairs={{192,0},{224,32},{0,64},{32,96},{64,128},{96,160},{128,192},{160,2... | collective-permute-start | bytes 196616 | tf_op jit(solution)/shard_map/ppermute | solution.py:556
  7.9 5.4 %collective-permute-start.1 = (bf16[64,512]{1,0:T(8,128)(2,1)S(1)}, bf16[64,512]{1,0:T(8,128)(2,1)S(1)}, u32[]{:S(2)}, u32[]{:S(2)}) collective-permute-start(bf16[64,512]{1,0:T(8,128)(2,1)S(1)} %shard_map.153.own_ref), channel_id=1, source_target_pairs={{128,0},{160,32},{192,64},{224,96},{0,128},{32,160},{64,192},{96,2... | collective-permute-start | bytes 196616 | tf_op jit(solution)/shard_map/ppermute | solution.py:556
  13.3 2.7 %collective-permute-start = (bf16[64,512]{1,0:T(8,128)(2,1)S(1)}, bf16[64,512]{1,0:T(8,128)(2,1)S(1)}, u32[]{:S(2)}, u32[]{:S(2)}) collective-permute-start(bf16[64,512]{1,0:T(8,128)(2,1)S(1)} %shard_map.153.own_ref), channel_id=1, source_target_pairs={{64,0},{96,32},{128,64},{160,96},{192,128},{224,160},{0,192},{32,2... | collective-permute-start | bytes 196616 | tf_op jit(solution)/shard_map/ppermute | solution.py:556
  16.0 1.5 %collective-permute-done.1.two_ref = bf16[64,512]{1,0:T(8,128)(2,1)S(1)} collective-permute-done((bf16[64,512]{1,0:T(8,128)(2,1)S(1)}, bf16[64,512]{1,0:T(8,128)(2,1)S(1)}, u32[]{:S(2)}, u32[]{:S(2)}) %collective-permute-start.1) | collective-permute-done | bytes 65568 | tf_op jit(solution)/shard_map/ppermute | solution.py:556
  17.4 2.8 %collective-permute-done.one_ref = bf16[64,512]{1,0:T(8,128)(2,1)S(1)} collective-permute-done((bf16[64,512]{1,0:T(8,128)(2,1)S(1)}, bf16[64,512]{1,0:T(8,128)(2,1)S(1)}, u32[]{:S(2)}, u32[]{:S(2)}) %collective-permute-start) | collective-permute-done | bytes 65568 | tf_op jit(solution)/shard_map/ppermute | solution.py:556
  20.4 3.5 %collective-permute-start.7 = (bf16[32,8,512]{2,1,0:T(8,128)(2,1)S(1)}, bf16[32,8,512]{2,1,0:T(8,128)(2,1)S(1)}, u32[]{:S(2)}, u32[]{:S(2)}) collective-permute-start(bf16[32,8,512]{2,1,0:T(8,128)(2,1)S(1)} %get-tuple-element.33), channel_id=1, source_target_pairs={{0,224},{32,64},{64,32},{96,128},{128,96},{160,192},{192,160},{224... | collective-permute-start | bytes 786440 | tf_op jit(solution)/shard_map/ppermute | solution.py:582
  24.0 0.8 shard_map.154
  24.8 7.7 %all-to-all-start = ((bf16[32,16,128]{2,1,0:T(8,128)(2,1)}), bf16[32,16,128]{2,1,0:T(8,128)(2,1)S(1)}, u32[]{:S(2)}, u32[]{:S(2)}) async-start(bf16[32,16,128]{2,1,0:T(8,128)(2,1)} %get-tuple-element.21), calls=%async_computation | async-start | bytes 262144 | tf_op jit(solution)/shard_map/all_to_all | solution.py:575
  32.5 1.5 %collective-permute-start.5 = (bf16[112,128]{1,0:T(8,128)(2,1)S(1)}, bf16[112,128]{1,0:T(8,128)(2,1)S(1)}, u32[]{:S(2)}, u32[]{:S(2)}) collective-permute-start(bf16[112,128]{1,0:T(8,128)(2,1)S(1)} %get-tuple-element.23), channel_id=1, source_target_pairs={{0,1},{1,2},{2,3},{3,4},{4,5},{5,6},{6,7},{7,8},{8,9},{9,10},{10,1... | collective-permute-start | bytes 86024 | tf_op jit(solution)/shard_map/ppermute | solution.py:574
  34.0 2.7 %collective-permute-start.4 = (bf16[112,128]{1,0:T(8,128)(2,1)S(1)}, bf16[112,128]{1,0:T(8,128)(2,1)S(1)}, u32[]{:S(2)}, u32[]{:S(2)}) collective-permute-start(bf16[112,128]{1,0:T(8,128)(2,1)S(1)} %get-tuple-element.22.own_ref), channel_id=1, source_target_pairs={{1,0},{2,1},{3,2},{4,3},{5,4},{6,5},{7,6},{8,7},{9,8},{10,9},{11,1... | collective-permute-start | bytes 86024 | tf_op jit(solution)/shard_map/ppermute | solution.py:573
  36.7 2.1 %collective-permute-done.5.left_ref = bf16[112,128]{1,0:T(8,128)(2,1)S(1)} collective-permute-done((bf16[112,128]{1,0:T(8,128)(2,1)S(1)}, bf16[112,128]{1,0:T(8,128)(2,1)S(1)}, u32[]{:S(2)}, u32[]{:S(2)}) %collective-permute-start.5) | collective-permute-done | bytes 28704 | tf_op jit(solution)/shard_map/ppermute | solution.py:574
  39.3 0.6 copy-done.8
  39.9 22.5 %shard_map.155 = (bf16[32,16,512]{2,1,0:T(8,128)(2,1)}, bf16[304,128]{1,0:T(8,128)(2,1)S(1)}) custom-call(s32[2]{0:T(128)S(1)} %copy-done.8, bf16[8,32,512]{2,1,0:T(8,128)(2,1)S(1)} %get-tuple-element.20.feats_ref, bf16[32,16,128]{2,1,0:T(8,128)(2,1)S(1)} %all-to-all-done.bands_ref, bf16[112,128]{1,0:T(8,128)(2,1)S(1)} %get-tuple-element.22.own_ref, ...), custom_call_target="tpu_custom_call" | custom-call | tf_op jit(solution)/shard_map/pallas_call | solution.py:518
  62.5 1.3 %collective-permute-done.8 = bf16[304,128]{1,0:T(8,128)(2,1)S(1)} collective-permute-done((bf16[304,128]{1,0:T(8,128)(2,1)S(1)}, bf16[304,128]{1,0:T(8,128)(2,1)S(1)}, u32[]{:S(2)}, u32[]{:S(2)}) %collective-permute-start.8) | collective-permute-done | bytes 77856 | tf_op jit(solution)/shard_map/ppermute | solution.py:639
  63.8 1.4 %collective-permute-start.11 = (bf16[304,128]{1,0:T(8,128)(2,1)S(1)}, bf16[304,128]{1,0:T(8,128)(2,1)S(1)}, u32[]{:S(2)}, u32[]{:S(2)}) collective-permute-start(bf16[304,128]{1,0:T(8,128)(2,1)S(1)} %add_convert_fusion.own_ref), channel_id=1, source_target_pairs={{0,192},{32,224},{64,0},{96,32},{128,64},{160,96},{192,128},{224,1... | collective-permute-start | bytes 233480 | tf_op jit(solution)/shard_map/ppermute | solution.py:636
  65.2 3.4 %collective-permute-start.10 = (bf16[304,128]{1,0:T(8,128)(2,1)S(1)}, bf16[304,128]{1,0:T(8,128)(2,1)S(1)}, u32[]{:S(2)}, u32[]{:S(2)}) collective-permute-start(bf16[304,128]{1,0:T(8,128)(2,1)S(1)} %add_convert_fusion.own_ref), channel_id=1, source_target_pairs={{0,128},{32,160},{64,192},{96,224},{128,0},{160,32},{192,64},{224,... | collective-permute-start | bytes 233480 | tf_op jit(solution)/shard_map/ppermute | solution.py:636
  68.5 0.7 collective-permute-start.9
  69.2 3.1 %collective-permute-done.11.c_ref = bf16[304,128]{1,0:T(8,128)(2,1)S(1)} collective-permute-done((bf16[304,128]{1,0:T(8,128)(2,1)S(1)}, bf16[304,128]{1,0:T(8,128)(2,1)S(1)}, u32[]{:S(2)}, u32[]{:S(2)}) %collective-permute-start.11) | collective-permute-done | bytes 77856 | tf_op jit(solution)/shard_map/ppermute | solution.py:636
  72.3 3.7 %collective-permute-done.10.b_ref = bf16[304,128]{1,0:T(8,128)(2,1)S(1)} collective-permute-done((bf16[304,128]{1,0:T(8,128)(2,1)S(1)}, bf16[304,128]{1,0:T(8,128)(2,1)S(1)}, u32[]{:S(2)}, u32[]{:S(2)}) %collective-permute-start.10) | collective-permute-done | bytes 77856 | tf_op jit(solution)/shard_map/ppermute | solution.py:636
  76.4 1.4 %shard_map.156 = (bf16[32,512]{1,0:T(8,128)(2,1)}, bf16[240,128]{1,0:T(8,128)(2,1)S(1)}) custom-call(bf16[304,128]{1,0:T(8,128)(2,1)S(1)} %add_convert_fusion.own_ref, bf16[304,128]{1,0:T(8,128)(2,1)S(1)} %collective-permute-done.9.a_ref, bf16[304,128]{1,0:T(8,128)(2,1)S(1)} %collective-permute-done.10.b_ref, ...), custom_call_target="tpu_custom_call" | custom-call | tf_op jit(solution)/shard_map/pallas_call | solution.py:518
  77.8 6.0 %collective-permute-start.14 = (bf16[240,128]{1,0:T(8,128)(2,1)S(1)}, bf16[240,128]{1,0:T(8,128)(2,1)S(1)}, u32[]{:S(2)}, u32[]{:S(2)}) collective-permute-start(bf16[240,128]{1,0:T(8,128)(2,1)S(1)} %get-tuple-element.26), channel_id=1, source_target_pairs={{0,3},{1,0},{2,1},{3,2},{4,7},{5,4},{6,5},{7,6},{8,11},{9,8},{10,9... | collective-permute-start | bytes 184328 | tf_op jit(solution)/shard_map/ppermute | solution.py:636
  83.8 1.5 %collective-permute-start.12 = (bf16[240,128]{1,0:T(8,128)(2,1)S(1)}, bf16[240,128]{1,0:T(8,128)(2,1)S(1)}, u32[]{:S(2)}, u32[]{:S(2)}) collective-permute-start(bf16[240,128]{1,0:T(8,128)(2,1)S(1)} %get-tuple-element.26), channel_id=1, source_target_pairs={{0,2},{1,3},{2,0},{3,1},{4,6},{5,7},{6,4},{7,5},{8,10},{9,11},{10,... | collective-permute-start | bytes 184328 | tf_op jit(solution)/shard_map/ppermute | solution.py:636
  85.7 4.2 %collective-permute-done.13 = bf16[240,128]{1,0:T(8,128)(2,1)S(1)} collective-permute-done((bf16[240,128]{1,0:T(8,128)(2,1)S(1)}, bf16[240,128]{1,0:T(8,128)(2,1)S(1)}, u32[]{:S(2)}, u32[]{:S(2)}) %collective-permute-start.13) | collective-permute-done | bytes 61472 | tf_op jit(solution)/shard_map/ppermute | solution.py:636
  90.0 3.2 %collective-permute-start.16 = (bf16[240,128]{1,0:T(8,128)(2,1)S(1)}, bf16[240,128]{1,0:T(8,128)(2,1)S(1)}, u32[]{:S(2)}, u32[]{:S(2)}) collective-permute-start(bf16[240,128]{1,0:T(8,128)(2,1)S(1)} %add_convert_fusion.2), channel_id=1, source_target_pairs={{0,4},{1,5},{2,6},{3,7},{4,8},{5,9},{6,10},{7,11},{8,12},{9,13},{1... | collective-permute-start | bytes 184328 | tf_op jit(solution)/shard_map/ppermute | solution.py:636
  93.3 2.9 %collective-permute-done.17 = bf16[240,128]{1,0:T(8,128)(2,1)S(1)} collective-permute-done((bf16[240,128]{1,0:T(8,128)(2,1)S(1)}, bf16[240,128]{1,0:T(8,128)(2,1)S(1)}, u32[]{:S(2)}, u32[]{:S(2)}) %collective-permute-start.17) | collective-permute-done | bytes 61472 | tf_op jit(solution)/shard_map/ppermute | solution.py:636
  96.1 2.9 %collective-permute-done.15 = bf16[240,128]{1,0:T(8,128)(2,1)S(1)} collective-permute-done((bf16[240,128]{1,0:T(8,128)(2,1)S(1)}, bf16[240,128]{1,0:T(8,128)(2,1)S(1)}, u32[]{:S(2)}, u32[]{:S(2)}) %collective-permute-start.15) | collective-permute-done | bytes 61472 | tf_op jit(solution)/shard_map/ppermute | solution.py:636
  99.0 2.2 %collective-permute-start.18 = (bf16[240,128]{1,0:T(8,128)(2,1)S(1)}, bf16[240,128]{1,0:T(8,128)(2,1)S(1)}, u32[]{:S(2)}, u32[]{:S(2)}) collective-permute-start(bf16[240,128]{1,0:T(8,128)(2,1)S(1)} %add_convert_fusion.1.own_ref), channel_id=1, source_target_pairs={{0,16},{1,17},{2,18},{3,19},{4,20},{5,21},{6,22},{7,23},{8,24},{9,... | collective-permute-start | bytes 184328 | tf_op jit(solution)/shard_map/ppermute | solution.py:660
  101.2 2.2 %collective-permute-done.18.a_ref = bf16[240,128]{1,0:T(8,128)(2,1)S(1)} collective-permute-done((bf16[240,128]{1,0:T(8,128)(2,1)S(1)}, bf16[240,128]{1,0:T(8,128)(2,1)S(1)}, u32[]{:S(2)}, u32[]{:S(2)}) %collective-permute-start.18) | collective-permute-done | bytes 61472 | tf_op jit(solution)/shard_map/ppermute | solution.py:660
  103.4 1.0 shard_map.157
  (36 shorter events, 1.8 us)
Async XLA Ops:
  1.9 0.7 copy-start.7
  2.6 1.0 copy-start
  3.6 0.8 copy-start.6
  4.4 16.0 %copy-start.1 = (bf16[32,16,512]{2,1,0:T(8,128)(2,1)S(1)}, bf16[32,16,512]{2,1,0:T(8,128)(2,1)}, u32[]{:S(2)}) copy-start(bf16[32,16,512]{2,1,0:T(8,128)(2,1)} %cot_ref.3) | copy-start | bytes 1572868
  4.6 11.4 %collective-permute-start.2 = (bf16[64,512]{1,0:T(8,128)(2,1)S(1)}, bf16[64,512]{1,0:T(8,128)(2,1)S(1)}, u32[]{:S(2)}, u32[]{:S(2)}) collective-permute-start(bf16[64,512]{1,0:T(8,128)(2,1)S(1)} %shard_map.153.own_ref), channel_id=1, source_target_pairs={{192,0},{224,32},{0,64},{32,96},{64,128},{96,160},{128,192},{160,2... | collective-permute-start | bytes 196616 | tf_op jit(solution)/shard_map/ppermute | solution.py:556
  7.9 9.5 %collective-permute-start.1 = (bf16[64,512]{1,0:T(8,128)(2,1)S(1)}, bf16[64,512]{1,0:T(8,128)(2,1)S(1)}, u32[]{:S(2)}, u32[]{:S(2)}) collective-permute-start(bf16[64,512]{1,0:T(8,128)(2,1)S(1)} %shard_map.153.own_ref), channel_id=1, source_target_pairs={{128,0},{160,32},{192,64},{224,96},{0,128},{32,160},{64,192},{96,2... | collective-permute-start | bytes 196616 | tf_op jit(solution)/shard_map/ppermute | solution.py:556
  13.3 6.9 %collective-permute-start = (bf16[64,512]{1,0:T(8,128)(2,1)S(1)}, bf16[64,512]{1,0:T(8,128)(2,1)S(1)}, u32[]{:S(2)}, u32[]{:S(2)}) collective-permute-start(bf16[64,512]{1,0:T(8,128)(2,1)S(1)} %shard_map.153.own_ref), channel_id=1, source_target_pairs={{64,0},{96,32},{128,64},{160,96},{192,128},{224,160},{0,192},{32,2... | collective-permute-start | bytes 196616 | tf_op jit(solution)/shard_map/ppermute | solution.py:556
  20.3 3.7 %collective-permute-start.3 = (bf16[4,64,512]{2,1,0:T(8,128)(2,1)S(1)}, bf16[4,64,512]{2,1,0:T(8,128)(2,1)S(1)}, u32[]{:S(2)}, u32[]{:S(2)}) collective-permute-start(bf16[4,64,512]{2,1,0:T(8,128)(2,1)S(1)} %pad_maximum_fusion), channel_id=1, source_target_pairs={{0,32},{32,0},{64,96},{96,64},{128,160},{160,128},{192,224},{224,1... | collective-permute-start | bytes 786440 | tf_op jit(solution)/shard_map/ppermute | solution.py:559
  20.4 16.3 %collective-permute-start.7 = (bf16[32,8,512]{2,1,0:T(8,128)(2,1)S(1)}, bf16[32,8,512]{2,1,0:T(8,128)(2,1)S(1)}, u32[]{:S(2)}, u32[]{:S(2)}) collective-permute-start(bf16[32,8,512]{2,1,0:T(8,128)(2,1)S(1)} %get-tuple-element.33), channel_id=1, source_target_pairs={{0,224},{32,64},{64,32},{96,128},{128,96},{160,192},{192,160},{224... | collective-permute-start | bytes 786440 | tf_op jit(solution)/shard_map/ppermute | solution.py:582
  24.0 12.7 %collective-permute-start.6 = (bf16[32,8,512]{2,1,0:T(8,128)(2,1)S(1)}, bf16[32,8,512]{2,1,0:T(8,128)(2,1)S(1)}, u32[]{:S(2)}, u32[]{:S(2)}) collective-permute-start(bf16[32,8,512]{2,1,0:T(8,128)(2,1)S(1)} %get-tuple-element.34), channel_id=1, source_target_pairs={{0,32},{32,0},{64,96},{96,64},{128,160},{160,128},{192,224},{224,1... | collective-permute-start | bytes 786440 | tf_op jit(solution)/shard_map/ppermute | solution.py:581
  24.8 14.5 %copy-start.2 = (bf16[32,32,3,3]{1,0,3,2:T(8,128)(2,1)S(1)}, bf16[32,32,3,3]{1,0,3,2:T(8,128)(2,1)}, u32[]{:S(2)}) copy-start(bf16[32,32,3,3]{1,0,3,2:T(8,128)(2,1)} %param.14) | copy-start | bytes 55300
  24.8 14.5 %copy-start.3 = (bf16[32,32,3,3]{1,0,3,2:T(8,128)(2,1)S(1)}, bf16[32,32,3,3]{1,0,3,2:T(8,128)(2,1)}, u32[]{:S(2)}) copy-start(bf16[32,32,3,3]{1,0,3,2:T(8,128)(2,1)} %param.15) | copy-start | bytes 55300
  24.8 14.5 %copy-start.5 = (bf16[256,32]{0,1:T(8,128)(2,1)S(1)}, bf16[256,32]{0,1:T(8,128)(2,1)}, u32[]{:S(2)}) copy-start(bf16[256,32]{0,1:T(8,128)(2,1)} %param.12) | copy-start | bytes 49156
  24.8 14.5 %all-to-all-start = ((bf16[32,16,128]{2,1,0:T(8,128)(2,1)}), bf16[32,16,128]{2,1,0:T(8,128)(2,1)S(1)}, u32[]{:S(2)}, u32[]{:S(2)}) async-start(bf16[32,16,128]{2,1,0:T(8,128)(2,1)} %get-tuple-element.21), calls=%async_computation | async-start | bytes 262144 | tf_op jit(solution)/shard_map/all_to_all | solution.py:575
  32.5 6.8 %copy-start.4 = (bf16[256,32]{0,1:T(8,128)(2,1)S(1)}, bf16[256,32]{0,1:T(8,128)(2,1)}, u32[]{:S(2)}) copy-start(bf16[256,32]{0,1:T(8,128)(2,1)} %param.13) | copy-start | bytes 49156
  32.5 6.3 %collective-permute-start.5 = (bf16[112,128]{1,0:T(8,128)(2,1)S(1)}, bf16[112,128]{1,0:T(8,128)(2,1)S(1)}, u32[]{:S(2)}, u32[]{:S(2)}) collective-permute-start(bf16[112,128]{1,0:T(8,128)(2,1)S(1)} %get-tuple-element.23), channel_id=1, source_target_pairs={{0,1},{1,2},{2,3},{3,4},{4,5},{5,6},{6,7},{7,8},{8,9},{9,10},{10,1... | collective-permute-start | bytes 86024 | tf_op jit(solution)/shard_map/ppermute | solution.py:574
  34.0 4.8 %collective-permute-start.4 = (bf16[112,128]{1,0:T(8,128)(2,1)S(1)}, bf16[112,128]{1,0:T(8,128)(2,1)S(1)}, u32[]{:S(2)}, u32[]{:S(2)}) collective-permute-start(bf16[112,128]{1,0:T(8,128)(2,1)S(1)} %get-tuple-element.22.own_ref), channel_id=1, source_target_pairs={{1,0},{2,1},{3,2},{4,3},{5,4},{6,5},{7,6},{8,7},{9,8},{10,9},{11,1... | collective-permute-start | bytes 86024 | tf_op jit(solution)/shard_map/ppermute | solution.py:573
  39.3 0.7 copy-start.8
  62.4 1.4 %collective-permute-start.8 = (bf16[304,128]{1,0:T(8,128)(2,1)S(1)}, bf16[304,128]{1,0:T(8,128)(2,1)S(1)}, u32[]{:S(2)}, u32[]{:S(2)}) collective-permute-start(bf16[304,128]{1,0:T(8,128)(2,1)S(1)} %get-tuple-element.25), channel_id=1, source_target_pairs={{0,32},{32,0},{64,96},{96,64},{128,160},{160,128},{192,224},{224,1... | collective-permute-start | bytes 233480 | tf_op jit(solution)/shard_map/ppermute | solution.py:639
  63.8 8.5 %collective-permute-start.11 = (bf16[304,128]{1,0:T(8,128)(2,1)S(1)}, bf16[304,128]{1,0:T(8,128)(2,1)S(1)}, u32[]{:S(2)}, u32[]{:S(2)}) collective-permute-start(bf16[304,128]{1,0:T(8,128)(2,1)S(1)} %add_convert_fusion.own_ref), channel_id=1, source_target_pairs={{0,192},{32,224},{64,0},{96,32},{128,64},{160,96},{192,128},{224,1... | collective-permute-start | bytes 233480 | tf_op jit(solution)/shard_map/ppermute | solution.py:636
  65.2 10.9 %collective-permute-start.10 = (bf16[304,128]{1,0:T(8,128)(2,1)S(1)}, bf16[304,128]{1,0:T(8,128)(2,1)S(1)}, u32[]{:S(2)}, u32[]{:S(2)}) collective-permute-start(bf16[304,128]{1,0:T(8,128)(2,1)S(1)} %add_convert_fusion.own_ref), channel_id=1, source_target_pairs={{0,128},{32,160},{64,192},{96,224},{128,0},{160,32},{192,64},{224,... | collective-permute-start | bytes 233480 | tf_op jit(solution)/shard_map/ppermute | solution.py:636
  68.5 7.8 %collective-permute-start.9 = (bf16[304,128]{1,0:T(8,128)(2,1)S(1)}, bf16[304,128]{1,0:T(8,128)(2,1)S(1)}, u32[]{:S(2)}, u32[]{:S(2)}) collective-permute-start(bf16[304,128]{1,0:T(8,128)(2,1)S(1)} %add_convert_fusion.own_ref), channel_id=1, source_target_pairs={{0,64},{32,96},{64,128},{96,160},{128,192},{160,224},{192,0},{224,... | collective-permute-start | bytes 233480 | tf_op jit(solution)/shard_map/ppermute | solution.py:636
  77.8 7.9 %collective-permute-start.14 = (bf16[240,128]{1,0:T(8,128)(2,1)S(1)}, bf16[240,128]{1,0:T(8,128)(2,1)S(1)}, u32[]{:S(2)}, u32[]{:S(2)}) collective-permute-start(bf16[240,128]{1,0:T(8,128)(2,1)S(1)} %get-tuple-element.26), channel_id=1, source_target_pairs={{0,3},{1,0},{2,1},{3,2},{4,7},{5,4},{6,5},{7,6},{8,11},{9,8},{10,9... | collective-permute-start | bytes 184328 | tf_op jit(solution)/shard_map/ppermute | solution.py:636
  83.8 6.1 %collective-permute-start.13 = (bf16[240,128]{1,0:T(8,128)(2,1)S(1)}, bf16[240,128]{1,0:T(8,128)(2,1)S(1)}, u32[]{:S(2)}, u32[]{:S(2)}) collective-permute-start(bf16[240,128]{1,0:T(8,128)(2,1)S(1)} %get-tuple-element.26), channel_id=1, source_target_pairs={{0,1},{1,2},{2,3},{3,0},{4,5},{5,6},{6,7},{7,4},{8,9},{9,10},{10,1... | collective-permute-start | bytes 184328 | tf_op jit(solution)/shard_map/ppermute | solution.py:636
  83.8 6.1 %collective-permute-start.12 = (bf16[240,128]{1,0:T(8,128)(2,1)S(1)}, bf16[240,128]{1,0:T(8,128)(2,1)S(1)}, u32[]{:S(2)}, u32[]{:S(2)}) collective-permute-start(bf16[240,128]{1,0:T(8,128)(2,1)S(1)} %get-tuple-element.26), channel_id=1, source_target_pairs={{0,2},{1,3},{2,0},{3,1},{4,6},{5,7},{6,4},{7,5},{8,10},{9,11},{10,... | collective-permute-start | bytes 184328 | tf_op jit(solution)/shard_map/ppermute | solution.py:636
  90.0 6.2 %collective-permute-start.17 = (bf16[240,128]{1,0:T(8,128)(2,1)S(1)}, bf16[240,128]{1,0:T(8,128)(2,1)S(1)}, u32[]{:S(2)}, u32[]{:S(2)}) collective-permute-start(bf16[240,128]{1,0:T(8,128)(2,1)S(1)} %add_convert_fusion.2), channel_id=1, source_target_pairs={{0,12},{1,13},{2,14},{3,15},{4,0},{5,1},{6,2},{7,3},{8,4},{9,5},{1... | collective-permute-start | bytes 184328 | tf_op jit(solution)/shard_map/ppermute | solution.py:636
  90.0 6.1 %collective-permute-start.16 = (bf16[240,128]{1,0:T(8,128)(2,1)S(1)}, bf16[240,128]{1,0:T(8,128)(2,1)S(1)}, u32[]{:S(2)}, u32[]{:S(2)}) collective-permute-start(bf16[240,128]{1,0:T(8,128)(2,1)S(1)} %add_convert_fusion.2), channel_id=1, source_target_pairs={{0,4},{1,5},{2,6},{3,7},{4,8},{5,9},{6,10},{7,11},{8,12},{9,13},{1... | collective-permute-start | bytes 184328 | tf_op jit(solution)/shard_map/ppermute | solution.py:636
  93.3 5.7 %collective-permute-start.15 = (bf16[240,128]{1,0:T(8,128)(2,1)S(1)}, bf16[240,128]{1,0:T(8,128)(2,1)S(1)}, u32[]{:S(2)}, u32[]{:S(2)}) collective-permute-start(bf16[240,128]{1,0:T(8,128)(2,1)S(1)} %add_convert_fusion.2), channel_id=1, source_target_pairs={{0,8},{1,9},{2,10},{3,11},{4,12},{5,13},{6,14},{7,15},{8,0},{9,1},... | collective-permute-start | bytes 184328 | tf_op jit(solution)/shard_map/ppermute | solution.py:636
  99.0 4.4 %collective-permute-start.18 = (bf16[240,128]{1,0:T(8,128)(2,1)S(1)}, bf16[240,128]{1,0:T(8,128)(2,1)S(1)}, u32[]{:S(2)}, u32[]{:S(2)}) collective-permute-start(bf16[240,128]{1,0:T(8,128)(2,1)S(1)} %add_convert_fusion.1.own_ref), channel_id=1, source_target_pairs={{0,16},{1,17},{2,18},{3,19},{4,20},{5,21},{6,22},{7,23},{8,24},{9,... | collective-permute-start | bytes 184328 | tf_op jit(solution)/shard_map/ppermute | solution.py:660

commit v4 on v3

--- a/solution.py
+++ b/solution.py
@@ -172,7 +172,9 @@
     t1,
     t2,
     t2m,
-    pv,
+    zv,
+    gk,
+    xv,
     hv,
     gv,
     g1,
@@ -181,7 +183,6 @@
     first_out,
     row_all,
     row3,
-    qv,
     keep_rows,
     seed_rows,
     base_ref,
@@ -202,7 +203,7 @@
     def hits(s, half):
         return [far + 8 * half == 4 + (a - 1) * s for a in range(3)]
 
-    def build(target, weight, s, mirrored):
+    def build(target, weight, s, mirrored, by_tap=False):
         masks = [hits(s, half) for half in range(2)]
         for b in range(3):
             grown = []
@@ -220,10 +221,10 @@
                         jnp.broadcast_to(grown[a][:, None, :], (K, 8, BLK)),
                         whole,
                     )
-                at = (half * 3 + b) * BLK
+                at = (b * 2 + half if by_tap else half * 3 + b) * BLK
                 target[:, at : at + BLK] = whole.reshape(BLK, BLK).astype(bf16)
 
-    build(t1, w1_ref, s1, False)
+    build(t1, w1_ref, s1, False, True)
     build(t2, w2_ref, s2, False)
     build(t2m, w2_ref, s2, True)
 
@@ -242,7 +243,24 @@
         every[32 * t : 32 * t + 32, COLS:] = halo
     weight = pltpu.roll(wc_ref[...].astype(f32), lax.rem(256 - 64 * turn, 256), 1).astype(bf16)
     q = dot(weight, every[...])
-    qv[...] = q
+    place_of = jnp.where(iota((1, WIDE), 1) < COLS, 0, jnp.where(iota((1, WIDE), 1) < 576, 1, 2))
+    tile_of = [(place_of == m).astype(f32) for m in range(3)]
+    ones = jnp.zeros((K, WIDE), f32)
+    for m in range(3):
+        row = iota((K, WIDE), 0)
+        ones = jnp.where(jnp.logical_or(row == m, row == m + 3), tile_of[m], ones)
+    q_rest = q - q.astype(bf16).astype(f32)
+    for b, move in enumerate((behind, lambda x, s: x, ahead)):
+        moved = move(q, s1)
+        flags = move(ones, s1)
+        for m in range(3):
+            at = 128 * b + K * m
+            xv[at : at + K, :] = (moved * flags[m : m + 1]).astype(bf16)
+        xv[128 * b + 96 : 128 * b + 128, :] = flags.astype(bf16)
+        xv[384 + K * b : 384 + K * b + K, :] = (move(q_rest, s1) * flags[0:1]).astype(bf16)
+        xv[512 + K * b : 512 + K * b + K, :] = xv[128 * b : 128 * b + K, :]
+    xv[480:512, :] = jnp.zeros((K, WIDE), bf16)
+    xv[608:640, :] = jnp.zeros((K, WIDE), bf16)
 
     bands = bands_ref[...].astype(f32)[:, 0:8, :].reshape(256, 128).astype(bf16)
     row_t = dot(wr_ref[...], bands)
@@ -319,17 +337,40 @@
             at = pl.multiple_of(block * 3 * BLK + b * BLK + 16 * p, 16)
             target[pl.ds(at, 16), :] = moved
 
-    def pair_block(k, carry):
-        rows = row3[pl.ds(pl.multiple_of(8 * k, 8), 8), :]
+    lane_m = jnp.where(lane128 < 96, lane128 // K, lane128 - 96)
+    for k in range(6):
+        rows = row3[8 * k : 8 * k + 8, :]
         keep = keep_rows[k // 2]
+        keep = jnp.where(
+            lane_m == 0,
+            keep[:, 0:1],
+            jnp.where(lane_m == 1, keep[:, COLS : COLS + 1], keep[:, WIDE - 1 : WIDE]),
+        )
+        keep = jnp.where(lane_m < 3, keep, 0.0)
         for p in range(K // 2):
             parts = []
             for ch in (2 * p, 2 * p + 1):
-                parts.append(keep * (rows[:, ch : ch + 1] + qv[ch : ch + 1, :]))
-            store_shifted(pv, k, p, jnp.concatenate(parts, axis=0), s1)
-        return carry
-
-    lax.fori_loop(0, 6, pair_block, 0)
+                picked = jnp.where(lane128 % K == ch, keep, 0.0)
+                parts.append(jnp.where(lane128 < 96, picked, keep * rows[:, ch : ch + 1]))
+            at = k * BLK + 16 * p
+            zv[at : at + 16, :] = jnp.concatenate(parts, axis=0).astype(bf16)
+    for k in (0, 2, 4):
+        both = zv[k * BLK : (k + 2) * BLK, :]
+        if k < 4:
+            both = jnp.concatenate([both, zv[(k + 1) * BLK : (k + 3) * BLK, :]], axis=1)
+        taps = [dot(t1[:, 2 * BLK * b : 2 * BLK * (b + 1)], both) for b in range(3)]
+        for i in range(2 if k < 4 else 1):
+            own_tile = jnp.zeros((BLK, 128), f32)
+            for b in range(3):
+                found = taps[b][:, 128 * i : 128 * i + 128]
+                rest = found - found.astype(bf16).astype(f32)
+                rest = jnp.where(jnp.logical_and(lane128 >= 99, lane128 < 102), pltpu.roll(rest, 3, 1), found)
+                gk[k + i, :, 128 * b : 128 * b + 128] = rest.astype(bf16)
+                here = jnp.logical_and(lane128 >= K * b, lane128 < K * b + K)
+                own_tile = jnp.where(here, pltpu.roll(found, K * b, 1) if b else found, own_tile)
+            rounded = own_tile.astype(bf16)
+            gk[k + i, :, 384:512] = rounded
+            gk[k + i, :, 512:640] = (own_tile - rounded.astype(f32)).astype(bf16)
 
     def convolve(k, weight, values, to):
         acc[to] = dot(weight[...], values[k * 3 * BLK : (k + 2) * 3 * BLK, :])
@@ -383,7 +424,10 @@
             acc[at_acc] * d1[k * BLK : (k + 1) * BLK, :]
         ).astype(bf16)
 
-    jobs = [(convolve, k, t1, pv, functools.partial(hidden_block, k)) for k in range(5)]
+    def convolve_first(k, weight, values, to):
+        acc[to] = dot(weight[k], values[...])
+
+    jobs = [(convolve_first, k, gk, xv, functools.partial(hidden_block, k)) for k in range(5)]
     jobs += [(convolve, k, t2, hv, functools.partial(grad_block, k)) for k in range(4)]
     jobs += [(convolve, k, t2m, gv, functools.partial(back_block, k)) for k in range(3)]
     for i, (start, k, weight, values, _) in enumerate(jobs):
@@ -605,7 +649,9 @@
             pltpu.VMEM((BLK, 6 * BLK), bf16),
             pltpu.VMEM((BLK, 6 * BLK), bf16),
             pltpu.VMEM((BLK, 6 * BLK), bf16),
-            pltpu.VMEM((18 * BLK, WIDE), bf16),
+            pltpu.VMEM((6 * BLK, 128), bf16),
+            pltpu.VMEM((5, BLK, 640), bf16),
+            pltpu.VMEM((640, WIDE), bf16),
             pltpu.VMEM((15 * BLK, WIDE), bf16),
             pltpu.VMEM((12 * BLK, WIDE), bf16),
             pltpu.VMEM((3 * BLK, WIDE), bf16),
@@ -614,7 +660,6 @@
             pltpu.VMEM((BLK, COLS), f32),
             pltpu.VMEM((128, K), f32),
             pltpu.VMEM((48, K), f32),
-            pltpu.VMEM((K, WIDE), f32),
             pltpu.VMEM((3, 1, WIDE), f32),
             pltpu.VMEM((3, 1, WIDE), jnp.int32),
             pltpu.VMEM((8, WIDE), jnp.int32),

time: 105 us -> 99.1 us (0.944)
  Pallas kernels: 25.8 us -> 20 us
    pallas_call x5, Pallas kernels: 25.8 us -> 20 us  [call(): pl.pallas_call(kernel, out_shape=shapes, in_specs=[pl.BlockSpec(memory_sp...]
where the time goes in v4:
time: 99.1 us; the launch traced here: 98.6 us
  starting transfers between devices  45.4 us (46%)
  waiting for transfers between devices  27.8 us (28%)
  Pallas kernels  20 us (20%)
  local copies, waits for them, and re-layouts  3.17 us (3%)
  between operations  2.07 us (2%)
    pallas_call x5, Pallas kernels, call(): pl.pallas_call(kernel, out_shape=shapes, in_specs=[pl.BlockSpec(memory_sp...  20 us
    ppermute x9, waiting for transfers between devices, quarters(): lax.ppermute(x, axis, [(i, turned(i, s)) for i in range(count)])  17.5 us
    ppermute x9, starting transfers between devices, quarters(): lax.ppermute(x, axis, [(i, turned(i, s)) for i in range(count)])  16.1 us
    ppermute x3, starting transfers between devices, per_device(): lax.ppermute(own, 'row', [((i + 2 * s) % rows, i) for i in range(rows)])  11.4 us
    all_to_all x1, starting transfers between devices, per_device(): bands = lax.all_to_all(bands, 'col', 0, 0)  7.7 us
    ppermute x3, waiting for transfers between devices, per_device(): lax.ppermute(own, 'row', [((i + 2 * s) % rows, i) for i in range(rows)])  4.27 us
    ppermute x1, starting transfers between devices, per_device(): outer = lax.ppermute(outer, 'row', pairs).reshape(BLK, COLS)  3.55 us
    unnamed x18, local copies, waits for them, and re-layouts  3.13 us
  transfers between devices with their start and end apart: 20, of which 13 were waited for; matrix products, arithmetic and copies ran while one was open for 0% of the time, Pallas kernels for 1%

profile of v4, /device:TPU:6, one launch (start us, length us, event | category | flops | bytes accessed | tf_op | source)
XLA Modules:
  0.0 98.6 jit_solution(10527970433703352063)
XLA Ops:
  1.9 0.7 copy-done.7
  2.6 1.0 %copy-done = bf16[32,16,512]{2,1,0:T(8,128)(2,1)S(1)} copy-done((bf16[32,16,512]{2,1,0:T(8,128)(2,1)S(1)}, bf16[32,16,512]{2,1,0:T(8,128)(2,1)}, u32[]{:S(2)}) %copy-start) | copy-done | bytes 524312
  3.7 0.8 copy-done.6
  4.6 3.3 %collective-permute-start.2 = (bf16[64,512]{1,0:T(8,128)(2,1)S(1)}, bf16[64,512]{1,0:T(8,128)(2,1)S(1)}, u32[]{:S(2)}, u32[]{:S(2)}) collective-permute-start(bf16[64,512]{1,0:T(8,128)(2,1)S(1)} %shard_map.153.own_ref), channel_id=1, source_target_pairs={{192,0},{224,32},{0,64},{32,96},{64,128},{96,160},{128,192},{160,2... | collective-permute-start | bytes 196616 | tf_op jit(solution)/shard_map/ppermute | solution.py:600
  7.9 5.4 %collective-permute-start.1 = (bf16[64,512]{1,0:T(8,128)(2,1)S(1)}, bf16[64,512]{1,0:T(8,128)(2,1)S(1)}, u32[]{:S(2)}, u32[]{:S(2)}) collective-permute-start(bf16[64,512]{1,0:T(8,128)(2,1)S(1)} %shard_map.153.own_ref), channel_id=1, source_target_pairs={{128,0},{160,32},{192,64},{224,96},{0,128},{32,160},{64,192},{96,2... | collective-permute-start | bytes 196616 | tf_op jit(solution)/shard_map/ppermute | solution.py:600
  13.3 2.7 %collective-permute-start = (bf16[64,512]{1,0:T(8,128)(2,1)S(1)}, bf16[64,512]{1,0:T(8,128)(2,1)S(1)}, u32[]{:S(2)}, u32[]{:S(2)}) collective-permute-start(bf16[64,512]{1,0:T(8,128)(2,1)S(1)} %shard_map.153.own_ref), channel_id=1, source_target_pairs={{64,0},{96,32},{128,64},{160,96},{192,128},{224,160},{0,192},{32,2... | collective-permute-start | bytes 196616 | tf_op jit(solution)/shard_map/ppermute | solution.py:600
  16.0 1.5 %collective-permute-done.1.two_ref = bf16[64,512]{1,0:T(8,128)(2,1)S(1)} collective-permute-done((bf16[64,512]{1,0:T(8,128)(2,1)S(1)}, bf16[64,512]{1,0:T(8,128)(2,1)S(1)}, u32[]{:S(2)}, u32[]{:S(2)}) %collective-permute-start.1) | collective-permute-done | bytes 65568 | tf_op jit(solution)/shard_map/ppermute | solution.py:600
  17.4 2.8 %collective-permute-done.one_ref = bf16[64,512]{1,0:T(8,128)(2,1)S(1)} collective-permute-done((bf16[64,512]{1,0:T(8,128)(2,1)S(1)}, bf16[64,512]{1,0:T(8,128)(2,1)S(1)}, u32[]{:S(2)}, u32[]{:S(2)}) %collective-permute-start) | collective-permute-done | bytes 65568 | tf_op jit(solution)/shard_map/ppermute | solution.py:600
  20.4 3.5 %collective-permute-start.7 = (bf16[32,8,512]{2,1,0:T(8,128)(2,1)S(1)}, bf16[32,8,512]{2,1,0:T(8,128)(2,1)S(1)}, u32[]{:S(2)}, u32[]{:S(2)}) collective-permute-start(bf16[32,8,512]{2,1,0:T(8,128)(2,1)S(1)} %get-tuple-element.33), channel_id=1, source_target_pairs={{0,224},{32,64},{64,32},{96,128},{128,96},{160,192},{192,160},{224... | collective-permute-start | bytes 786440 | tf_op jit(solution)/shard_map/ppermute | solution.py:626
  24.0 0.8 shard_map.154
  24.8 7.7 %all-to-all-start = ((bf16[32,16,128]{2,1,0:T(8,128)(2,1)}), bf16[32,16,128]{2,1,0:T(8,128)(2,1)S(1)}, u32[]{:S(2)}, u32[]{:S(2)}) async-start(bf16[32,16,128]{2,1,0:T(8,128)(2,1)} %get-tuple-element.21), calls=%async_computation | async-start | bytes 262144 | tf_op jit(solution)/shard_map/all_to_all | solution.py:619
  32.5 1.5 %collective-permute-start.5 = (bf16[112,128]{1,0:T(8,128)(2,1)S(1)}, bf16[112,128]{1,0:T(8,128)(2,1)S(1)}, u32[]{:S(2)}, u32[]{:S(2)}) collective-permute-start(bf16[112,128]{1,0:T(8,128)(2,1)S(1)} %get-tuple-element.23), channel_id=1, source_target_pairs={{0,1},{1,2},{2,3},{3,4},{4,5},{5,6},{6,7},{7,8},{8,9},{9,10},{10,1... | collective-permute-start | bytes 86024 | tf_op jit(solution)/shard_map/ppermute | solution.py:618
  34.0 2.7 %collective-permute-start.4 = (bf16[112,128]{1,0:T(8,128)(2,1)S(1)}, bf16[112,128]{1,0:T(8,128)(2,1)S(1)}, u32[]{:S(2)}, u32[]{:S(2)}) collective-permute-start(bf16[112,128]{1,0:T(8,128)(2,1)S(1)} %get-tuple-element.22.own_ref), channel_id=1, source_target_pairs={{1,0},{2,1},{3,2},{4,3},{5,4},{6,5},{7,6},{8,7},{9,8},{10,9},{11,1... | collective-permute-start | bytes 86024 | tf_op jit(solution)/shard_map/ppermute | solution.py:617
  36.7 2.1 %collective-permute-done.5.left_ref = bf16[112,128]{1,0:T(8,128)(2,1)S(1)} collective-permute-done((bf16[112,128]{1,0:T(8,128)(2,1)S(1)}, bf16[112,128]{1,0:T(8,128)(2,1)S(1)}, u32[]{:S(2)}, u32[]{:S(2)}) %collective-permute-start.5) | collective-permute-done | bytes 28704 | tf_op jit(solution)/shard_map/ppermute | solution.py:618
  39.3 0.6 copy-done.8
  39.9 16.7 %shard_map.155 = (bf16[32,16,512]{2,1,0:T(8,128)(2,1)}, bf16[304,128]{1,0:T(8,128)(2,1)S(1)}) custom-call(s32[2]{0:T(128)S(1)} %copy-done.8, bf16[8,32,512]{2,1,0:T(8,128)(2,1)S(1)} %get-tuple-element.20.feats_ref, bf16[32,16,128]{2,1,0:T(8,128)(2,1)S(1)} %all-to-all-done.bands_ref, bf16[112,128]{1,0:T(8,128)(2,1)S(1)} %get-tuple-element.22.own_ref, ...), custom_call_target="tpu_custom_call" | custom-call | tf_op jit(solution)/shard_map/pallas_call | solution.py:562
  56.7 1.3 %collective-permute-done.8 = bf16[304,128]{1,0:T(8,128)(2,1)S(1)} collective-permute-done((bf16[304,128]{1,0:T(8,128)(2,1)S(1)}, bf16[304,128]{1,0:T(8,128)(2,1)S(1)}, u32[]{:S(2)}, u32[]{:S(2)}) %collective-permute-start.8) | collective-permute-done | bytes 77856 | tf_op jit(solution)/shard_map/ppermute | solution.py:684
  58.0 1.4 %collective-permute-start.11 = (bf16[304,128]{1,0:T(8,128)(2,1)S(1)}, bf16[304,128]{1,0:T(8,128)(2,1)S(1)}, u32[]{:S(2)}, u32[]{:S(2)}) collective-permute-start(bf16[304,128]{1,0:T(8,128)(2,1)S(1)} %add_convert_fusion.own_ref), channel_id=1, source_target_pairs={{0,192},{32,224},{64,0},{96,32},{128,64},{160,96},{192,128},{224,1... | collective-permute-start | bytes 233480 | tf_op jit(solution)/shard_map/ppermute | solution.py:681
  59.3 3.4 %collective-permute-start.10 = (bf16[304,128]{1,0:T(8,128)(2,1)S(1)}, bf16[304,128]{1,0:T(8,128)(2,1)S(1)}, u32[]{:S(2)}, u32[]{:S(2)}) collective-permute-start(bf16[304,128]{1,0:T(8,128)(2,1)S(1)} %add_convert_fusion.own_ref), channel_id=1, source_target_pairs={{0,128},{32,160},{64,192},{96,224},{128,0},{160,32},{192,64},{224,... | collective-permute-start | bytes 233480 | tf_op jit(solution)/shard_map/ppermute | solution.py:681
  62.7 0.7 collective-permute-start.9
  63.4 3.1 %collective-permute-done.11.c_ref = bf16[304,128]{1,0:T(8,128)(2,1)S(1)} collective-permute-done((bf16[304,128]{1,0:T(8,128)(2,1)S(1)}, bf16[304,128]{1,0:T(8,128)(2,1)S(1)}, u32[]{:S(2)}, u32[]{:S(2)}) %collective-permute-start.11) | collective-permute-done | bytes 77856 | tf_op jit(solution)/shard_map/ppermute | solution.py:681
  66.5 3.8 %collective-permute-done.10.b_ref = bf16[304,128]{1,0:T(8,128)(2,1)S(1)} collective-permute-done((bf16[304,128]{1,0:T(8,128)(2,1)S(1)}, bf16[304,128]{1,0:T(8,128)(2,1)S(1)}, u32[]{:S(2)}, u32[]{:S(2)}) %collective-permute-start.10) | collective-permute-done | bytes 77856 | tf_op jit(solution)/shard_map/ppermute | solution.py:681
  70.6 1.4 %shard_map.156 = (bf16[32,512]{1,0:T(8,128)(2,1)}, bf16[240,128]{1,0:T(8,128)(2,1)S(1)}) custom-call(bf16[304,128]{1,0:T(8,128)(2,1)S(1)} %add_convert_fusion.own_ref, bf16[304,128]{1,0:T(8,128)(2,1)S(1)} %collective-permute-done.9.a_ref, bf16[304,128]{1,0:T(8,128)(2,1)S(1)} %collective-permute-done.10.b_ref, ...), custom_call_target="tpu_custom_call" | custom-call | tf_op jit(solution)/shard_map/pallas_call | solution.py:562
  72.0 5.9 %collective-permute-start.14 = (bf16[240,128]{1,0:T(8,128)(2,1)S(1)}, bf16[240,128]{1,0:T(8,128)(2,1)S(1)}, u32[]{:S(2)}, u32[]{:S(2)}) collective-permute-start(bf16[240,128]{1,0:T(8,128)(2,1)S(1)} %get-tuple-element.26), channel_id=1, source_target_pairs={{0,3},{1,0},{2,1},{3,2},{4,7},{5,4},{6,5},{7,6},{8,11},{9,8},{10,9... | collective-permute-start | bytes 184328 | tf_op jit(solution)/shard_map/ppermute | solution.py:681
  77.9 1.5 %collective-permute-start.12 = (bf16[240,128]{1,0:T(8,128)(2,1)S(1)}, bf16[240,128]{1,0:T(8,128)(2,1)S(1)}, u32[]{:S(2)}, u32[]{:S(2)}) collective-permute-start(bf16[240,128]{1,0:T(8,128)(2,1)S(1)} %get-tuple-element.26), channel_id=1, source_target_pairs={{0,2},{1,3},{2,0},{3,1},{4,6},{5,7},{6,4},{7,5},{8,10},{9,11},{10,... | collective-permute-start | bytes 184328 | tf_op jit(solution)/shard_map/ppermute | solution.py:681
  79.8 4.2 %collective-permute-done.13 = bf16[240,128]{1,0:T(8,128)(2,1)S(1)} collective-permute-done((bf16[240,128]{1,0:T(8,128)(2,1)S(1)}, bf16[240,128]{1,0:T(8,128)(2,1)S(1)}, u32[]{:S(2)}, u32[]{:S(2)}) %collective-permute-start.13) | collective-permute-done | bytes 61472 | tf_op jit(solution)/shard_map/ppermute | solution.py:681
  84.1 3.2 %collective-permute-start.16 = (bf16[240,128]{1,0:T(8,128)(2,1)S(1)}, bf16[240,128]{1,0:T(8,128)(2,1)S(1)}, u32[]{:S(2)}, u32[]{:S(2)}) collective-permute-start(bf16[240,128]{1,0:T(8,128)(2,1)S(1)} %add_convert_fusion.2), channel_id=1, source_target_pairs={{0,4},{1,5},{2,6},{3,7},{4,8},{5,9},{6,10},{7,11},{8,12},{9,13},{1... | collective-permute-start | bytes 184328 | tf_op jit(solution)/shard_map/ppermute | solution.py:681
  87.4 2.9 %collective-permute-done.17 = bf16[240,128]{1,0:T(8,128)(2,1)S(1)} collective-permute-done((bf16[240,128]{1,0:T(8,128)(2,1)S(1)}, bf16[240,128]{1,0:T(8,128)(2,1)S(1)}, u32[]{:S(2)}, u32[]{:S(2)}) %collective-permute-start.17) | collective-permute-done | bytes 61472 | tf_op jit(solution)/shard_map/ppermute | solution.py:681
  90.2 2.9 %collective-permute-done.15 = bf16[240,128]{1,0:T(8,128)(2,1)S(1)} collective-permute-done((bf16[240,128]{1,0:T(8,128)(2,1)S(1)}, bf16[240,128]{1,0:T(8,128)(2,1)S(1)}, u32[]{:S(2)}, u32[]{:S(2)}) %collective-permute-start.15) | collective-permute-done | bytes 61472 | tf_op jit(solution)/shard_map/ppermute | solution.py:681
  93.1 2.3 %collective-permute-start.18 = (bf16[240,128]{1,0:T(8,128)(2,1)S(1)}, bf16[240,128]{1,0:T(8,128)(2,1)S(1)}, u32[]{:S(2)}, u32[]{:S(2)}) collective-permute-start(bf16[240,128]{1,0:T(8,128)(2,1)S(1)} %add_convert_fusion.1.own_ref), channel_id=1, source_target_pairs={{0,16},{1,17},{2,18},{3,19},{4,20},{5,21},{6,22},{7,23},{8,24},{9,... | collective-permute-start | bytes 184328 | tf_op jit(solution)/shard_map/ppermute | solution.py:705
  95.4 2.2 %collective-permute-done.18.a_ref = bf16[240,128]{1,0:T(8,128)(2,1)S(1)} collective-permute-done((bf16[240,128]{1,0:T(8,128)(2,1)S(1)}, bf16[240,128]{1,0:T(8,128)(2,1)S(1)}, u32[]{:S(2)}, u32[]{:S(2)}) %collective-permute-start.18) | collective-permute-done | bytes 61472 | tf_op jit(solution)/shard_map/ppermute | solution.py:705
  97.6 1.0 %shard_map.157 = (bf16[8,16]{1,0:T(8,128)(2,1)}, f32[32,256]{1,0:T(8,128)}, f32[32,256]{1,0:T(8,128)}, f32[9,32,32]{2,1,0:T(8,128)}, f32[9,32,32]{2,1,0:T(8,128)}) custom-call(bf16[240,128]{1,0:T(8,128)(2,1)S(1)} %add_convert_fusion.1.own_ref, bf16[240,128]{1,0:T(8,128)(2,1)S(1)} %collective-permute-done.18.a_ref, ...), custom_call_target="tpu_custom_call" | custom-call | tf_op jit(solution)/shard_map/pallas_call | solution.py:562
  (36 shorter events, 1.8 us)
Async XLA Ops:
  1.9 0.7 copy-start.7
  2.6 1.0 %copy-start = (bf16[32,16,512]{2,1,0:T(8,128)(2,1)S(1)}, bf16[32,16,512]{2,1,0:T(8,128)(2,1)}, u32[]{:S(2)}) copy-start(bf16[32,16,512]{2,1,0:T(8,128)(2,1)} %cot_ref.3) | copy-start | bytes 1572868
  3.6 0.8 copy-start.6
  4.4 16.0 %copy-start.1 = (bf16[32,16,512]{2,1,0:T(8,128)(2,1)S(1)}, bf16[32,16,512]{2,1,0:T(8,128)(2,1)}, u32[]{:S(2)}) copy-start(bf16[32,16,512]{2,1,0:T(8,128)(2,1)} %cot_ref.3) | copy-start | bytes 1572868
  4.6 11.4 %collective-permute-start.2 = (bf16[64,512]{1,0:T(8,128)(2,1)S(1)}, bf16[64,512]{1,0:T(8,128)(2,1)S(1)}, u32[]{:S(2)}, u32[]{:S(2)}) collective-permute-start(bf16[64,512]{1,0:T(8,128)(2,1)S(1)} %shard_map.153.own_ref), channel_id=1, source_target_pairs={{192,0},{224,32},{0,64},{32,96},{64,128},{96,160},{128,192},{160,2... | collective-permute-start | bytes 196616 | tf_op jit(solution)/shard_map/ppermute | solution.py:600
  7.9 9.5 %collective-permute-start.1 = (bf16[64,512]{1,0:T(8,128)(2,1)S(1)}, bf16[64,512]{1,0:T(8,128)(2,1)S(1)}, u32[]{:S(2)}, u32[]{:S(2)}) collective-permute-start(bf16[64,512]{1,0:T(8,128)(2,1)S(1)} %shard_map.153.own_ref), channel_id=1, source_target_pairs={{128,0},{160,32},{192,64},{224,96},{0,128},{32,160},{64,192},{96,2... | collective-permute-start | bytes 196616 | tf_op jit(solution)/shard_map/ppermute | solution.py:600
  13.3 6.9 %collective-permute-start = (bf16[64,512]{1,0:T(8,128)(2,1)S(1)}, bf16[64,512]{1,0:T(8,128)(2,1)S(1)}, u32[]{:S(2)}, u32[]{:S(2)}) collective-permute-start(bf16[64,512]{1,0:T(8,128)(2,1)S(1)} %shard_map.153.own_ref), channel_id=1, source_target_pairs={{64,0},{96,32},{128,64},{160,96},{192,128},{224,160},{0,192},{32,2... | collective-permute-start | bytes 196616 | tf_op jit(solution)/shard_map/ppermute | solution.py:600
  20.3 3.7 %collective-permute-start.3 = (bf16[4,64,512]{2,1,0:T(8,128)(2,1)S(1)}, bf16[4,64,512]{2,1,0:T(8,128)(2,1)S(1)}, u32[]{:S(2)}, u32[]{:S(2)}) collective-permute-start(bf16[4,64,512]{2,1,0:T(8,128)(2,1)S(1)} %pad_maximum_fusion), channel_id=1, source_target_pairs={{0,32},{32,0},{64,96},{96,64},{128,160},{160,128},{192,224},{224,1... | collective-permute-start | bytes 786440 | tf_op jit(solution)/shard_map/ppermute | solution.py:603
  20.4 16.3 %collective-permute-start.7 = (bf16[32,8,512]{2,1,0:T(8,128)(2,1)S(1)}, bf16[32,8,512]{2,1,0:T(8,128)(2,1)S(1)}, u32[]{:S(2)}, u32[]{:S(2)}) collective-permute-start(bf16[32,8,512]{2,1,0:T(8,128)(2,1)S(1)} %get-tuple-element.33), channel_id=1, source_target_pairs={{0,224},{32,64},{64,32},{96,128},{128,96},{160,192},{192,160},{224... | collective-permute-start | bytes 786440 | tf_op jit(solution)/shard_map/ppermute | solution.py:626
  24.0 12.7 %collective-permute-start.6 = (bf16[32,8,512]{2,1,0:T(8,128)(2,1)S(1)}, bf16[32,8,512]{2,1,0:T(8,128)(2,1)S(1)}, u32[]{:S(2)}, u32[]{:S(2)}) collective-permute-start(bf16[32,8,512]{2,1,0:T(8,128)(2,1)S(1)} %get-tuple-element.34), channel_id=1, source_target_pairs={{0,32},{32,0},{64,96},{96,64},{128,160},{160,128},{192,224},{224,1... | collective-permute-start | bytes 786440 | tf_op jit(solution)/shard_map/ppermute | solution.py:625
  24.8 14.5 %copy-start.2 = (bf16[32,32,3,3]{1,0,3,2:T(8,128)(2,1)S(1)}, bf16[32,32,3,3]{1,0,3,2:T(8,128)(2,1)}, u32[]{:S(2)}) copy-start(bf16[32,32,3,3]{1,0,3,2:T(8,128)(2,1)} %param.14) | copy-start | bytes 55300
  24.8 14.5 %copy-start.3 = (bf16[32,32,3,3]{1,0,3,2:T(8,128)(2,1)S(1)}, bf16[32,32,3,3]{1,0,3,2:T(8,128)(2,1)}, u32[]{:S(2)}) copy-start(bf16[32,32,3,3]{1,0,3,2:T(8,128)(2,1)} %param.15) | copy-start | bytes 55300
  24.8 14.5 %copy-start.5 = (bf16[256,32]{0,1:T(8,128)(2,1)S(1)}, bf16[256,32]{0,1:T(8,128)(2,1)}, u32[]{:S(2)}) copy-start(bf16[256,32]{0,1:T(8,128)(2,1)} %param.12) | copy-start | bytes 49156
  24.8 14.5 %all-to-all-start = ((bf16[32,16,128]{2,1,0:T(8,128)(2,1)}), bf16[32,16,128]{2,1,0:T(8,128)(2,1)S(1)}, u32[]{:S(2)}, u32[]{:S(2)}) async-start(bf16[32,16,128]{2,1,0:T(8,128)(2,1)} %get-tuple-element.21), calls=%async_computation | async-start | bytes 262144 | tf_op jit(solution)/shard_map/all_to_all | solution.py:619
  32.5 6.8 %copy-start.4 = (bf16[256,32]{0,1:T(8,128)(2,1)S(1)}, bf16[256,32]{0,1:T(8,128)(2,1)}, u32[]{:S(2)}) copy-start(bf16[256,32]{0,1:T(8,128)(2,1)} %param.13) | copy-start | bytes 49156
  32.5 6.3 %collective-permute-start.5 = (bf16[112,128]{1,0:T(8,128)(2,1)S(1)}, bf16[112,128]{1,0:T(8,128)(2,1)S(1)}, u32[]{:S(2)}, u32[]{:S(2)}) collective-permute-start(bf16[112,128]{1,0:T(8,128)(2,1)S(1)} %get-tuple-element.23), channel_id=1, source_target_pairs={{0,1},{1,2},{2,3},{3,4},{4,5},{5,6},{6,7},{7,8},{8,9},{9,10},{10,1... | collective-permute-start | bytes 86024 | tf_op jit(solution)/shard_map/ppermute | solution.py:618
  34.0 4.8 %collective-permute-start.4 = (bf16[112,128]{1,0:T(8,128)(2,1)S(1)}, bf16[112,128]{1,0:T(8,128)(2,1)S(1)}, u32[]{:S(2)}, u32[]{:S(2)}) collective-permute-start(bf16[112,128]{1,0:T(8,128)(2,1)S(1)} %get-tuple-element.22.own_ref), channel_id=1, source_target_pairs={{1,0},{2,1},{3,2},{4,3},{5,4},{6,5},{7,6},{8,7},{9,8},{10,9},{11,1... | collective-permute-start | bytes 86024 | tf_op jit(solution)/shard_map/ppermute | solution.py:617
  39.3 0.7 copy-start.8
  56.6 1.4 %collective-permute-start.8 = (bf16[304,128]{1,0:T(8,128)(2,1)S(1)}, bf16[304,128]{1,0:T(8,128)(2,1)S(1)}, u32[]{:S(2)}, u32[]{:S(2)}) collective-permute-start(bf16[304,128]{1,0:T(8,128)(2,1)S(1)} %get-tuple-element.25), channel_id=1, source_target_pairs={{0,32},{32,0},{64,96},{96,64},{128,160},{160,128},{192,224},{224,1... | collective-permute-start | bytes 233480 | tf_op jit(solution)/shard_map/ppermute | solution.py:684
  58.0 8.5 %collective-permute-start.11 = (bf16[304,128]{1,0:T(8,128)(2,1)S(1)}, bf16[304,128]{1,0:T(8,128)(2,1)S(1)}, u32[]{:S(2)}, u32[]{:S(2)}) collective-permute-start(bf16[304,128]{1,0:T(8,128)(2,1)S(1)} %add_convert_fusion.own_ref), channel_id=1, source_target_pairs={{0,192},{32,224},{64,0},{96,32},{128,64},{160,96},{192,128},{224,1... | collective-permute-start | bytes 233480 | tf_op jit(solution)/shard_map/ppermute | solution.py:681
  59.3 10.9 %collective-permute-start.10 = (bf16[304,128]{1,0:T(8,128)(2,1)S(1)}, bf16[304,128]{1,0:T(8,128)(2,1)S(1)}, u32[]{:S(2)}, u32[]{:S(2)}) collective-permute-start(bf16[304,128]{1,0:T(8,128)(2,1)S(1)} %add_convert_fusion.own_ref), channel_id=1, source_target_pairs={{0,128},{32,160},{64,192},{96,224},{128,0},{160,32},{192,64},{224,... | collective-permute-start | bytes 233480 | tf_op jit(solution)/shard_map/ppermute | solution.py:681
  62.7 7.8 %collective-permute-start.9 = (bf16[304,128]{1,0:T(8,128)(2,1)S(1)}, bf16[304,128]{1,0:T(8,128)(2,1)S(1)}, u32[]{:S(2)}, u32[]{:S(2)}) collective-permute-start(bf16[304,128]{1,0:T(8,128)(2,1)S(1)} %add_convert_fusion.own_ref), channel_id=1, source_target_pairs={{0,64},{32,96},{64,128},{96,160},{128,192},{160,224},{192,0},{224,... | collective-permute-start | bytes 233480 | tf_op jit(solution)/shard_map/ppermute | solution.py:681
  72.0 7.8 %collective-permute-start.14 = (bf16[240,128]{1,0:T(8,128)(2,1)S(1)}, bf16[240,128]{1,0:T(8,128)(2,1)S(1)}, u32[]{:S(2)}, u32[]{:S(2)}) collective-permute-start(bf16[240,128]{1,0:T(8,128)(2,1)S(1)} %get-tuple-element.26), channel_id=1, source_target_pairs={{0,3},{1,0},{2,1},{3,2},{4,7},{5,4},{6,5},{7,6},{8,11},{9,8},{10,9... | collective-permute-start | bytes 184328 | tf_op jit(solution)/shard_map/ppermute | solution.py:681
  77.9 6.1 %collective-permute-start.13 = (bf16[240,128]{1,0:T(8,128)(2,1)S(1)}, bf16[240,128]{1,0:T(8,128)(2,1)S(1)}, u32[]{:S(2)}, u32[]{:S(2)}) collective-permute-start(bf16[240,128]{1,0:T(8,128)(2,1)S(1)} %get-tuple-element.26), channel_id=1, source_target_pairs={{0,1},{1,2},{2,3},{3,0},{4,5},{5,6},{6,7},{7,4},{8,9},{9,10},{10,1... | collective-permute-start | bytes 184328 | tf_op jit(solution)/shard_map/ppermute | solution.py:681
  77.9 6.1 %collective-permute-start.12 = (bf16[240,128]{1,0:T(8,128)(2,1)S(1)}, bf16[240,128]{1,0:T(8,128)(2,1)S(1)}, u32[]{:S(2)}, u32[]{:S(2)}) collective-permute-start(bf16[240,128]{1,0:T(8,128)(2,1)S(1)} %get-tuple-element.26), channel_id=1, source_target_pairs={{0,2},{1,3},{2,0},{3,1},{4,6},{5,7},{6,4},{7,5},{8,10},{9,11},{10,... | collective-permute-start | bytes 184328 | tf_op jit(solution)/shard_map/ppermute | solution.py:681
  84.0 6.2 %collective-permute-start.17 = (bf16[240,128]{1,0:T(8,128)(2,1)S(1)}, bf16[240,128]{1,0:T(8,128)(2,1)S(1)}, u32[]{:S(2)}, u32[]{:S(2)}) collective-permute-start(bf16[240,128]{1,0:T(8,128)(2,1)S(1)} %add_convert_fusion.2), channel_id=1, source_target_pairs={{0,12},{1,13},{2,14},{3,15},{4,0},{5,1},{6,2},{7,3},{8,4},{9,5},{1... | collective-permute-start | bytes 184328 | tf_op jit(solution)/shard_map/ppermute | solution.py:681
  84.1 6.1 %collective-permute-start.16 = (bf16[240,128]{1,0:T(8,128)(2,1)S(1)}, bf16[240,128]{1,0:T(8,128)(2,1)S(1)}, u32[]{:S(2)}, u32[]{:S(2)}) collective-permute-start(bf16[240,128]{1,0:T(8,128)(2,1)S(1)} %add_convert_fusion.2), channel_id=1, source_target_pairs={{0,4},{1,5},{2,6},{3,7},{4,8},{5,9},{6,10},{7,11},{8,12},{9,13},{1... | collective-permute-start | bytes 184328 | tf_op jit(solution)/shard_map/ppermute | solution.py:681
  87.4 5.7 %collective-permute-start.15 = (bf16[240,128]{1,0:T(8,128)(2,1)S(1)}, bf16[240,128]{1,0:T(8,128)(2,1)S(1)}, u32[]{:S(2)}, u32[]{:S(2)}) collective-permute-start(bf16[240,128]{1,0:T(8,128)(2,1)S(1)} %add_convert_fusion.2), channel_id=1, source_target_pairs={{0,8},{1,9},{2,10},{3,11},{4,12},{5,13},{6,14},{7,15},{8,0},{9,1},... | collective-permute-start | bytes 184328 | tf_op jit(solution)/shard_map/ppermute | solution.py:681
  93.1 4.5 %collective-permute-start.18 = (bf16[240,128]{1,0:T(8,128)(2,1)S(1)}, bf16[240,128]{1,0:T(8,128)(2,1)S(1)}, u32[]{:S(2)}, u32[]{:S(2)}) collective-permute-start(bf16[240,128]{1,0:T(8,128)(2,1)S(1)} %add_convert_fusion.1.own_ref), channel_id=1, source_target_pairs={{0,16},{1,17},{2,18},{3,19},{4,20},{5,21},{6,22},{7,23},{8,24},{9,... | collective-permute-start | bytes 184328 | tf_op jit(solution)/shard_map/ppermute | solution.py:705

commit v5 on v4

--- a/solution.py
+++ b/solution.py
@@ -41,6 +41,22 @@
     )
 
 
+def split(x):
+    high = x.astype(bf16)
+    return high, (x - high.astype(f32)).astype(bf16)
+
+
+def fine(product, exact, x):
+    high, low = split(x)
+    return product(exact, high) + product(exact, low)
+
+
+def fine_nt(a, b):
+    a_high, a_low = split(a)
+    b_high, b_low = split(b)
+    return dot_nt(a_high, b_high) + (dot_nt(a_high, b_low) + dot_nt(a_low, b_high))
+
+
 def iota(shape, dim):
     return lax.broadcasted_iota(jnp.int32, shape, dim)
 
@@ -82,7 +98,7 @@
     return value, slope
 
 
-def first_kernel(seed_ref, mask_ref, cols_ref, band_ref, cot_ref, out_ref):
+def first_kernel(seed_ref, mask_ref, cols_ref, band_ref, cot_first_ref, cot_last_ref, out_ref):
     out_ref[0:32, :] = cols_ref[...]
     lane = iota((8, 128), 1)
     seed = seed_ref[0, 0]
@@ -94,11 +110,11 @@
     out_ref[32:48, 0:128] = jnp.concatenate([band, numbers.astype(f32)], axis=0).astype(bf16)
     out_ref[32:48, 128:] = jnp.zeros((16, COLS - 128), bf16)
     lane = iota((16, 128), 1)
-    for side, cols, shift in ((0, slice(0, 128), 0), (1, slice(COLS - 128, COLS), 8)):
+    for side, cot_ref, shift in ((0, cot_first_ref, 0), (1, cot_last_ref, 8)):
         for half in range(2):
             total = jnp.zeros((16, 128), f32)
             for i in range(16):
-                piece = cot_ref[16 * half + i, :, cols].astype(f32)
+                piece = cot_ref[16 * half + i].astype(f32)
                 turn = (8 * i + shift) % 128
                 piece = pltpu.roll(piece, turn, 1) if turn else piece
                 here = jnp.logical_and(lane >= 8 * i, lane < 8 * i + 8)
@@ -109,7 +125,7 @@
 
 def pack_kernel(
     own_ref, one_ref, two_ref, three_ref, other_ref,
-    feats_ref, west_ref, east_ref, bands_ref,
+    feats_ref, first_ref, second_ref, bands_ref,
 ):
     even = lax.rem(lax.axis_index("row"), 2) == 0
     lane = iota((32, 128), 1)
@@ -140,15 +156,16 @@
         seeds = jnp.where(here[:8], extra[8:16], seeds)
     blank = jnp.zeros((8, 128), f32)
     tail = jnp.concatenate([seeds, blank], axis=0).astype(bf16)
-    for ref, value in ((west_ref, west), (east_ref, east)):
-        ref[0:32, :] = value.astype(bf16)
-        ref[96:112, :] = tail
     around = [edges[7], edges[0], edges[1]], [edges[0], edges[1], edges[2]]
     three = [jnp.where(even, x, y) for x, y in zip(*around)]
     rows = jnp.concatenate([three[0][8:16], three[1], three[2][0:8]], axis=0).astype(bf16)
-    for ref, at in ((west_ref, 0), (east_ref, 256)):
-        ref[32:64, :] = rows[:, at : at + 128]
-        ref[64:96, :] = rows[:, at + 128 : at + 256]
+    whole = []
+    for value, at in ((west, 0), (east, 256)):
+        halves = [rows[:, at : at + 128], rows[:, at + 128 : at + 256]]
+        whole.append(jnp.concatenate([value.astype(bf16)] + halves + [tail], axis=0))
+    even_col = lax.rem(lax.axis_index("col"), 2) == 0
+    first_ref[...] = jnp.where(even_col, whole[1], whole[0])
+    second_ref[...] = jnp.where(even_col, whole[0], whole[1])
     chunk = jnp.concatenate([bands, blank], axis=0).astype(bf16)
     bands_ref[...] = jnp.broadcast_to(chunk[None], (32, 16, 128))
 
@@ -158,8 +175,8 @@
     feats_ref,
     bands_ref,
     own_ref,
-    right_ref,
-    left_ref,
+    one_ref,
+    two_ref,
     wr_ref,
     wc_ref,
     w1_ref,
@@ -195,6 +212,9 @@
     r = lax.axis_index("row")
     c = lax.axis_index("col")
     turn = r // 2
+    even_col = lax.rem(c, 2) == 0
+    right_all = jnp.where(even_col, one_ref[...], two_ref[...])
+    left_all = jnp.where(even_col, two_ref[...], one_ref[...])
 
     spread = (iota((K, BLK), 1) // 8 == iota((K, BLK), 0)).astype(f32).astype(bf16)
     sub = iota((8, BLK), 0)
@@ -229,8 +249,8 @@
     build(t2m, w2_ref, s2, True)
 
     lane = iota((K, 128), 1)
-    right = right_ref[0:32, :].astype(f32)
-    left = left_ref[0:32, :].astype(f32)
+    right = right_all[0:32].astype(f32)
+    left = left_all[0:32].astype(f32)
     for t in range(8):
         r_turn = (128 - 16 * t) % 128
         l_turn = (112 - 16 * t) % 128
@@ -277,8 +297,8 @@
             pl.ds(pl.multiple_of(16 * slot, 16), 16), :
         ]
         sides = []
-        for ref in (own_ref, right_ref, left_ref):
-            piece = ref[96:112, :].astype(f32)[0:1]
+        for edge in (own_ref[...], right_all, left_all):
+            piece = edge[96:112].astype(f32)[0:1]
             piece = pltpu.roll(piece, lax.rem(128 - 16 * slot, 128), 1)
             number = piece[:, 0:1] * 65536.0 + piece[:, 1:2] * 256.0 + piece[:, 2:3]
             sides.append((number, piece[:, 3:4]))
@@ -299,8 +319,8 @@
     lane32 = iota((32, 128), 1)
     for ch in range(K):
         first = 32 + ch // 16 * 32
-        right = right_ref[first : first + 32, :].astype(f32)
-        left = left_ref[first : first + 32, :].astype(f32)
+        right = right_all[first : first + 32].astype(f32)
+        left = left_all[first : first + 32].astype(f32)
         r_turn = (128 - 8 * ch) % 128
         l_turn = (120 - 8 * ch) % 128
         cot_halo[32 * ch : 32 * ch + 32, :] = jnp.where(
@@ -445,58 +465,54 @@
             start = (k + half) * 3 * BLK
             total = total + dot_nt(grads, hv[start : start + 3 * BLK, 0:COLS])
         crossed.append(total)
-    gather8 = (iota((3 * BLK, 96), 0) // 8 == iota((3 * BLK, 96), 1)).astype(f32)
-    masks = [hits(s2, half) for half in range(2)]
-    second_rows = []
+    gather8 = (iota((3 * BLK, 96), 0) // 8 == iota((3 * BLK, 96), 1)).astype(f32).astype(bf16)
+    offset = iota((8, 3 * BLK), 1) % 8 - iota((8, 3 * BLK), 0)
+    folded = []
     for a in range(3):
         found = jnp.zeros((K, 8, 3 * BLK), f32)
         for half in range(2):
-            m = jnp.concatenate([masks[half][a].astype(f32)] * 3, axis=1)
-            found = found + crossed[half].reshape(K, 8, 3 * BLK) * m[None]
-        second_rows.append(dot(jnp.sum(found, axis=1), gather8, HIGH))
-    second_total = jnp.concatenate(second_rows, axis=0)
-
-    place_j = iota((WIDE, 384), 0)
+            m = offset + 8 * half == 4 + (a - 1) * s2
+            found = jnp.where(
+                jnp.broadcast_to(m[None], found.shape), crossed[half].reshape(found.shape), found
+            )
+        folded.append(jnp.sum(found, axis=1))
+    folded = jnp.concatenate(folded, axis=0)
+    second_total = fine(lambda e, x: dot(x, e), gather8, folded)
+
+    place_j = iota((WIDE, 128), 0)
     place_j = jnp.where(place_j < 576, place_j, place_j - WIDE)
-    moved_j = place_j + (iota((WIDE, 384), 1) // 128 - 1) * s1
-    window = jnp.logical_and(moved_j >= 0, moved_j < COLS).astype(f32).astype(bf16)
-    by_row = dot(g1[...], window)
-    which = iota((3 * BLK, 384), 0)
-    which = which // BLK * 8 + which % 8
-    by_row = jnp.where(iota((3 * BLK, 384), 1) % 128 == which, by_row, 0.0)
-    same = (iota((K, 3 * BLK), 1) % BLK // 8 == iota((K, 3 * BLK), 0)).astype(f32)
-    by_row = dot(same, by_row, HIGH)
+    which = iota((3 * BLK, 128), 0)
+    which = iota((3 * BLK, 128), 1) == which // BLK * 8 + which % 8
+    same = (iota((K, 3 * BLK), 1) % BLK // 8 == iota((K, 3 * BLK), 0)).astype(f32).astype(bf16)
+    by_row = []
+    for b in range(3):
+        moved_j = place_j + (b - 1) * s1
+        window = jnp.logical_and(moved_j >= 0, moved_j < COLS).astype(f32).astype(bf16)
+        by_row.append(fine(dot, same, jnp.where(which, dot(g1[...], window), 0.0)))
     across = iota((96, 3 * BLK), 1)
     down = iota((96, 3 * BLK), 0)
     moved_i = across // BLK * 8 + across % 8 - 4 + (down // K - 1) * s1
     inside = jnp.logical_and(moved_i >= 0, moved_i < ROWS)
     inside = jnp.logical_and(inside, across % BLK // 8 == down % K)
     by_col = dot(inside.astype(f32).astype(bf16), g1[...])
-    by_col = [ahead(by_col, s1), by_col, behind(by_col, s1)]
+    by_col = jnp.concatenate([ahead(by_col, s1), by_col, behind(by_col, s1)], axis=0)
 
     keep_own = keep_rows[1][:, 0:1]
-
-    col_sum = jnp.zeros((K, WIDE), f32)
+    weights = [w1_ref[a * 3 + b] for b in range(3) for a in range(3)]
+    col_sum = fine(dot_tn, jnp.concatenate(weights, axis=0), by_col)
     row_sum = jnp.zeros((K, 128), f32)
-    first_cols = []
-    row_taps = []
+    turned = []
     for a in range(3):
-        seen = jnp.zeros((K, 128), f32)
-        for b in range(3):
-            seen = seen + dot_tn(
-                w1_ref[a * 3 + b].astype(f32), by_row[:, 128 * b : 128 * b + 128], HIGH
-            )
-        row_sum = row_sum + pltpu.roll(seen, 128 - (4 - (a - 1) * s1), 1)
-    for b in range(3):
-        flat = jnp.concatenate([w1_ref[a * 3 + b] for a in range(3)], axis=0).astype(f32)
-        col_sum = col_sum + dot_tn(flat, by_col[b], HIGH)
-        from_cols = dot_nt(by_col[b][:, :COLS], q[:, :COLS], HIGH)
-        from_rows = []
-        for a in range(3):
-            moved = pltpu.roll(by_row[:, 128 * b : 128 * b + 128], 128 - (4 - (a - 1) * s1), 1)
-            from_rows.append(dot_nt(moved, row_t, HIGH))
-        first_cols.append(from_cols + jnp.concatenate(from_rows, axis=0))
-    first_total = jnp.concatenate(first_cols, axis=1) * keep_own
+        turns = 128 - (4 - (a - 1) * s1)
+        flat = jnp.concatenate([w1_ref[a * 3 + b] for b in range(3)], axis=0)
+        row_sum = row_sum + pltpu.roll(
+            fine(dot_tn, flat, jnp.concatenate(by_row, axis=0)), turns, 1
+        )
+        turned.append([pltpu.roll(by_row[b], turns, 1) for b in range(3)])
+    turned = jnp.concatenate([turned[a][b] for b in range(3) for a in range(3)], axis=0)
+    first_all = fine_nt(by_col[:, :COLS], q[:, :COLS]) + fine_nt(turned, row_t)
+    first_total = jnp.concatenate([first_all[96 * b : 96 * b + 96] for b in range(3)], axis=1)
+    first_total = first_total * keep_own
     row_sum = jnp.where(lane128 < 16, row_sum * keep_own, 0.0)
     row_sum = pltpu.roll(row_sum, 16 * r, 1)
 
@@ -520,13 +536,14 @@
 ):
     r = lax.axis_index("row")
     total = four(own_ref, a_ref, b_ref, c_ref)
-    weight = pltpu.roll(wc_ref[...].astype(f32), lax.rem(256 - 32 * r, 256), 1)[:, 0:K]
+    weight = pltpu.roll(wc_ref[...].astype(f32), lax.rem(256 - 32 * r, 256), 1)
+    weight = weight[:, 0:K].astype(bf16)
     grad_w = jnp.zeros((K, 256), f32)
     for g in range(4):
         part = total[32 * g : 32 * g + 32, :]
-        gcols_ref[:, 128 * g : 128 * g + 128] = dot_tn(weight, part, HIGH).astype(bf16)
+        gcols_ref[:, 128 * g : 128 * g + 128] = fine(dot_tn, weight, part).astype(bf16)
         seen = feats_ref[:, :, 128 * g : 128 * g + 128].reshape(256, 128)
-        grad_w = grad_w + dot_nt(part, seen.astype(f32), HIGH)
+        grad_w = grad_w + fine(lambda e, x: dot_nt(x, e), seen, part)
     grad_w = pltpu.roll(grad_w, 64 * (r // 2), 1)
     send_ref[0:176, :] = total[128:304].astype(bf16)
     send_ref[176:208, :] = grad_w[:, 0:128].astype(bf16)
@@ -551,19 +568,23 @@
     gwc_ref[:, 128:256] = total[208:240]
     bands = bands_ref[...].astype(f32)[:, 0:8, :].reshape(256, 128)
     turned = pltpu.roll(rows, lax.rem(128 - 32 * (r // 2), 128), 1)
-    gwr_ref[...] = dot_nt(turned, bands, HIGH)
+    gwr_ref[...] = fine(lambda e, x: dot_nt(x, e), bands.astype(bf16), turned)
     mine = pltpu.roll(wr_ref[...].astype(f32), lax.rem(256 - 8 * c, 256), 1)[:, 0:128]
-    mine = dot_tn(mine, pltpu.roll(rows, lax.rem(128 - 16 * r, 128), 1), HIGH)
+    mine = fine(dot_tn, mine.astype(bf16), pltpu.roll(rows, lax.rem(128 - 16 * r, 128), 1))
     gband_ref[...] = mine[0:8, 0:16].astype(bf16)
 
 
-def call(kernel, shapes, args, scratch=(), scalars=0, limit=8):
+def call(kernel, shapes, args, scratch=(), scalars=0, limit=8, blocks={}):
     whole = pl.BlockSpec(memory_space=pltpu.VMEM)
+    specs = [pl.BlockSpec(memory_space=pltpu.SMEM)] * scalars
+    specs += [whole] * (len(args) - scalars)
+    for i, (dims, at) in blocks.items():
+        specs[i] = pl.BlockSpec(dims, lambda _, at=at: at)
     return pl.pallas_call(
         kernel,
         out_shape=shapes,
-        in_specs=[pl.BlockSpec(memory_space=pltpu.SMEM)] * scalars
-        + [whole] * (len(args) - scalars),
+        grid=(1,) if blocks else (),
+        in_specs=specs,
         out_specs=jax.tree.map(lambda _: whole, shapes),
         scratch_shapes=list(scratch),
         compiler_params=pltpu.CompilerParams(vmem_limit_bytes=limit * 1024 * 1024),
@@ -593,7 +614,8 @@
     own = call(
         first_kernel,
         shape((64, COLS), bf16),
-        (drop_seeds, tile_mask, cols_t, band_emb.T, cotangent),
+        (drop_seeds, tile_mask, cols_t, band_emb.T, cotangent, cotangent),
+        blocks={4: ((K, ROWS, 128), (0, 0, 0)), 5: ((K, ROWS, 128), (0, 0, COLS // 128 - 1))},
         scalars=2,
     )
     beyond = [
@@ -602,7 +624,7 @@
     flip = [(i, i ^ 1) for i in range(rows)]
     other = lax.ppermute(jnp.stack([own] + beyond), "row", flip)
 
-    feats, west_edge, east_edge, bands = call(
+    feats, edge_first, edge_second, bands = call(
         pack_kernel,
         (
             shape((8, K, COLS), bf16),
@@ -612,10 +634,10 @@
         ),
         (own, *beyond, other),
     )
-    east = [(i, (i + 1) % cols) for i in range(cols)]
-    west = [(j, i) for i, j in east]
-    right = lax.ppermute(west_edge, "col", west)
-    left = lax.ppermute(east_edge, "col", east)
+    inside = [(i, i ^ 1) for i in range(cols)]
+    between = [(i, (i + 1 if i % 2 else i - 1) % cols) for i in range(cols)]
+    edge_one = lax.ppermute(edge_first, "col", inside)
+    edge_two = lax.ppermute(edge_second, "col", between)
     bands = lax.all_to_all(bands, "col", 0, 0)
 
     core = lax.rem(lax.axis_index("row"), 2)
@@ -634,9 +656,9 @@
             dilations,
             feats,
             bands,
-            west_edge,
-            right,
-            left,
+            edge_first,
+            edge_one,
+            edge_two,
             w_row.T,
             w_col.T,
             w1,

time: 99.1 us -> 96.9 us (0.978)
  starting transfers between devices: 45.4 us -> 43.2 us
    ppermute x9, starting transfers between devices: 16.1 us -> 14.2 us  [quarters(): lax.ppermute(x, axis, [(i, turned(i, s)) for i in range(count)])]
    ppermute x2, waiting for transfers between devices: 2.1 us -> 3.86 us  [the longest x1 3.27 us: per_device(): edge_two = lax.ppermute(edge_second, 'col', between)]
    ppermute x2, starting transfers between devices: 4.21 us -> 3.06 us  [the longest x1 3.05 us: per_device(): edge_two = lax.ppermute(edge_second, 'col', between)]
  transfers between devices with their start and end apart: 20 -> 20, of which waited for: 13 -> 12; matrix products, arithmetic and copies ran while one was open for 0% -> 0% of each run, Pallas kernels for 1% -> 1%
where the time goes in v5:
time: 96.9 us; the launch traced here: 96.5 us
  starting transfers between devices  43.2 us (45%)
  waiting for transfers between devices  28.6 us (30%)
  Pallas kernels  19.3 us (20%)
  local copies, waits for them, and re-layouts  3.16 us (3%)
  between operations  2.07 us (2%)
    pallas_call x5, Pallas kernels, call(): pl.pallas_call(kernel, out_shape=shapes, grid=(1,) if blocks else (), in_...  19.3 us
    ppermute x9, waiting for transfers between devices, quarters(): lax.ppermute(x, axis, [(i, turned(i, s)) for i in range(count)])  17 us
    ppermute x9, starting transfers between devices, quarters(): lax.ppermute(x, axis, [(i, turned(i, s)) for i in range(count)])  14.2 us
    ppermute x3, starting transfers between devices, per_device(): lax.ppermute(own, 'row', [((i + 2 * s) % rows, i) for i in range(rows)])  11.4 us
    all_to_all x1, starting transfers between devices, per_device(): bands = lax.all_to_all(bands, 'col', 0, 0)  7.7 us
    ppermute x3, waiting for transfers between devices, per_device(): lax.ppermute(own, 'row', [((i + 2 * s) % rows, i) for i in range(rows)])  4.27 us
    ppermute x1, starting transfers between devices, per_device(): outer = lax.ppermute(outer, 'row', pairs).reshape(BLK, COLS)  3.55 us
    ppermute x1, waiting for transfers between devices, per_device(): edge_two = lax.ppermute(edge_second, 'col', between)  3.27 us
  transfers between devices with their start and end apart: 20, of which 12 were waited for; matrix products, arithmetic and copies ran while one was open for 0% of the time, Pallas kernels for 1%

profile of v5, /device:TPU:6, one launch (start us, length us, event | category | flops | bytes accessed | tf_op | source)
XLA Modules:
  0.0 96.5 jit_solution(2922085211208923266)
XLA Ops:
  1.9 0.7 copy-done.7
  2.6 1.0 %copy-done = bf16[32,16,512]{2,1,0:T(8,128)(2,1)S(1)} copy-done((bf16[32,16,512]{2,1,0:T(8,128)(2,1)S(1)}, bf16[32,16,512]{2,1,0:T(8,128)(2,1)}, u32[]{:S(2)}) %copy-start) | copy-done | bytes 524312
  3.7 0.8 copy-done.6
  4.6 3.3 %collective-permute-start.2 = (bf16[64,512]{1,0:T(8,128)(2,1)S(1)}, bf16[64,512]{1,0:T(8,128)(2,1)S(1)}, u32[]{:S(2)}, u32[]{:S(2)}) collective-permute-start(bf16[64,512]{1,0:T(8,128)(2,1)S(1)} %shard_map.153.own_ref), channel_id=1, source_target_pairs={{192,0},{224,32},{0,64},{32,96},{64,128},{96,160},{128,192},{160,2... | collective-permute-start | bytes 196616 | tf_op jit(solution)/shard_map/ppermute | solution.py:622
  7.9 5.4 %collective-permute-start.1 = (bf16[64,512]{1,0:T(8,128)(2,1)S(1)}, bf16[64,512]{1,0:T(8,128)(2,1)S(1)}, u32[]{:S(2)}, u32[]{:S(2)}) collective-permute-start(bf16[64,512]{1,0:T(8,128)(2,1)S(1)} %shard_map.153.own_ref), channel_id=1, source_target_pairs={{128,0},{160,32},{192,64},{224,96},{0,128},{32,160},{64,192},{96,2... | collective-permute-start | bytes 196616 | tf_op jit(solution)/shard_map/ppermute | solution.py:622
  13.3 2.7 %collective-permute-start = (bf16[64,512]{1,0:T(8,128)(2,1)S(1)}, bf16[64,512]{1,0:T(8,128)(2,1)S(1)}, u32[]{:S(2)}, u32[]{:S(2)}) collective-permute-start(bf16[64,512]{1,0:T(8,128)(2,1)S(1)} %shard_map.153.own_ref), channel_id=1, source_target_pairs={{64,0},{96,32},{128,64},{160,96},{192,128},{224,160},{0,192},{32,2... | collective-permute-start | bytes 196616 | tf_op jit(solution)/shard_map/ppermute | solution.py:622
  16.0 1.5 %collective-permute-done.1.two_ref = bf16[64,512]{1,0:T(8,128)(2,1)S(1)} collective-permute-done((bf16[64,512]{1,0:T(8,128)(2,1)S(1)}, bf16[64,512]{1,0:T(8,128)(2,1)S(1)}, u32[]{:S(2)}, u32[]{:S(2)}) %collective-permute-start.1) | collective-permute-done | bytes 65568 | tf_op jit(solution)/shard_map/ppermute | solution.py:622
  17.4 2.8 %collective-permute-done.one_ref = bf16[64,512]{1,0:T(8,128)(2,1)S(1)} collective-permute-done((bf16[64,512]{1,0:T(8,128)(2,1)S(1)}, bf16[64,512]{1,0:T(8,128)(2,1)S(1)}, u32[]{:S(2)}, u32[]{:S(2)}) %collective-permute-start) | collective-permute-done | bytes 65568 | tf_op jit(solution)/shard_map/ppermute | solution.py:622
  20.5 3.5 %collective-permute-start.7 = (bf16[32,8,512]{2,1,0:T(8,128)(2,1)S(1)}, bf16[32,8,512]{2,1,0:T(8,128)(2,1)S(1)}, u32[]{:S(2)}, u32[]{:S(2)}) collective-permute-start(bf16[32,8,512]{2,1,0:T(8,128)(2,1)S(1)} %get-tuple-element.33), channel_id=1, source_target_pairs={{0,224},{32,64},{64,32},{96,128},{128,96},{160,192},{192,160},{224... | collective-permute-start | bytes 786440 | tf_op jit(solution)/shard_map/ppermute | solution.py:648
  24.0 0.8 shard_map.154
  24.8 7.7 %all-to-all-start = ((bf16[32,16,128]{2,1,0:T(8,128)(2,1)}), bf16[32,16,128]{2,1,0:T(8,128)(2,1)S(1)}, u32[]{:S(2)}, u32[]{:S(2)}) async-start(bf16[32,16,128]{2,1,0:T(8,128)(2,1)} %get-tuple-element.21), calls=%async_computation | async-start | bytes 262144 | tf_op jit(solution)/shard_map/all_to_all | solution.py:641
  32.5 3.1 %collective-permute-start.5 = (bf16[112,128]{1,0:T(8,128)(2,1)S(1)}, bf16[112,128]{1,0:T(8,128)(2,1)S(1)}, u32[]{:S(2)}, u32[]{:S(2)}) collective-permute-start(bf16[112,128]{1,0:T(8,128)(2,1)S(1)} %get-tuple-element.23), channel_id=1, source_target_pairs={{0,31},{1,2},{2,1},{3,4},{4,3},{5,6},{6,5},{7,8},{8,7},{9,10},{10,... | collective-permute-start | bytes 86024 | tf_op jit(solution)/shard_map/ppermute | solution.py:640
  35.6 3.3 %collective-permute-done.5.two_ref = bf16[112,128]{1,0:T(8,128)(2,1)S(1)} collective-permute-done((bf16[112,128]{1,0:T(8,128)(2,1)S(1)}, bf16[112,128]{1,0:T(8,128)(2,1)S(1)}, u32[]{:S(2)}, u32[]{:S(2)}) %collective-permute-start.5) | collective-permute-done | bytes 28704 | tf_op jit(solution)/shard_map/ppermute | solution.py:640
  38.9 0.6 collective-permute-done.4.one_ref
  39.5 0.6 copy-done.8
  40.1 16.4 %shard_map.155 = (bf16[32,16,512]{2,1,0:T(8,128)(2,1)}, bf16[304,128]{1,0:T(8,128)(2,1)S(1)}) custom-call(s32[2]{0:T(128)S(1)} %copy-done.8, bf16[8,32,512]{2,1,0:T(8,128)(2,1)S(1)} %get-tuple-element.20.feats_ref, bf16[32,16,128]{2,1,0:T(8,128)(2,1)S(1)} %all-to-all-done.bands_ref, bf16[112,128]{1,0:T(8,128)(2,1)S(1)} %get-tuple-element.22.own_ref, ...), custom_call_target="tpu_custom_call" | custom-call | tf_op jit(solution)/shard_map/pallas_call | solution.py:583
  56.5 1.3 %collective-permute-done.8 = bf16[304,128]{1,0:T(8,128)(2,1)S(1)} collective-permute-done((bf16[304,128]{1,0:T(8,128)(2,1)S(1)}, bf16[304,128]{1,0:T(8,128)(2,1)S(1)}, u32[]{:S(2)}, u32[]{:S(2)}) %collective-permute-start.8) | collective-permute-done | bytes 77856 | tf_op jit(solution)/shard_map/ppermute | solution.py:706
  57.8 1.4 %collective-permute-start.11 = (bf16[304,128]{1,0:T(8,128)(2,1)S(1)}, bf16[304,128]{1,0:T(8,128)(2,1)S(1)}, u32[]{:S(2)}, u32[]{:S(2)}) collective-permute-start(bf16[304,128]{1,0:T(8,128)(2,1)S(1)} %add_convert_fusion.own_ref), channel_id=1, source_target_pairs={{0,192},{32,224},{64,0},{96,32},{128,64},{160,96},{192,128},{224,1... | collective-permute-start | bytes 233480 | tf_op jit(solution)/shard_map/ppermute | solution.py:703
  59.2 3.4 %collective-permute-start.10 = (bf16[304,128]{1,0:T(8,128)(2,1)S(1)}, bf16[304,128]{1,0:T(8,128)(2,1)S(1)}, u32[]{:S(2)}, u32[]{:S(2)}) collective-permute-start(bf16[304,128]{1,0:T(8,128)(2,1)S(1)} %add_convert_fusion.own_ref), channel_id=1, source_target_pairs={{0,128},{32,160},{64,192},{96,224},{128,0},{160,32},{192,64},{224,... | collective-permute-start | bytes 233480 | tf_op jit(solution)/shard_map/ppermute | solution.py:703
  62.6 0.7 collective-permute-start.9
  63.2 1.0 %collective-permute-done.11.c_ref = bf16[304,128]{1,0:T(8,128)(2,1)S(1)} collective-permute-done((bf16[304,128]{1,0:T(8,128)(2,1)S(1)}, bf16[304,128]{1,0:T(8,128)(2,1)S(1)}, u32[]{:S(2)}, u32[]{:S(2)}) %collective-permute-start.11) | collective-permute-done | bytes 77856 | tf_op jit(solution)/shard_map/ppermute | solution.py:703
  64.2 5.8 %collective-permute-done.10.b_ref = bf16[304,128]{1,0:T(8,128)(2,1)S(1)} collective-permute-done((bf16[304,128]{1,0:T(8,128)(2,1)S(1)}, bf16[304,128]{1,0:T(8,128)(2,1)S(1)}, u32[]{:S(2)}, u32[]{:S(2)}) %collective-permute-start.10) | collective-permute-done | bytes 77856 | tf_op jit(solution)/shard_map/ppermute | solution.py:703
  70.0 1.0 %shard_map.156 = (bf16[32,512]{1,0:T(8,128)(2,1)}, bf16[240,128]{1,0:T(8,128)(2,1)S(1)}) custom-call(bf16[304,128]{1,0:T(8,128)(2,1)S(1)} %add_convert_fusion.own_ref, bf16[304,128]{1,0:T(8,128)(2,1)S(1)} %collective-permute-done.9.a_ref, bf16[304,128]{1,0:T(8,128)(2,1)S(1)} %collective-permute-done.10.b_ref, ...), custom_call_target="tpu_custom_call" | custom-call | tf_op jit(solution)/shard_map/pallas_call | solution.py:583
  71.0 3.9 %collective-permute-start.14 = (bf16[240,128]{1,0:T(8,128)(2,1)S(1)}, bf16[240,128]{1,0:T(8,128)(2,1)S(1)}, u32[]{:S(2)}, u32[]{:S(2)}) collective-permute-start(bf16[240,128]{1,0:T(8,128)(2,1)S(1)} %get-tuple-element.26), channel_id=1, source_target_pairs={{0,3},{1,0},{2,1},{3,2},{4,7},{5,4},{6,5},{7,6},{8,11},{9,8},{10,9... | collective-permute-start | bytes 184328 | tf_op jit(solution)/shard_map/ppermute | solution.py:703
  75.0 1.5 %collective-permute-start.12 = (bf16[240,128]{1,0:T(8,128)(2,1)S(1)}, bf16[240,128]{1,0:T(8,128)(2,1)S(1)}, u32[]{:S(2)}, u32[]{:S(2)}) collective-permute-start(bf16[240,128]{1,0:T(8,128)(2,1)S(1)} %get-tuple-element.26), channel_id=1, source_target_pairs={{0,2},{1,3},{2,0},{3,1},{4,6},{5,7},{6,4},{7,5},{8,10},{9,11},{10,... | collective-permute-start | bytes 184328 | tf_op jit(solution)/shard_map/ppermute | solution.py:703
  76.8 4.2 %collective-permute-done.13 = bf16[240,128]{1,0:T(8,128)(2,1)S(1)} collective-permute-done((bf16[240,128]{1,0:T(8,128)(2,1)S(1)}, bf16[240,128]{1,0:T(8,128)(2,1)S(1)}, u32[]{:S(2)}, u32[]{:S(2)}) %collective-permute-start.13) | collective-permute-done | bytes 61472 | tf_op jit(solution)/shard_map/ppermute | solution.py:703
  81.2 3.2 %collective-permute-start.16 = (bf16[240,128]{1,0:T(8,128)(2,1)S(1)}, bf16[240,128]{1,0:T(8,128)(2,1)S(1)}, u32[]{:S(2)}, u32[]{:S(2)}) collective-permute-start(bf16[240,128]{1,0:T(8,128)(2,1)S(1)} %add_convert_fusion.2), channel_id=1, source_target_pairs={{0,4},{1,5},{2,6},{3,7},{4,8},{5,9},{6,10},{7,11},{8,12},{9,13},{1... | collective-permute-start | bytes 184328 | tf_op jit(solution)/shard_map/ppermute | solution.py:703
  84.5 2.4 %collective-permute-done.17 = bf16[240,128]{1,0:T(8,128)(2,1)S(1)} collective-permute-done((bf16[240,128]{1,0:T(8,128)(2,1)S(1)}, bf16[240,128]{1,0:T(8,128)(2,1)S(1)}, u32[]{:S(2)}, u32[]{:S(2)}) %collective-permute-start.17) | collective-permute-done | bytes 61472 | tf_op jit(solution)/shard_map/ppermute | solution.py:703
  86.9 3.2 %collective-permute-done.15 = bf16[240,128]{1,0:T(8,128)(2,1)S(1)} collective-permute-done((bf16[240,128]{1,0:T(8,128)(2,1)S(1)}, bf16[240,128]{1,0:T(8,128)(2,1)S(1)}, u32[]{:S(2)}, u32[]{:S(2)}) %collective-permute-start.15) | collective-permute-done | bytes 61472 | tf_op jit(solution)/shard_map/ppermute | solution.py:703
  90.2 3.2 %collective-permute-start.18 = (bf16[240,128]{1,0:T(8,128)(2,1)S(1)}, bf16[240,128]{1,0:T(8,128)(2,1)S(1)}, u32[]{:S(2)}, u32[]{:S(2)}) collective-permute-start(bf16[240,128]{1,0:T(8,128)(2,1)S(1)} %add_convert_fusion.1.own_ref), channel_id=1, source_target_pairs={{0,16},{1,17},{2,18},{3,19},{4,20},{5,21},{6,22},{7,23},{8,24},{9,... | collective-permute-start | bytes 184328 | tf_op jit(solution)/shard_map/ppermute | solution.py:727
  93.3 2.2 %collective-permute-done.18.a_ref = bf16[240,128]{1,0:T(8,128)(2,1)S(1)} collective-permute-done((bf16[240,128]{1,0:T(8,128)(2,1)S(1)}, bf16[240,128]{1,0:T(8,128)(2,1)S(1)}, u32[]{:S(2)}, u32[]{:S(2)}) %collective-permute-start.18) | collective-permute-done | bytes 61472 | tf_op jit(solution)/shard_map/ppermute | solution.py:727
  95.5 0.9 shard_map.157
  (36 shorter events, 1.1 us)
Async XLA Ops:
  1.9 0.7 copy-start.7
  2.6 1.0 %copy-start = (bf16[32,16,512]{2,1,0:T(8,128)(2,1)S(1)}, bf16[32,16,512]{2,1,0:T(8,128)(2,1)}, u32[]{:S(2)}) copy-start(bf16[32,16,512]{2,1,0:T(8,128)(2,1)} %cot_ref.1) | copy-start | bytes 1572868
  3.6 0.8 copy-start.6
  4.6 15.8 %copy-start.1 = (bf16[32,16,512]{2,1,0:T(8,128)(2,1)S(1)}, bf16[32,16,512]{2,1,0:T(8,128)(2,1)}, u32[]{:S(2)}) copy-start(bf16[32,16,512]{2,1,0:T(8,128)(2,1)} %cot_ref.1) | copy-start | bytes 1572868
  4.6 11.4 %collective-permute-start.2 = (bf16[64,512]{1,0:T(8,128)(2,1)S(1)}, bf16[64,512]{1,0:T(8,128)(2,1)S(1)}, u32[]{:S(2)}, u32[]{:S(2)}) collective-permute-start(bf16[64,512]{1,0:T(8,128)(2,1)S(1)} %shard_map.153.own_ref), channel_id=1, source_target_pairs={{192,0},{224,32},{0,64},{32,96},{64,128},{96,160},{128,192},{160,2... | collective-permute-start | bytes 196616 | tf_op jit(solution)/shard_map/ppermute | solution.py:622
  7.9 9.5 %collective-permute-start.1 = (bf16[64,512]{1,0:T(8,128)(2,1)S(1)}, bf16[64,512]{1,0:T(8,128)(2,1)S(1)}, u32[]{:S(2)}, u32[]{:S(2)}) collective-permute-start(bf16[64,512]{1,0:T(8,128)(2,1)S(1)} %shard_map.153.own_ref), channel_id=1, source_target_pairs={{128,0},{160,32},{192,64},{224,96},{0,128},{32,160},{64,192},{96,2... | collective-permute-start | bytes 196616 | tf_op jit(solution)/shard_map/ppermute | solution.py:622
  13.3 6.9 %collective-permute-start = (bf16[64,512]{1,0:T(8,128)(2,1)S(1)}, bf16[64,512]{1,0:T(8,128)(2,1)S(1)}, u32[]{:S(2)}, u32[]{:S(2)}) collective-permute-start(bf16[64,512]{1,0:T(8,128)(2,1)S(1)} %shard_map.153.own_ref), channel_id=1, source_target_pairs={{64,0},{96,32},{128,64},{160,96},{192,128},{224,160},{0,192},{32,2... | collective-permute-start | bytes 196616 | tf_op jit(solution)/shard_map/ppermute | solution.py:622
  20.3 3.7 %collective-permute-start.3 = (bf16[4,64,512]{2,1,0:T(8,128)(2,1)S(1)}, bf16[4,64,512]{2,1,0:T(8,128)(2,1)S(1)}, u32[]{:S(2)}, u32[]{:S(2)}) collective-permute-start(bf16[4,64,512]{2,1,0:T(8,128)(2,1)S(1)} %pad_maximum_fusion), channel_id=1, source_target_pairs={{0,32},{32,0},{64,96},{96,64},{128,160},{160,128},{192,224},{224,1... | collective-permute-start | bytes 786440 | tf_op jit(solution)/shard_map/ppermute | solution.py:625
  20.5 15.1 %collective-permute-start.7 = (bf16[32,8,512]{2,1,0:T(8,128)(2,1)S(1)}, bf16[32,8,512]{2,1,0:T(8,128)(2,1)S(1)}, u32[]{:S(2)}, u32[]{:S(2)}) collective-permute-start(bf16[32,8,512]{2,1,0:T(8,128)(2,1)S(1)} %get-tuple-element.33), channel_id=1, source_target_pairs={{0,224},{32,64},{64,32},{96,128},{128,96},{160,192},{192,160},{224... | collective-permute-start | bytes 786440 | tf_op jit(solution)/shard_map/ppermute | solution.py:648
  24.0 11.6 %collective-permute-start.6 = (bf16[32,8,512]{2,1,0:T(8,128)(2,1)S(1)}, bf16[32,8,512]{2,1,0:T(8,128)(2,1)S(1)}, u32[]{:S(2)}, u32[]{:S(2)}) collective-permute-start(bf16[32,8,512]{2,1,0:T(8,128)(2,1)S(1)} %get-tuple-element.34), channel_id=1, source_target_pairs={{0,32},{32,0},{64,96},{96,64},{128,160},{160,128},{192,224},{224,1... | collective-permute-start | bytes 786440 | tf_op jit(solution)/shard_map/ppermute | solution.py:647
  24.8 14.7 %copy-start.2 = (bf16[32,32,3,3]{1,0,3,2:T(8,128)(2,1)S(1)}, bf16[32,32,3,3]{1,0,3,2:T(8,128)(2,1)}, u32[]{:S(2)}) copy-start(bf16[32,32,3,3]{1,0,3,2:T(8,128)(2,1)} %param.14) | copy-start | bytes 55300
  24.8 14.7 %copy-start.3 = (bf16[32,32,3,3]{1,0,3,2:T(8,128)(2,1)S(1)}, bf16[32,32,3,3]{1,0,3,2:T(8,128)(2,1)}, u32[]{:S(2)}) copy-start(bf16[32,32,3,3]{1,0,3,2:T(8,128)(2,1)} %param.15) | copy-start | bytes 55300
  24.8 14.7 %copy-start.5 = (bf16[256,32]{0,1:T(8,128)(2,1)S(1)}, bf16[256,32]{0,1:T(8,128)(2,1)}, u32[]{:S(2)}) copy-start(bf16[256,32]{0,1:T(8,128)(2,1)} %param.12) | copy-start | bytes 49156
  24.8 14.6 %all-to-all-start = ((bf16[32,16,128]{2,1,0:T(8,128)(2,1)}), bf16[32,16,128]{2,1,0:T(8,128)(2,1)S(1)}, u32[]{:S(2)}, u32[]{:S(2)}) async-start(bf16[32,16,128]{2,1,0:T(8,128)(2,1)} %get-tuple-element.21), calls=%async_computation | async-start | bytes 262144 | tf_op jit(solution)/shard_map/all_to_all | solution.py:641
  32.5 7.0 %copy-start.4 = (bf16[256,32]{0,1:T(8,128)(2,1)S(1)}, bf16[256,32]{0,1:T(8,128)(2,1)}, u32[]{:S(2)}) copy-start(bf16[256,32]{0,1:T(8,128)(2,1)} %param.13) | copy-start | bytes 49156
  32.5 6.3 %collective-permute-start.5 = (bf16[112,128]{1,0:T(8,128)(2,1)S(1)}, bf16[112,128]{1,0:T(8,128)(2,1)S(1)}, u32[]{:S(2)}, u32[]{:S(2)}) collective-permute-start(bf16[112,128]{1,0:T(8,128)(2,1)S(1)} %get-tuple-element.23), channel_id=1, source_target_pairs={{0,31},{1,2},{2,1},{3,4},{4,3},{5,6},{6,5},{7,8},{8,7},{9,10},{10,... | collective-permute-start | bytes 86024 | tf_op jit(solution)/shard_map/ppermute | solution.py:640
  35.6 3.9 %collective-permute-start.4 = (bf16[112,128]{1,0:T(8,128)(2,1)S(1)}, bf16[112,128]{1,0:T(8,128)(2,1)S(1)}, u32[]{:S(2)}, u32[]{:S(2)}) collective-permute-start(bf16[112,128]{1,0:T(8,128)(2,1)S(1)} %get-tuple-element.22.own_ref), channel_id=1, source_target_pairs={{0,1},{1,0},{2,3},{3,2},{4,5},{5,4},{6,7},{7,6},{8,9},{9,8},{10,11... | collective-permute-start | bytes 86024 | tf_op jit(solution)/shard_map/ppermute | solution.py:639
  39.5 0.7 copy-start.8
  56.5 1.3 %collective-permute-start.8 = (bf16[304,128]{1,0:T(8,128)(2,1)S(1)}, bf16[304,128]{1,0:T(8,128)(2,1)S(1)}, u32[]{:S(2)}, u32[]{:S(2)}) collective-permute-start(bf16[304,128]{1,0:T(8,128)(2,1)S(1)} %get-tuple-element.25), channel_id=1, source_target_pairs={{0,32},{32,0},{64,96},{96,64},{128,160},{160,128},{192,224},{224,1... | collective-permute-start | bytes 233480 | tf_op jit(solution)/shard_map/ppermute | solution.py:706
  57.8 6.4 %collective-permute-start.11 = (bf16[304,128]{1,0:T(8,128)(2,1)S(1)}, bf16[304,128]{1,0:T(8,128)(2,1)S(1)}, u32[]{:S(2)}, u32[]{:S(2)}) collective-permute-start(bf16[304,128]{1,0:T(8,128)(2,1)S(1)} %add_convert_fusion.own_ref), channel_id=1, source_target_pairs={{0,192},{32,224},{64,0},{96,32},{128,64},{160,96},{192,128},{224,1... | collective-permute-start | bytes 233480 | tf_op jit(solution)/shard_map/ppermute | solution.py:703
  59.2 10.8 %collective-permute-start.10 = (bf16[304,128]{1,0:T(8,128)(2,1)S(1)}, bf16[304,128]{1,0:T(8,128)(2,1)S(1)}, u32[]{:S(2)}, u32[]{:S(2)}) collective-permute-start(bf16[304,128]{1,0:T(8,128)(2,1)S(1)} %add_convert_fusion.own_ref), channel_id=1, source_target_pairs={{0,128},{32,160},{64,192},{96,224},{128,0},{160,32},{192,64},{224,... | collective-permute-start | bytes 233480 | tf_op jit(solution)/shard_map/ppermute | solution.py:703
  62.6 7.4 %collective-permute-start.9 = (bf16[304,128]{1,0:T(8,128)(2,1)S(1)}, bf16[304,128]{1,0:T(8,128)(2,1)S(1)}, u32[]{:S(2)}, u32[]{:S(2)}) collective-permute-start(bf16[304,128]{1,0:T(8,128)(2,1)S(1)} %add_convert_fusion.own_ref), channel_id=1, source_target_pairs={{0,64},{32,96},{64,128},{96,160},{128,192},{160,224},{192,0},{224,... | collective-permute-start | bytes 233480 | tf_op jit(solution)/shard_map/ppermute | solution.py:703
  71.0 5.8 %collective-permute-start.14 = (bf16[240,128]{1,0:T(8,128)(2,1)S(1)}, bf16[240,128]{1,0:T(8,128)(2,1)S(1)}, u32[]{:S(2)}, u32[]{:S(2)}) collective-permute-start(bf16[240,128]{1,0:T(8,128)(2,1)S(1)} %get-tuple-element.26), channel_id=1, source_target_pairs={{0,3},{1,0},{2,1},{3,2},{4,7},{5,4},{6,5},{7,6},{8,11},{9,8},{10,9... | collective-permute-start | bytes 184328 | tf_op jit(solution)/shard_map/ppermute | solution.py:703
  74.9 6.1 %collective-permute-start.13 = (bf16[240,128]{1,0:T(8,128)(2,1)S(1)}, bf16[240,128]{1,0:T(8,128)(2,1)S(1)}, u32[]{:S(2)}, u32[]{:S(2)}) collective-permute-start(bf16[240,128]{1,0:T(8,128)(2,1)S(1)} %get-tuple-element.26), channel_id=1, source_target_pairs={{0,1},{1,2},{2,3},{3,0},{4,5},{5,6},{6,7},{7,4},{8,9},{9,10},{10,1... | collective-permute-start | bytes 184328 | tf_op jit(solution)/shard_map/ppermute | solution.py:703
  75.0 6.1 %collective-permute-start.12 = (bf16[240,128]{1,0:T(8,128)(2,1)S(1)}, bf16[240,128]{1,0:T(8,128)(2,1)S(1)}, u32[]{:S(2)}, u32[]{:S(2)}) collective-permute-start(bf16[240,128]{1,0:T(8,128)(2,1)S(1)} %get-tuple-element.26), channel_id=1, source_target_pairs={{0,2},{1,3},{2,0},{3,1},{4,6},{5,7},{6,4},{7,5},{8,10},{9,11},{10,... | collective-permute-start | bytes 184328 | tf_op jit(solution)/shard_map/ppermute | solution.py:703
  81.1 5.8 %collective-permute-start.17 = (bf16[240,128]{1,0:T(8,128)(2,1)S(1)}, bf16[240,128]{1,0:T(8,128)(2,1)S(1)}, u32[]{:S(2)}, u32[]{:S(2)}) collective-permute-start(bf16[240,128]{1,0:T(8,128)(2,1)S(1)} %add_convert_fusion.2), channel_id=1, source_target_pairs={{0,12},{1,13},{2,14},{3,15},{4,0},{5,1},{6,2},{7,3},{8,4},{9,5},{1... | collective-permute-start | bytes 184328 | tf_op jit(solution)/shard_map/ppermute | solution.py:703
  81.2 5.7 %collective-permute-start.16 = (bf16[240,128]{1,0:T(8,128)(2,1)S(1)}, bf16[240,128]{1,0:T(8,128)(2,1)S(1)}, u32[]{:S(2)}, u32[]{:S(2)}) collective-permute-start(bf16[240,128]{1,0:T(8,128)(2,1)S(1)} %add_convert_fusion.2), channel_id=1, source_target_pairs={{0,4},{1,5},{2,6},{3,7},{4,8},{5,9},{6,10},{7,11},{8,12},{9,13},{1... | collective-permute-start | bytes 184328 | tf_op jit(solution)/shard_map/ppermute | solution.py:703
  84.4 5.7 %collective-permute-start.15 = (bf16[240,128]{1,0:T(8,128)(2,1)S(1)}, bf16[240,128]{1,0:T(8,128)(2,1)S(1)}, u32[]{:S(2)}, u32[]{:S(2)}) collective-permute-start(bf16[240,128]{1,0:T(8,128)(2,1)S(1)} %add_convert_fusion.2), channel_id=1, source_target_pairs={{0,8},{1,9},{2,10},{3,11},{4,12},{5,13},{6,14},{7,15},{8,0},{9,1},... | collective-permute-start | bytes 184328 | tf_op jit(solution)/shard_map/ppermute | solution.py:703
  90.2 5.4 %collective-permute-start.18 = (bf16[240,128]{1,0:T(8,128)(2,1)S(1)}, bf16[240,128]{1,0:T(8,128)(2,1)S(1)}, u32[]{:S(2)}, u32[]{:S(2)}) collective-permute-start(bf16[240,128]{1,0:T(8,128)(2,1)S(1)} %add_convert_fusion.1.own_ref), channel_id=1, source_target_pairs={{0,16},{1,17},{2,18},{3,19},{4,20},{5,21},{6,22},{7,23},{8,24},{9,... | collective-permute-start | bytes 184328 | tf_op jit(solution)/shard_map/ppermute | solution.py:727

commit v6 on v5

--- a/solution.py
+++ b/solution.py
@@ -166,8 +166,7 @@
     even_col = lax.rem(lax.axis_index("col"), 2) == 0
     first_ref[...] = jnp.where(even_col, whole[1], whole[0])
     second_ref[...] = jnp.where(even_col, whole[0], whole[1])
-    chunk = jnp.concatenate([bands, blank], axis=0).astype(bf16)
-    bands_ref[...] = jnp.broadcast_to(chunk[None], (32, 16, 128))
+    bands_ref[...] = jnp.broadcast_to(bands.astype(bf16)[None], (32, 8, 128))
 
 
 def main_kernel(
@@ -630,7 +629,7 @@
             shape((8, K, COLS), bf16),
             shape((112, 128), bf16),
             shape((112, 128), bf16),
-            shape((32, 16, 128), bf16),
+            shape((32, 8, 128), bf16),
         ),
         (own, *beyond, other),
     )

time: 96.9 us -> 96.9 us (level)
  no operation moved by 1% of the time
where the time goes in v6:
time: 96.9 us; the launch traced here: 96.5 us
  starting transfers between devices  43.1 us (44%)
  waiting for transfers between devices  28.6 us (30%)
  Pallas kernels  19.3 us (20%)
  local copies, waits for them, and re-layouts  3.16 us (3%)
  between operations  2.08 us (2%)
    pallas_call x5, Pallas kernels, call(): pl.pallas_call(kernel, out_shape=shapes, grid=(1,) if blocks else (), in_...  19.3 us
    ppermute x9, waiting for transfers between devices, quarters(): lax.ppermute(x, axis, [(i, turned(i, s)) for i in range(count)])  17 us
    ppermute x9, starting transfers between devices, quarters(): lax.ppermute(x, axis, [(i, turned(i, s)) for i in range(count)])  14.1 us
    ppermute x3, starting transfers between devices, per_device(): lax.ppermute(own, 'row', [((i + 2 * s) % rows, i) for i in range(rows)])  11.4 us
    all_to_all x1, starting transfers between devices, per_device(): bands = lax.all_to_all(bands, 'col', 0, 0)  7.7 us
    ppermute x3, waiting for transfers between devices, per_device(): lax.ppermute(own, 'row', [((i + 2 * s) % rows, i) for i in range(rows)])  4.27 us
    ppermute x1, starting transfers between devices, per_device(): outer = lax.ppermute(outer, 'row', pairs).reshape(BLK, COLS)  3.55 us
    ppermute x1, starting transfers between devices, per_device(): lax.ppermute(terms, 'col', [(i, (i + 16) % cols) for i in range(cols)])  3.2 us
  transfers between devices with their start and end apart: 20, of which 12 were waited for; matrix products, arithmetic and copies ran while one was open for 0% of the time, Pallas kernels for 1%

profile of v6, /device:TPU:6, one launch (start us, length us, event | category | flops | bytes accessed | tf_op | source)
XLA Modules:
  0.0 96.5 jit_solution(14731034008527630495)
XLA Ops:
  1.9 0.7 copy-done.7
  2.6 1.0 %copy-done = bf16[32,16,512]{2,1,0:T(8,128)(2,1)S(1)} copy-done((bf16[32,16,512]{2,1,0:T(8,128)(2,1)S(1)}, bf16[32,16,512]{2,1,0:T(8,128)(2,1)}, u32[]{:S(2)}) %copy-start) | copy-done | bytes 524312
  3.7 0.8 copy-done.6
  4.6 3.3 %collective-permute-start.2 = (bf16[64,512]{1,0:T(8,128)(2,1)S(1)}, bf16[64,512]{1,0:T(8,128)(2,1)S(1)}, u32[]{:S(2)}, u32[]{:S(2)}) collective-permute-start(bf16[64,512]{1,0:T(8,128)(2,1)S(1)} %shard_map.153.own_ref), channel_id=1, source_target_pairs={{192,0},{224,32},{0,64},{32,96},{64,128},{96,160},{128,192},{160,2... | collective-permute-start | bytes 196616 | tf_op jit(solution)/shard_map/ppermute | solution.py:621
  7.9 5.4 %collective-permute-start.1 = (bf16[64,512]{1,0:T(8,128)(2,1)S(1)}, bf16[64,512]{1,0:T(8,128)(2,1)S(1)}, u32[]{:S(2)}, u32[]{:S(2)}) collective-permute-start(bf16[64,512]{1,0:T(8,128)(2,1)S(1)} %shard_map.153.own_ref), channel_id=1, source_target_pairs={{128,0},{160,32},{192,64},{224,96},{0,128},{32,160},{64,192},{96,2... | collective-permute-start | bytes 196616 | tf_op jit(solution)/shard_map/ppermute | solution.py:621
  13.3 2.7 %collective-permute-start = (bf16[64,512]{1,0:T(8,128)(2,1)S(1)}, bf16[64,512]{1,0:T(8,128)(2,1)S(1)}, u32[]{:S(2)}, u32[]{:S(2)}) collective-permute-start(bf16[64,512]{1,0:T(8,128)(2,1)S(1)} %shard_map.153.own_ref), channel_id=1, source_target_pairs={{64,0},{96,32},{128,64},{160,96},{192,128},{224,160},{0,192},{32,2... | collective-permute-start | bytes 196616 | tf_op jit(solution)/shard_map/ppermute | solution.py:621
  16.0 1.5 %collective-permute-done.1.two_ref = bf16[64,512]{1,0:T(8,128)(2,1)S(1)} collective-permute-done((bf16[64,512]{1,0:T(8,128)(2,1)S(1)}, bf16[64,512]{1,0:T(8,128)(2,1)S(1)}, u32[]{:S(2)}, u32[]{:S(2)}) %collective-permute-start.1) | collective-permute-done | bytes 65568 | tf_op jit(solution)/shard_map/ppermute | solution.py:621
  17.4 2.8 %collective-permute-done.one_ref = bf16[64,512]{1,0:T(8,128)(2,1)S(1)} collective-permute-done((bf16[64,512]{1,0:T(8,128)(2,1)S(1)}, bf16[64,512]{1,0:T(8,128)(2,1)S(1)}, u32[]{:S(2)}, u32[]{:S(2)}) %collective-permute-start) | collective-permute-done | bytes 65568 | tf_op jit(solution)/shard_map/ppermute | solution.py:621
  20.5 3.5 %collective-permute-start.7 = (bf16[32,8,512]{2,1,0:T(8,128)(2,1)S(1)}, bf16[32,8,512]{2,1,0:T(8,128)(2,1)S(1)}, u32[]{:S(2)}, u32[]{:S(2)}) collective-permute-start(bf16[32,8,512]{2,1,0:T(8,128)(2,1)S(1)} %get-tuple-element.33), channel_id=1, source_target_pairs={{0,224},{32,64},{64,32},{96,128},{128,96},{160,192},{192,160},{224... | collective-permute-start | bytes 786440 | tf_op jit(solution)/shard_map/ppermute | solution.py:647
  24.0 0.8 shard_map.154
  24.8 7.7 %all-to-all-start = ((bf16[32,8,128]{2,1,0:T(8,128)(2,1)}), bf16[32,8,128]{2,1,0:T(8,128)(2,1)S(1)}, u32[]{:S(2)}, u32[]{:S(2)}) async-start(bf16[32,8,128]{2,1,0:T(8,128)(2,1)} %get-tuple-element.21), calls=%async_computation | async-start | bytes 131072 | tf_op jit(solution)/shard_map/all_to_all | solution.py:640
  32.5 3.1 %collective-permute-start.5 = (bf16[112,128]{1,0:T(8,128)(2,1)S(1)}, bf16[112,128]{1,0:T(8,128)(2,1)S(1)}, u32[]{:S(2)}, u32[]{:S(2)}) collective-permute-start(bf16[112,128]{1,0:T(8,128)(2,1)S(1)} %get-tuple-element.23), channel_id=1, source_target_pairs={{0,31},{1,2},{2,1},{3,4},{4,3},{5,6},{6,5},{7,8},{8,7},{9,10},{10,... | collective-permute-start | bytes 86024 | tf_op jit(solution)/shard_map/ppermute | solution.py:639
  35.6 3.1 %collective-permute-done.5.two_ref = bf16[112,128]{1,0:T(8,128)(2,1)S(1)} collective-permute-done((bf16[112,128]{1,0:T(8,128)(2,1)S(1)}, bf16[112,128]{1,0:T(8,128)(2,1)S(1)}, u32[]{:S(2)}, u32[]{:S(2)}) %collective-permute-start.5) | collective-permute-done | bytes 28704 | tf_op jit(solution)/shard_map/ppermute | solution.py:639
  38.7 0.8 collective-permute-done.4.one_ref
  39.5 0.6 copy-done.8
  40.1 16.4 %shard_map.155 = (bf16[32,16,512]{2,1,0:T(8,128)(2,1)}, bf16[304,128]{1,0:T(8,128)(2,1)S(1)}) custom-call(s32[2]{0:T(128)S(1)} %copy-done.8, bf16[8,32,512]{2,1,0:T(8,128)(2,1)S(1)} %get-tuple-element.20.feats_ref, bf16[32,8,128]{2,1,0:T(8,128)(2,1)S(1)} %all-to-all-done.bands_ref, bf16[112,128]{1,0:T(8,128)(2,1)S(1)} %get-tuple-element.22.own_ref, ...), custom_call_target="tpu_custom_call" | custom-call | tf_op jit(solution)/shard_map/pallas_call | solution.py:582
  56.5 1.3 %collective-permute-done.8 = bf16[304,128]{1,0:T(8,128)(2,1)S(1)} collective-permute-done((bf16[304,128]{1,0:T(8,128)(2,1)S(1)}, bf16[304,128]{1,0:T(8,128)(2,1)S(1)}, u32[]{:S(2)}, u32[]{:S(2)}) %collective-permute-start.8) | collective-permute-done | bytes 77856 | tf_op jit(solution)/shard_map/ppermute | solution.py:705
  57.8 1.3 %collective-permute-start.11 = (bf16[304,128]{1,0:T(8,128)(2,1)S(1)}, bf16[304,128]{1,0:T(8,128)(2,1)S(1)}, u32[]{:S(2)}, u32[]{:S(2)}) collective-permute-start(bf16[304,128]{1,0:T(8,128)(2,1)S(1)} %add_convert_fusion.own_ref), channel_id=1, source_target_pairs={{0,192},{32,224},{64,0},{96,32},{128,64},{160,96},{192,128},{224,1... | collective-permute-start | bytes 233480 | tf_op jit(solution)/shard_map/ppermute | solution.py:702
  59.2 3.4 %collective-permute-start.10 = (bf16[304,128]{1,0:T(8,128)(2,1)S(1)}, bf16[304,128]{1,0:T(8,128)(2,1)S(1)}, u32[]{:S(2)}, u32[]{:S(2)}) collective-permute-start(bf16[304,128]{1,0:T(8,128)(2,1)S(1)} %add_convert_fusion.own_ref), channel_id=1, source_target_pairs={{0,128},{32,160},{64,192},{96,224},{128,0},{160,32},{192,64},{224,... | collective-permute-start | bytes 233480 | tf_op jit(solution)/shard_map/ppermute | solution.py:702
  62.6 0.7 collective-permute-start.9
  63.2 1.0 %collective-permute-done.11.c_ref = bf16[304,128]{1,0:T(8,128)(2,1)S(1)} collective-permute-done((bf16[304,128]{1,0:T(8,128)(2,1)S(1)}, bf16[304,128]{1,0:T(8,128)(2,1)S(1)}, u32[]{:S(2)}, u32[]{:S(2)}) %collective-permute-start.11) | collective-permute-done | bytes 77856 | tf_op jit(solution)/shard_map/ppermute | solution.py:702
  64.2 5.8 %collective-permute-done.10.b_ref = bf16[304,128]{1,0:T(8,128)(2,1)S(1)} collective-permute-done((bf16[304,128]{1,0:T(8,128)(2,1)S(1)}, bf16[304,128]{1,0:T(8,128)(2,1)S(1)}, u32[]{:S(2)}, u32[]{:S(2)}) %collective-permute-start.10) | collective-permute-done | bytes 77856 | tf_op jit(solution)/shard_map/ppermute | solution.py:702
  70.0 1.0 %shard_map.156 = (bf16[32,512]{1,0:T(8,128)(2,1)}, bf16[240,128]{1,0:T(8,128)(2,1)S(1)}) custom-call(bf16[304,128]{1,0:T(8,128)(2,1)S(1)} %add_convert_fusion.own_ref, bf16[304,128]{1,0:T(8,128)(2,1)S(1)} %collective-permute-done.9.a_ref, bf16[304,128]{1,0:T(8,128)(2,1)S(1)} %collective-permute-done.10.b_ref, ...), custom_call_target="tpu_custom_call" | custom-call | tf_op jit(solution)/shard_map/pallas_call | solution.py:582
  71.0 3.9 %collective-permute-start.14 = (bf16[240,128]{1,0:T(8,128)(2,1)S(1)}, bf16[240,128]{1,0:T(8,128)(2,1)S(1)}, u32[]{:S(2)}, u32[]{:S(2)}) collective-permute-start(bf16[240,128]{1,0:T(8,128)(2,1)S(1)} %get-tuple-element.26), channel_id=1, source_target_pairs={{0,3},{1,0},{2,1},{3,2},{4,7},{5,4},{6,5},{7,6},{8,11},{9,8},{10,9... | collective-permute-start | bytes 184328 | tf_op jit(solution)/shard_map/ppermute | solution.py:702
  74.9 1.5 %collective-permute-start.12 = (bf16[240,128]{1,0:T(8,128)(2,1)S(1)}, bf16[240,128]{1,0:T(8,128)(2,1)S(1)}, u32[]{:S(2)}, u32[]{:S(2)}) collective-permute-start(bf16[240,128]{1,0:T(8,128)(2,1)S(1)} %get-tuple-element.26), channel_id=1, source_target_pairs={{0,2},{1,3},{2,0},{3,1},{4,6},{5,7},{6,4},{7,5},{8,10},{9,11},{10,... | collective-permute-start | bytes 184328 | tf_op jit(solution)/shard_map/ppermute | solution.py:702
  76.8 4.2 %collective-permute-done.13 = bf16[240,128]{1,0:T(8,128)(2,1)S(1)} collective-permute-done((bf16[240,128]{1,0:T(8,128)(2,1)S(1)}, bf16[240,128]{1,0:T(8,128)(2,1)S(1)}, u32[]{:S(2)}, u32[]{:S(2)}) %collective-permute-start.13) | collective-permute-done | bytes 61472 | tf_op jit(solution)/shard_map/ppermute | solution.py:702
  81.1 3.2 %collective-permute-start.16 = (bf16[240,128]{1,0:T(8,128)(2,1)S(1)}, bf16[240,128]{1,0:T(8,128)(2,1)S(1)}, u32[]{:S(2)}, u32[]{:S(2)}) collective-permute-start(bf16[240,128]{1,0:T(8,128)(2,1)S(1)} %add_convert_fusion.2), channel_id=1, source_target_pairs={{0,4},{1,5},{2,6},{3,7},{4,8},{5,9},{6,10},{7,11},{8,12},{9,13},{1... | collective-permute-start | bytes 184328 | tf_op jit(solution)/shard_map/ppermute | solution.py:702
  84.4 2.4 %collective-permute-done.17 = bf16[240,128]{1,0:T(8,128)(2,1)S(1)} collective-permute-done((bf16[240,128]{1,0:T(8,128)(2,1)S(1)}, bf16[240,128]{1,0:T(8,128)(2,1)S(1)}, u32[]{:S(2)}, u32[]{:S(2)}) %collective-permute-start.17) | collective-permute-done | bytes 61472 | tf_op jit(solution)/shard_map/ppermute | solution.py:702
  86.9 3.2 %collective-permute-done.15 = bf16[240,128]{1,0:T(8,128)(2,1)S(1)} collective-permute-done((bf16[240,128]{1,0:T(8,128)(2,1)S(1)}, bf16[240,128]{1,0:T(8,128)(2,1)S(1)}, u32[]{:S(2)}, u32[]{:S(2)}) %collective-permute-start.15) | collective-permute-done | bytes 61472 | tf_op jit(solution)/shard_map/ppermute | solution.py:702
  90.1 3.2 %collective-permute-start.18 = (bf16[240,128]{1,0:T(8,128)(2,1)S(1)}, bf16[240,128]{1,0:T(8,128)(2,1)S(1)}, u32[]{:S(2)}, u32[]{:S(2)}) collective-permute-start(bf16[240,128]{1,0:T(8,128)(2,1)S(1)} %add_convert_fusion.1.own_ref), channel_id=1, source_target_pairs={{0,16},{1,17},{2,18},{3,19},{4,20},{5,21},{6,22},{7,23},{8,24},{9,... | collective-permute-start | bytes 184328 | tf_op jit(solution)/shard_map/ppermute | solution.py:726
  93.3 2.2 %collective-permute-done.18.a_ref = bf16[240,128]{1,0:T(8,128)(2,1)S(1)} collective-permute-done((bf16[240,128]{1,0:T(8,128)(2,1)S(1)}, bf16[240,128]{1,0:T(8,128)(2,1)S(1)}, u32[]{:S(2)}, u32[]{:S(2)}) %collective-permute-start.18) | collective-permute-done | bytes 61472 | tf_op jit(solution)/shard_map/ppermute | solution.py:726
  95.5 0.9 shard_map.157
  (36 shorter events, 1.0 us)
Async XLA Ops:
  1.9 0.7 copy-start.7
  2.6 1.0 %copy-start = (bf16[32,16,512]{2,1,0:T(8,128)(2,1)S(1)}, bf16[32,16,512]{2,1,0:T(8,128)(2,1)}, u32[]{:S(2)}) copy-start(bf16[32,16,512]{2,1,0:T(8,128)(2,1)} %cot_ref.1) | copy-start | bytes 1572868
  3.6 0.8 copy-start.6
  4.6 15.8 %copy-start.1 = (bf16[32,16,512]{2,1,0:T(8,128)(2,1)S(1)}, bf16[32,16,512]{2,1,0:T(8,128)(2,1)}, u32[]{:S(2)}) copy-start(bf16[32,16,512]{2,1,0:T(8,128)(2,1)} %cot_ref.1) | copy-start | bytes 1572868
  4.6 11.4 %collective-permute-start.2 = (bf16[64,512]{1,0:T(8,128)(2,1)S(1)}, bf16[64,512]{1,0:T(8,128)(2,1)S(1)}, u32[]{:S(2)}, u32[]{:S(2)}) collective-permute-start(bf16[64,512]{1,0:T(8,128)(2,1)S(1)} %shard_map.153.own_ref), channel_id=1, source_target_pairs={{192,0},{224,32},{0,64},{32,96},{64,128},{96,160},{128,192},{160,2... | collective-permute-start | bytes 196616 | tf_op jit(solution)/shard_map/ppermute | solution.py:621
  7.9 9.5 %collective-permute-start.1 = (bf16[64,512]{1,0:T(8,128)(2,1)S(1)}, bf16[64,512]{1,0:T(8,128)(2,1)S(1)}, u32[]{:S(2)}, u32[]{:S(2)}) collective-permute-start(bf16[64,512]{1,0:T(8,128)(2,1)S(1)} %shard_map.153.own_ref), channel_id=1, source_target_pairs={{128,0},{160,32},{192,64},{224,96},{0,128},{32,160},{64,192},{96,2... | collective-permute-start | bytes 196616 | tf_op jit(solution)/shard_map/ppermute | solution.py:621
  13.3 6.9 %collective-permute-start = (bf16[64,512]{1,0:T(8,128)(2,1)S(1)}, bf16[64,512]{1,0:T(8,128)(2,1)S(1)}, u32[]{:S(2)}, u32[]{:S(2)}) collective-permute-start(bf16[64,512]{1,0:T(8,128)(2,1)S(1)} %shard_map.153.own_ref), channel_id=1, source_target_pairs={{64,0},{96,32},{128,64},{160,96},{192,128},{224,160},{0,192},{32,2... | collective-permute-start | bytes 196616 | tf_op jit(solution)/shard_map/ppermute | solution.py:621
  20.3 3.7 %collective-permute-start.3 = (bf16[4,64,512]{2,1,0:T(8,128)(2,1)S(1)}, bf16[4,64,512]{2,1,0:T(8,128)(2,1)S(1)}, u32[]{:S(2)}, u32[]{:S(2)}) collective-permute-start(bf16[4,64,512]{2,1,0:T(8,128)(2,1)S(1)} %pad_maximum_fusion), channel_id=1, source_target_pairs={{0,32},{32,0},{64,96},{96,64},{128,160},{160,128},{192,224},{224,1... | collective-permute-start | bytes 786440 | tf_op jit(solution)/shard_map/ppermute | solution.py:624
  20.5 15.1 %collective-permute-start.7 = (bf16[32,8,512]{2,1,0:T(8,128)(2,1)S(1)}, bf16[32,8,512]{2,1,0:T(8,128)(2,1)S(1)}, u32[]{:S(2)}, u32[]{:S(2)}) collective-permute-start(bf16[32,8,512]{2,1,0:T(8,128)(2,1)S(1)} %get-tuple-element.33), channel_id=1, source_target_pairs={{0,224},{32,64},{64,32},{96,128},{128,96},{160,192},{192,160},{224... | collective-permute-start | bytes 786440 | tf_op jit(solution)/shard_map/ppermute | solution.py:647
  24.0 11.6 %collective-permute-start.6 = (bf16[32,8,512]{2,1,0:T(8,128)(2,1)S(1)}, bf16[32,8,512]{2,1,0:T(8,128)(2,1)S(1)}, u32[]{:S(2)}, u32[]{:S(2)}) collective-permute-start(bf16[32,8,512]{2,1,0:T(8,128)(2,1)S(1)} %get-tuple-element.34), channel_id=1, source_target_pairs={{0,32},{32,0},{64,96},{96,64},{128,160},{160,128},{192,224},{224,1... | collective-permute-start | bytes 786440 | tf_op jit(solution)/shard_map/ppermute | solution.py:646
  24.0 15.4 %copy-start.4 = (bf16[256,32]{0,1:T(8,128)(2,1)S(1)}, bf16[256,32]{0,1:T(8,128)(2,1)}, u32[]{:S(2)}) copy-start(bf16[256,32]{0,1:T(8,128)(2,1)} %param.13) | copy-start | bytes 49156
  24.0 15.4 %copy-start.5 = (bf16[256,32]{0,1:T(8,128)(2,1)S(1)}, bf16[256,32]{0,1:T(8,128)(2,1)}, u32[]{:S(2)}) copy-start(bf16[256,32]{0,1:T(8,128)(2,1)} %param.12) | copy-start | bytes 49156
  24.8 14.7 %copy-start.2 = (bf16[32,32,3,3]{1,0,3,2:T(8,128)(2,1)S(1)}, bf16[32,32,3,3]{1,0,3,2:T(8,128)(2,1)}, u32[]{:S(2)}) copy-start(bf16[32,32,3,3]{1,0,3,2:T(8,128)(2,1)} %param.14) | copy-start | bytes 55300
  24.8 14.7 %copy-start.3 = (bf16[32,32,3,3]{1,0,3,2:T(8,128)(2,1)S(1)}, bf16[32,32,3,3]{1,0,3,2:T(8,128)(2,1)}, u32[]{:S(2)}) copy-start(bf16[32,32,3,3]{1,0,3,2:T(8,128)(2,1)} %param.15) | copy-start | bytes 55300
  24.8 14.6 %all-to-all-start = ((bf16[32,8,128]{2,1,0:T(8,128)(2,1)}), bf16[32,8,128]{2,1,0:T(8,128)(2,1)S(1)}, u32[]{:S(2)}, u32[]{:S(2)}) async-start(bf16[32,8,128]{2,1,0:T(8,128)(2,1)} %get-tuple-element.21), calls=%async_computation | async-start | bytes 131072 | tf_op jit(solution)/shard_map/all_to_all | solution.py:640
  32.5 6.2 %collective-permute-start.5 = (bf16[112,128]{1,0:T(8,128)(2,1)S(1)}, bf16[112,128]{1,0:T(8,128)(2,1)S(1)}, u32[]{:S(2)}, u32[]{:S(2)}) collective-permute-start(bf16[112,128]{1,0:T(8,128)(2,1)S(1)} %get-tuple-element.23), channel_id=1, source_target_pairs={{0,31},{1,2},{2,1},{3,4},{4,3},{5,6},{6,5},{7,8},{8,7},{9,10},{10,... | collective-permute-start | bytes 86024 | tf_op jit(solution)/shard_map/ppermute | solution.py:639
  35.6 3.9 %collective-permute-start.4 = (bf16[112,128]{1,0:T(8,128)(2,1)S(1)}, bf16[112,128]{1,0:T(8,128)(2,1)S(1)}, u32[]{:S(2)}, u32[]{:S(2)}) collective-permute-start(bf16[112,128]{1,0:T(8,128)(2,1)S(1)} %get-tuple-element.22.own_ref), channel_id=1, source_target_pairs={{0,1},{1,0},{2,3},{3,2},{4,5},{5,4},{6,7},{7,6},{8,9},{9,8},{10,11... | collective-permute-start | bytes 86024 | tf_op jit(solution)/shard_map/ppermute | solution.py:638
  39.4 0.7 copy-start.8
  56.5 1.3 %collective-permute-start.8 = (bf16[304,128]{1,0:T(8,128)(2,1)S(1)}, bf16[304,128]{1,0:T(8,128)(2,1)S(1)}, u32[]{:S(2)}, u32[]{:S(2)}) collective-permute-start(bf16[304,128]{1,0:T(8,128)(2,1)S(1)} %get-tuple-element.25), channel_id=1, source_target_pairs={{0,32},{32,0},{64,96},{96,64},{128,160},{160,128},{192,224},{224,1... | collective-permute-start | bytes 233480 | tf_op jit(solution)/shard_map/ppermute | solution.py:705
  57.8 6.4 %collective-permute-start.11 = (bf16[304,128]{1,0:T(8,128)(2,1)S(1)}, bf16[304,128]{1,0:T(8,128)(2,1)S(1)}, u32[]{:S(2)}, u32[]{:S(2)}) collective-permute-start(bf16[304,128]{1,0:T(8,128)(2,1)S(1)} %add_convert_fusion.own_ref), channel_id=1, source_target_pairs={{0,192},{32,224},{64,0},{96,32},{128,64},{160,96},{192,128},{224,1... | collective-permute-start | bytes 233480 | tf_op jit(solution)/shard_map/ppermute | solution.py:702
  59.2 10.8 %collective-permute-start.10 = (bf16[304,128]{1,0:T(8,128)(2,1)S(1)}, bf16[304,128]{1,0:T(8,128)(2,1)S(1)}, u32[]{:S(2)}, u32[]{:S(2)}) collective-permute-start(bf16[304,128]{1,0:T(8,128)(2,1)S(1)} %add_convert_fusion.own_ref), channel_id=1, source_target_pairs={{0,128},{32,160},{64,192},{96,224},{128,0},{160,32},{192,64},{224,... | collective-permute-start | bytes 233480 | tf_op jit(solution)/shard_map/ppermute | solution.py:702
  62.6 7.4 %collective-permute-start.9 = (bf16[304,128]{1,0:T(8,128)(2,1)S(1)}, bf16[304,128]{1,0:T(8,128)(2,1)S(1)}, u32[]{:S(2)}, u32[]{:S(2)}) collective-permute-start(bf16[304,128]{1,0:T(8,128)(2,1)S(1)} %add_convert_fusion.own_ref), channel_id=1, source_target_pairs={{0,64},{32,96},{64,128},{96,160},{128,192},{160,224},{192,0},{224,... | collective-permute-start | bytes 233480 | tf_op jit(solution)/shard_map/ppermute | solution.py:702
  71.0 5.8 %collective-permute-start.14 = (bf16[240,128]{1,0:T(8,128)(2,1)S(1)}, bf16[240,128]{1,0:T(8,128)(2,1)S(1)}, u32[]{:S(2)}, u32[]{:S(2)}) collective-permute-start(bf16[240,128]{1,0:T(8,128)(2,1)S(1)} %get-tuple-element.26), channel_id=1, source_target_pairs={{0,3},{1,0},{2,1},{3,2},{4,7},{5,4},{6,5},{7,6},{8,11},{9,8},{10,9... | collective-permute-start | bytes 184328 | tf_op jit(solution)/shard_map/ppermute | solution.py:702
  74.9 6.1 %collective-permute-start.13 = (bf16[240,128]{1,0:T(8,128)(2,1)S(1)}, bf16[240,128]{1,0:T(8,128)(2,1)S(1)}, u32[]{:S(2)}, u32[]{:S(2)}) collective-permute-start(bf16[240,128]{1,0:T(8,128)(2,1)S(1)} %get-tuple-element.26), channel_id=1, source_target_pairs={{0,1},{1,2},{2,3},{3,0},{4,5},{5,6},{6,7},{7,4},{8,9},{9,10},{10,1... | collective-permute-start | bytes 184328 | tf_op jit(solution)/shard_map/ppermute | solution.py:702
  74.9 6.1 %collective-permute-start.12 = (bf16[240,128]{1,0:T(8,128)(2,1)S(1)}, bf16[240,128]{1,0:T(8,128)(2,1)S(1)}, u32[]{:S(2)}, u32[]{:S(2)}) collective-permute-start(bf16[240,128]{1,0:T(8,128)(2,1)S(1)} %get-tuple-element.26), channel_id=1, source_target_pairs={{0,2},{1,3},{2,0},{3,1},{4,6},{5,7},{6,4},{7,5},{8,10},{9,11},{10,... | collective-permute-start | bytes 184328 | tf_op jit(solution)/shard_map/ppermute | solution.py:702
  81.1 5.8 %collective-permute-start.17 = (bf16[240,128]{1,0:T(8,128)(2,1)S(1)}, bf16[240,128]{1,0:T(8,128)(2,1)S(1)}, u32[]{:S(2)}, u32[]{:S(2)}) collective-permute-start(bf16[240,128]{1,0:T(8,128)(2,1)S(1)} %add_convert_fusion.2), channel_id=1, source_target_pairs={{0,12},{1,13},{2,14},{3,15},{4,0},{5,1},{6,2},{7,3},{8,4},{9,5},{1... | collective-permute-start | bytes 184328 | tf_op jit(solution)/shard_map/ppermute | solution.py:702
  81.1 5.7 %collective-permute-start.16 = (bf16[240,128]{1,0:T(8,128)(2,1)S(1)}, bf16[240,128]{1,0:T(8,128)(2,1)S(1)}, u32[]{:S(2)}, u32[]{:S(2)}) collective-permute-start(bf16[240,128]{1,0:T(8,128)(2,1)S(1)} %add_convert_fusion.2), channel_id=1, source_target_pairs={{0,4},{1,5},{2,6},{3,7},{4,8},{5,9},{6,10},{7,11},{8,12},{9,13},{1... | collective-permute-start | bytes 184328 | tf_op jit(solution)/shard_map/ppermute | solution.py:702
  84.4 5.7 %collective-permute-start.15 = (bf16[240,128]{1,0:T(8,128)(2,1)S(1)}, bf16[240,128]{1,0:T(8,128)(2,1)S(1)}, u32[]{:S(2)}, u32[]{:S(2)}) collective-permute-start(bf16[240,128]{1,0:T(8,128)(2,1)S(1)} %add_convert_fusion.2), channel_id=1, source_target_pairs={{0,8},{1,9},{2,10},{3,11},{4,12},{5,13},{6,14},{7,15},{8,0},{9,1},... | collective-permute-start | bytes 184328 | tf_op jit(solution)/shard_map/ppermute | solution.py:702
  90.1 5.4 %collective-permute-start.18 = (bf16[240,128]{1,0:T(8,128)(2,1)S(1)}, bf16[240,128]{1,0:T(8,128)(2,1)S(1)}, u32[]{:S(2)}, u32[]{:S(2)}) collective-permute-start(bf16[240,128]{1,0:T(8,128)(2,1)S(1)} %add_convert_fusion.1.own_ref), channel_id=1, source_target_pairs={{0,16},{1,17},{2,18},{3,19},{4,20},{5,21},{6,22},{7,23},{8,24},{9,... | collective-permute-start | bytes 184328 | tf_op jit(solution)/shard_map/ppermute | solution.py:726
